TPU v7x, 32 devices: a whole 2x2x4 slice. The times are simulated.
32 devices in a mesh: tile: 4 (over x, core), orient: 8 (over z, y).
Axes of the slice: x: 2, y: 2, z: 4, core: 2. Of those that a mesh axis runs over, the one named last changes fastest.
Arguments:
- micrograph: bfloat16 [1024, 512], P('tile'), may hold values from -140 to 140
- templates: bfloat16 [16, 384, 384], P('orient', 'tile'), may hold values from -6 to 6
- defocus: float32 [4], replicated, may hold values from 8 to 40
- group_of_tile: int32 [4], P('tile'), may hold values from 0 to 3
Outputs:
- top_score: float32 [1024, 128], P(('tile', 'orient'))
- zscore: float32 [1024, 128], P(('tile', 'orient'))
All inputs are finite; a program needn't handle non-finite values.
Results may differ from a plain program's by a relative error of at most 0.0085.
Values may be sent and summed in bfloat16 or wider, within the bound.
No kernel may reach another device: no remote copies, remote signals or barrier semaphores. Data moves between devices by JAX's collectives and lax.ppermute only.
A program may use at most 64 MiB of HBM per device.

v0:
```python
import functools
import math

import jax
import jax.numpy as jnp
import ml_dtypes
import numpy as np
from jax import lax
from jax.experimental import pallas as pl
from jax.experimental.pallas import tpu as pltpu
from jax.sharding import PartitionSpec as P

TS = 384
STRIP = 256
OUTC = 128
CHUNK = 16
VMEM_BYTES = 40 * 1024 * 1024


def cos_sin(freqs, places, modulus):
    residue = freqs[:, None] * places[None, :] % modulus
    lowest = np.minimum(residue, modulus - residue)
    flipped = np.where(residue > modulus - residue, -1.0, 1.0).astype(np.float32)
    angle = lowest.astype(np.float32) * np.float32(2.0 * math.pi / modulus)
    sine = np.where(2 * lowest == modulus, np.float32(0.0), flipped * np.sin(angle))
    return np.cos(angle).astype(np.float32), sine.astype(np.float32)


def round_up(value, multiple):
    return -(-value // multiple) * multiple


@functools.lru_cache(maxsize=None)
def tables(width_rows, width_cols):
    half = width_cols // 2
    rows = width_rows // 2 + 1
    padded = round_up(rows, CHUNK)
    bf16 = ml_dtypes.bfloat16
    places = np.arange(width_cols)
    cos_v, sin_v = cos_sin(np.arange(half + 1), places, width_cols)
    packed_sin = sin_v[:half].copy()
    forward_sin = -packed_sin
    forward_sin[0] = cos_v[half]
    packed_sin[0] = cos_v[half]
    col = np.concatenate([cos_v[:half], forward_sin], 0).T.astype(bf16)
    back = (2.0 * np.concatenate([cos_v[:half], packed_sin], 0)[:, :OUTC].astype(bf16).astype(np.float32)).astype(bf16)
    cos_u, sin_u = cos_sin(np.arange(rows), np.arange(width_rows), width_rows)
    row = np.zeros((2 * padded, width_rows), np.float32)
    row[:rows] = cos_u
    row[padded : padded + rows] = -sin_u
    row = row.astype(bf16)
    weight = np.ones((rows, 1), np.float32)
    weight[0] = weight[-1] = 0.5
    out = np.zeros((2 * padded, STRIP), np.float32)
    out[:rows] = cos_u[:, :STRIP].astype(bf16).astype(np.float32) * weight
    out[padded : padded + rows] = sin_u[:, :STRIP].astype(bf16).astype(np.float32) * weight
    out = np.ascontiguousarray(out.T).astype(bf16)
    row_sum = row[:, :TS].astype(np.float32).sum(1, keepdims=True)
    col_sum = col[:TS].astype(np.float32).sum(0, keepdims=True)
    u = np.minimum(np.arange(padded), rows - 1).astype(np.float32) / np.float32(width_rows)
    v = np.arange(half).astype(np.float32) / np.float32(width_cols)
    v_last = v.copy()
    v_last[0] = 0.5
    radius = np.stack([u[:, None] ** 2 + w[None, :] ** 2 for w in (v, v_last)])
    return col, row, back, out, row_sum.astype(np.float32), col_sum.astype(np.float32), radius


def gather_blocks(value, axis):
    count = lax.axis_size(axis)
    place = lax.axis_index(axis)
    if count & (count - 1):
        whole = lax.all_gather(value, axis, axis=0)
        return [whole[j] for j in range(count)], jnp.arange(count, dtype=jnp.int32)
    held, index = [value], [0]
    step = count // 2
    while step:
        pairs = [(source, source ^ step) for source in range(count)]
        held = held + [lax.ppermute(block, axis, pairs) for block in held]
        index = index + [j ^ step for j in index]
        step //= 2
    return held, jnp.stack([place ^ j for j in index]).astype(jnp.int32)


def first_column(shape):
    return lax.broadcasted_iota(jnp.int32, shape, 1) == 0


def both_signs(cc, cs, sc, ss, first):
    plus_re = cc - jnp.where(first, 0.0, ss)
    plus_im = jnp.where(first, 0.0, cs) + sc
    minus_re = jnp.where(first, cs, cc + ss)
    minus_im = jnp.where(first, ss, cs - sc)
    return plus_re, plus_im, minus_re, minus_im


def spectrum_kernel(count, place_ref, *refs):
    blocks = refs[:count]
    col_ref, row_ref, ctf_ref, weighted_ref, part_ref, quad_ref, own_ref, power_ref = refs[count:]
    padded = row_ref.shape[0] // 2
    width_rows = row_ref.shape[1]
    half = col_ref.shape[1] // 2
    width_cols = col_ref.shape[0]
    first = first_column((CHUNK, half))
    part_ref[count * STRIP :, :] = jnp.zeros((part_ref.shape[0] - count * STRIP, 2 * half), jnp.bfloat16)
    for j in range(count):
        start = pl.multiple_of(place_ref[j] * STRIP, STRIP)
        part_ref[pl.ds(start, STRIP), :] = jnp.dot(
            blocks[j][...], col_ref[...], preferred_element_type=jnp.float32
        ).astype(jnp.bfloat16)
    for j in range(count):
        start = pl.multiple_of(place_ref[j] * STRIP, STRIP)
        quad_ref[...] = jnp.dot(
            row_ref[...], part_ref[pl.ds(start, width_rows), :], preferred_element_type=jnp.float32
        )
        for r in range(0, padded, CHUNK):
            up, down = slice(r, r + CHUNK), slice(padded + r, padded + r + CHUNK)
            signs = both_signs(
                quad_ref[up, :half], quad_ref[up, half:], quad_ref[down, :half], quad_ref[down, half:], first
            )
            plus = signs[0] * signs[0] + signs[1] * signs[1]
            minus = signs[2] * signs[2] + signs[3] * signs[3]
            if j == 0:
                for k in range(4):
                    own_ref[k, up] = signs[k]
                power_ref[0, up] = plus
                power_ref[1, up] = minus
            else:
                power_ref[0, up] += plus
                power_ref[1, up] += minus
    total = jnp.zeros((CHUNK, half), jnp.float32)
    for r in range(0, padded, CHUNK):
        total = total + (power_ref[0, r : r + CHUNK] + power_ref[1, r : r + CHUNK])
    last = width_rows // 2
    ends = (power_ref[0, 0:1] + power_ref[1, 0:1]) + (power_ref[0, last : last + 1] + power_ref[1, last : last + 1])
    mean = (2.0 * jnp.sum(total, keepdims=True) - jnp.sum(ends, keepdims=True)) / (count * width_rows * width_cols)
    for r in range(0, padded, CHUNK):
        up = slice(r, r + CHUNK)
        for side in range(2):
            gain = lax.rsqrt(power_ref[side, up] * (1.0 / count) + mean) * ctf_ref[side, up]
            weighted_ref[2 * side, up] = own_ref[2 * side, up] * gain
            weighted_ref[2 * side + 1, up] = own_ref[2 * side + 1, up] * gain


def score_kernel(count, place_ref, *refs):
    blocks = refs[:count]
    (weighted_ref, col_ref, row_ref, back_ref, out_ref, row_sum_ref, col_sum_ref) = refs[count : count + 7]
    score_ref, whole_ref, quad_ref, product_ref = refs[count + 7 :]
    padded = row_ref.shape[0] // 2
    half = col_ref.shape[1] // 2
    scale = 1.0 / (row_ref.shape[1] * col_ref.shape[0])
    first = first_column((CHUNK, half))
    tpl_count, depth = blocks[0].shape[:2]
    pieces = score_ref.shape[0]
    for index in range(tpl_count):
        sums = jnp.zeros((1, 1), jnp.float32)
        squares = jnp.zeros((1, 1), jnp.float32)
        for j in range(count):
            block = blocks[j][index]
            wide = block.astype(jnp.float32)
            sums = sums + jnp.sum(wide, keepdims=True)
            squares = squares + jnp.sum(wide * wide, keepdims=True)
            start = pl.multiple_of(place_ref[j] * depth, depth)
            whole_ref[index, pl.ds(start, depth), :] = block.astype(whole_ref.dtype)
        mean = sums / (TS * TS)
        spread = jnp.sqrt(squares / (TS * TS) - mean * mean + 1e-05)
        partial = jnp.dot(
            whole_ref[index].astype(jnp.bfloat16), col_ref[:TS, :], preferred_element_type=jnp.float32
        ).astype(jnp.bfloat16)
        quad_ref[...] = jnp.dot(row_ref[:, :TS], partial, preferred_element_type=jnp.float32)
        col_sum = mean * col_sum_ref[...]
        for r in range(0, padded, CHUNK):
            up, down = slice(r, r + CHUNK), slice(padded + r, padded + r + CHUNK)
            upper = quad_ref[up, :] - row_sum_ref[up, :] * col_sum
            lower = quad_ref[down, :] - row_sum_ref[down, :] * col_sum
            a, b, c, d = both_signs(upper[:, :half], upper[:, half:], lower[:, :half], lower[:, half:], first)
            p, q, s, t = (weighted_ref[k, up] for k in range(4))
            plus_re = p * a + q * b
            plus_im = q * a - p * b
            minus_re = s * c + t * d
            minus_im = t * c - s * d
            product_ref[up, :half] = (plus_re + jnp.where(first, 0.0, minus_re)).astype(jnp.bfloat16)
            product_ref[up, half:] = jnp.where(first, minus_re, -(plus_im + minus_im)).astype(jnp.bfloat16)
            product_ref[down, :half] = (jnp.where(first, 0.0, minus_im) - plus_im).astype(jnp.bfloat16)
            product_ref[down, half:] = jnp.where(first, -minus_im, minus_re - plus_re).astype(jnp.bfloat16)
        back = jnp.dot(product_ref[...], back_ref[...], preferred_element_type=jnp.float32).astype(jnp.bfloat16)
        score = jnp.dot(out_ref[...], back, preferred_element_type=jnp.float32) * (scale / spread)
        score_ref[:, index] = score.reshape(pieces, STRIP // pieces, OUTC).astype(jnp.bfloat16)


def on_device(kernel, operands, scratch, result):
    vmem, smem = pl.BlockSpec(memory_space=pltpu.VMEM), pl.BlockSpec(memory_space=pltpu.SMEM)
    return pl.pallas_call(
        kernel,
        out_shape=result,
        in_specs=[smem] + [vmem] * (len(operands) - 1),
        out_specs=vmem,
        scratch_shapes=scratch,
        compiler_params=pltpu.CompilerParams(vmem_limit_bytes=VMEM_BYTES),
    )(*operands)


def local(micrograph, templates, defocus, group_of_tile):
    width_cols = micrograph.shape[1]
    width_rows = STRIP + TS
    tpl_count, depth = templates.shape[:2]
    count = lax.axis_size("tile")
    orient_count = lax.axis_size("orient")
    col, row, back, out, row_sum, col_sum, radius = tables(width_rows, width_cols)
    padded, half = row.shape[0] // 2, width_cols // 2
    strips, places = gather_blocks(micrograph, "tile")
    pieces, _ = gather_blocks(templates, "tile")
    ctf = -jnp.sin(jnp.float32(math.pi) * defocus[group_of_tile[0]] * radius + 0.07)
    plane = (padded, half)
    weighted = on_device(
        functools.partial(spectrum_kernel, count),
        [places, *strips, col, row, ctf],
        [
            pltpu.VMEM((count * STRIP + TS, width_cols), jnp.bfloat16),
            pltpu.VMEM((2 * padded, width_cols), jnp.float32),
            pltpu.VMEM((4, *plane), jnp.float32),
            pltpu.VMEM((2, *plane), jnp.float32),
        ],
        jax.ShapeDtypeStruct((4, *plane), jnp.float32),
    )
    scores = on_device(
        functools.partial(score_kernel, count),
        [places, *pieces, weighted, col, row, back, out, row_sum, col_sum],
        [
            pltpu.VMEM((tpl_count, TS, TS), jnp.bfloat16 if depth % 16 == 0 else jnp.float32),
            pltpu.VMEM((2 * padded, width_cols), jnp.float32),
            pltpu.VMEM((2 * padded, width_cols), jnp.bfloat16),
        ],
        jax.ShapeDtypeStruct((orient_count, tpl_count, STRIP // orient_count, OUTC), jnp.bfloat16),
    )
    received = lax.all_to_all(scores, "orient", split_axis=0, concat_axis=0, tiled=True).astype(jnp.float32)
    orient_total = tpl_count * orient_count
    best = jnp.max(received, axis=(0, 1))
    score_mean = jnp.sum(received, axis=(0, 1)) / orient_total
    score_var = jnp.sum(received * received, axis=(0, 1)) / orient_total - score_mean * score_mean
    return (best, (best - score_mean) / jnp.sqrt(score_var + 1e-05))


def solution(mesh):
    placed = (P("tile", None), P("orient", "tile", None), P(), P("tile"))
    return jax.shard_map(
        local,
        mesh=mesh,
        in_specs=placed,
        out_specs=(P(("tile", "orient"), None), P(("tile", "orient"), None)),
        check_vma=False,
    )
```

profile of v0, /device:TPU:0, one launch (start us, length us, event | category | flops | bytes accessed | tf_op | source)
XLA Modules:
  0.0 40.2 jit_solution(452064610719544939)
XLA Ops:
  0.6 0.0 copy-start.1
  0.6 0.0 copy-start
  0.7 3.0 %collective-permute-start.3 = (bf16[256,512]{1,0:T(8,128)(2,1)}, bf16[256,512]{1,0:T(8,128)(2,1)S(1)}, u32[]{:S(2)}, u32[]{:S(2)}) collective-permute-start(bf16[256,512]{1,0:T(8,128)(2,1)} %refs_0_.2), channel_id=1, source_target_pairs={{0,16},{8,24},{16,0},{24,8},{1,17},{9,25},{17,1},{25,9},{2,18},{10... | collective-permute-start | bytes 786440 | tf_op jit(solution)/shard_map/ppermute | solution.py:78
  3.7 0.1 collective-permute-start
  3.7 0.0 collective-permute-start.4
  3.7 0.5 %collective-permute-start.1 = (bf16[2,96,384]{2,1,0:T(8,128)(2,1)}, bf16[2,96,384]{2,1,0:T(8,128)(2,1)S(1)}, u32[]{:S(2)}, u32[]{:S(2)}) collective-permute-start(bf16[2,96,384]{2,1,0:T(8,128)(2,1)} %refs_0_.3), channel_id=1, source_target_pairs={{0,8},{8,0},{16,24},{24,16},{1,9},{9,1},{17,25},{25,17},{2,10},{10... | collective-permute-start | bytes 442376 | tf_op jit(solution)/shard_map/ppermute | solution.py:78
  4.9 1.2 %dynamic_slice.3 = f32[1]{0:T(128)} dynamic-slice(f32[4]{0:T(128)} %param.13, s32[]{:T(128)S(6)} %select_n.3), dynamic_slice_sizes={1} | dynamic-slice | bytes 12 | tf_op jit(solution)/shard_map/dynamic_slice | solution.py:212
  6.8 6.5 %collective-permute-done.refs_1_ = bf16[2,96,384]{2,1,0:T(8,128)(2,1)S(1)} collective-permute-done((bf16[2,96,384]{2,1,0:T(8,128)(2,1)}, bf16[2,96,384]{2,1,0:T(8,128)(2,1)S(1)}, u32[]{:S(2)}, u32[]{:S(2)}) %collective-permute-start) | collective-permute-done | bytes 147488 | tf_op jit(solution)/shard_map/ppermute | solution.py:78
  13.3 0.0 collective-permute-start.2
  13.3 0.0 collective-permute-done.3.refs_1_
  13.3 0.5 %collective-permute-start.5 = (bf16[256,512]{1,0:T(8,128)(2,1)S(1)}, bf16[256,512]{1,0:T(8,128)(2,1)S(1)}, u32[]{:S(2)}, u32[]{:S(2)}) collective-permute-start(bf16[256,512]{1,0:T(8,128)(2,1)S(1)} %collective-permute-done.3.refs_1_), channel_id=1, source_target_pairs={{0,8},{8,0},{16,24},{24,16},{1,9},{9,1},{17,25},{25,17},{2,10},{10... | collective-permute-start | bytes 786440 | tf_op jit(solution)/shard_map/ppermute | solution.py:78
  13.9 3.3 %sine_negate_fusion.refs_6_ = f32[2,336,256]{2,1,0:T(8,128)S(1)} fusion(f32[2,336,256]{2,1,0:T(8,128)} %constant.45.clone, f32[]{:T(128)} %bitcast.5), kind=kLoop, calls=%fused_computation | loop fusion | flops 516096 | bytes 1376260 | tf_op jit(solution)/shard_map/neg | solution.py:212
  17.1 0.0 copy-start.7
  17.2 0.1 pad_add_fusion.place_ref
  17.2 0.0 collective-permute-done.4.refs_2_
  17.2 0.0 collective-permute-done.5.refs_3_
  17.3 0.0 copy-start.4
  17.3 1.0 %copy-done.4 = bf16[256,512]{1,0:T(8,128)(2,1)S(1)} copy-done((bf16[256,512]{1,0:T(8,128)(2,1)S(1)}, bf16[256,512]{1,0:T(8,128)(2,1)}, u32[]{:S(2)}) %copy-start.4) | copy-done | bytes 262168
  18.3 4.1 %shard_map.122.refs_4_ = f32[4,336,256]{2,1,0:T(8,128)S(1)} custom-call(s32[4]{0:T(128)S(1)} %pad_add_fusion.place_ref, bf16[256,512]{1,0:T(8,128)(2,1)S(1)} %copy-done.4, bf16[256,512]{1,0:T(8,128)(2,1)S(1)} %collective-permute-done.3.refs_1_, bf16[256,512]{1,0:T(8,128)(2,1)S(1)} %collective-permute-done.4.refs_2_, ...), custom_call_target="tpu_custom_call" | custom-call | tf_op jit(solution)/shard_map/pallas_call | solution.py:192
  22.4 0.0 collective-permute-done.1.refs_2_
  22.4 0.0 collective-permute-done.2.refs_3_
  22.5 3.8 %shard_map.123 = bf16[8,2,32,128]{3,2,1,0:T(8,128)(2,1)S(1)} custom-call(s32[4]{0:T(128)S(1)} %pad_add_fusion.place_ref, bf16[2,96,384]{2,1,0:T(8,128)(2,1)S(1)} %copy-done.5, bf16[2,96,384]{2,1,0:T(8,128)(2,1)S(1)} %collective-permute-done.refs_1_, bf16[2,96,384]{2,1,0:T(8,128)(2,1)S(1)} %collective-permute-done.1.refs_2_, ...), custom_call_target="tpu_custom_call" | custom-call | tf_op jit(solution)/shard_map/pallas_call | solution.py:192
  26.3 13.2 %all_to_all.5 = bf16[8,2,32,128]{3,2,1,0:T(8,128)(2,1)S(1)} all-to-all(bf16[8,2,32,128]{3,2,1,0:T(8,128)(2,1)S(1)} %shard_map.123), channel_id=1, replica_groups=mesh['tile'=4,'orient'=8] {'orient'}, dimensions={0} | all-to-all | bytes 262144 | tf_op jit(solution)/shard_map/all_to_all | solution.py:235
  39.6 0.6 %rsqrt_multiply_fusion = (f32[32,128]{1,0:T(8,128)}, f32[32,128]{1,0:T(8,128)}) fusion(f32[32,128]{1,0:T(8,128)S(1)} %get-tuple-element.3, f32[32,128]{1,0:T(8,128)S(1)} %get-tuple-element.2, bf16[32,128]{1,0:T(8,128)(2,1)S(1)} %reduce_max.14), kind=kLoop, calls=%fused_computation.4 | loop fusion | flops 32768 | bytes 73728 | tf_op jit(solution)/shard_map/div | solution.py:240
  (13 shorter events, 0.1 us)
Async XLA Ops:
  0.6 16.6 %copy-start.1 = (bf16[512,512]{1,0:T(8,128)(2,1)S(1)}, bf16[512,512]{1,0:T(8,128)(2,1)}, u32[]{:S(2)}) copy-start(bf16[512,512]{1,0:T(8,128)(2,1)} %constant.46.clone.refs_4_.refs_5_) | copy-start | bytes 1572868
  0.6 16.6 %copy-start = (bf16[672,640]{1,0:T(8,128)(2,1)S(1)}, bf16[672,640]{1,0:T(8,128)(2,1)}, u32[]{:S(2)}) copy-start(bf16[672,640]{1,0:T(8,128)(2,1)} %constant.47.clone.refs_5_.refs_6_) | copy-start | bytes 2580484
  0.7 12.7 %collective-permute-start.3 = (bf16[256,512]{1,0:T(8,128)(2,1)}, bf16[256,512]{1,0:T(8,128)(2,1)S(1)}, u32[]{:S(2)}, u32[]{:S(2)}) collective-permute-start(bf16[256,512]{1,0:T(8,128)(2,1)} %refs_0_.2), channel_id=1, source_target_pairs={{0,16},{8,24},{16,0},{24,8},{1,17},{9,25},{17,1},{25,9},{2,18},{10... | collective-permute-start | bytes 786440 | tf_op jit(solution)/shard_map/ppermute | solution.py:78
  3.7 9.7 %collective-permute-start = (bf16[2,96,384]{2,1,0:T(8,128)(2,1)}, bf16[2,96,384]{2,1,0:T(8,128)(2,1)S(1)}, u32[]{:S(2)}, u32[]{:S(2)}) collective-permute-start(bf16[2,96,384]{2,1,0:T(8,128)(2,1)} %refs_0_.3), channel_id=1, source_target_pairs={{0,16},{8,24},{16,0},{24,8},{1,17},{9,25},{17,1},{25,9},{2,18},{10... | collective-permute-start | bytes 442376 | tf_op jit(solution)/shard_map/ppermute | solution.py:78
  3.7 13.5 %collective-permute-start.4 = (bf16[256,512]{1,0:T(8,128)(2,1)}, bf16[256,512]{1,0:T(8,128)(2,1)S(1)}, u32[]{:S(2)}, u32[]{:S(2)}) collective-permute-start(bf16[256,512]{1,0:T(8,128)(2,1)} %refs_0_.2), channel_id=1, source_target_pairs={{0,8},{8,0},{16,24},{24,16},{1,9},{9,1},{17,25},{25,17},{2,10},{10... | collective-permute-start | bytes 786440 | tf_op jit(solution)/shard_map/ppermute | solution.py:78
  3.7 18.7 %collective-permute-start.1 = (bf16[2,96,384]{2,1,0:T(8,128)(2,1)}, bf16[2,96,384]{2,1,0:T(8,128)(2,1)S(1)}, u32[]{:S(2)}, u32[]{:S(2)}) collective-permute-start(bf16[2,96,384]{2,1,0:T(8,128)(2,1)} %refs_0_.3), channel_id=1, source_target_pairs={{0,8},{8,0},{16,24},{24,16},{1,9},{9,1},{17,25},{25,17},{2,10},{10... | collective-permute-start | bytes 442376 | tf_op jit(solution)/shard_map/ppermute | solution.py:78
  13.3 9.1 %collective-permute-start.2 = (bf16[2,96,384]{2,1,0:T(8,128)(2,1)S(1)}, bf16[2,96,384]{2,1,0:T(8,128)(2,1)S(1)}, u32[]{:S(2)}, u32[]{:S(2)}) collective-permute-start(bf16[2,96,384]{2,1,0:T(8,128)(2,1)S(1)} %collective-permute-done.refs_1_), channel_id=1, source_target_pairs={{0,8},{8,0},{16,24},{24,16},{1,9},{9,1},{17,25},{25,17},{2,10},{10... | collective-permute-start | bytes 442376 | tf_op jit(solution)/shard_map/ppermute | solution.py:78
  13.3 3.9 %collective-permute-start.5 = (bf16[256,512]{1,0:T(8,128)(2,1)S(1)}, bf16[256,512]{1,0:T(8,128)(2,1)S(1)}, u32[]{:S(2)}, u32[]{:S(2)}) collective-permute-start(bf16[256,512]{1,0:T(8,128)(2,1)S(1)} %collective-permute-done.3.refs_1_), channel_id=1, source_target_pairs={{0,8},{8,0},{16,24},{24,16},{1,9},{9,1},{17,25},{25,17},{2,10},{10... | collective-permute-start | bytes 786440 | tf_op jit(solution)/shard_map/ppermute | solution.py:78
  17.1 5.3 %copy-start.7 = (f32[1,512]{1,0:T(1,128)S(1)}, f32[1,512]{1,0:T(1,128)}, u32[]{:S(2)}) copy-start(f32[1,512]{1,0:T(1,128)} %constant.51.clone.refs_10_) | copy-start | bytes 6148
  17.2 5.2 %copy-start.2 = (bf16[256,672]{1,0:T(8,128)(2,1)S(1)}, bf16[256,672]{1,0:T(8,128)(2,1)}, u32[]{:S(2)}) copy-start(bf16[256,672]{1,0:T(8,128)(2,1)} %constant.49.clone.refs_8_) | copy-start | bytes 1032196
  17.2 5.2 %copy-start.3 = (f32[672,1]{1,0:T(8,128)S(1)}, f32[672,1]{1,0:T(8,128)}, u32[]{:S(2)}) copy-start(f32[672,1]{1,0:T(8,128)} %constant.50.clone.refs_9_) | copy-start | bytes 8068
  17.3 1.0 %copy-start.4 = (bf16[256,512]{1,0:T(8,128)(2,1)S(1)}, bf16[256,512]{1,0:T(8,128)(2,1)}, u32[]{:S(2)}) copy-start(bf16[256,512]{1,0:T(8,128)(2,1)} %refs_0_.2) | copy-start | bytes 786436
  18.3 4.2 %copy-start.5 = (bf16[2,96,384]{2,1,0:T(8,128)(2,1)S(1)}, bf16[2,96,384]{2,1,0:T(8,128)(2,1)}, u32[]{:S(2)}) copy-start(bf16[2,96,384]{2,1,0:T(8,128)(2,1)} %refs_0_.3) | copy-start | bytes 442372
  18.3 4.2 %copy-start.6 = (bf16[512,128]{1,0:T(8,128)(2,1)S(1)}, bf16[512,128]{1,0:T(8,128)(2,1)}, u32[]{:S(2)}) copy-start(bf16[512,128]{1,0:T(8,128)(2,1)} %constant.48.clone.refs_7_) | copy-start | bytes 393220
where the time goes:
time: 40.4 us; the launch traced here: 40.2 us
  blocking collectives  13.2 us (33%)
  Pallas kernels  7.9 us (20%)
  waiting for transfers between devices  6.55 us (16%)
  starting transfers between devices  4.1 us (10%)
  other arithmetic  4.04 us (10%)
  local copies, waits for them, and re-layouts  2.29 us (6%)
  between operations  2.09 us (5%)
    all_to_all x1, blocking collectives, local(): lax.all_to_all(scores, 'orient', split_axis=0, concat_axis=0, tiled=True)  13.2 us
    pallas_call x2, Pallas kernels, on_device(): pl.pallas_call(kernel, out_shape=result, in_specs=[smem] + [vmem] * (len(...  7.9 us
    ppermute x6, waiting for transfers between devices, gather_blocks(): held = held + [lax.ppermute(block, axis, pairs) for block in held]  6.55 us
    ppermute x6, starting transfers between devices, gather_blocks(): held = held + [lax.ppermute(block, axis, pairs) for block in held]  4.1 us
    neg x1, other arithmetic, local(): -jnp.sin(jnp.float32(math.pi) * defocus[group_of_tile[0]] * radius + 0.07)  3.27 us
    dynamic_slice x1, local copies, waits for them, and re-layouts, local(): defocus[group_of_tile[0]]  1.24 us
    unnamed x16, local copies, waits for them, and re-layouts  1.04 us
  transfers between devices with their start and end apart: 6, of which 1 were waited for; matrix products, arithmetic and copies ran while one was open for 11% of the time, Pallas kernels for 10%

commit v1 on v0

v1 whole, which is shorter than its diff:
```python
import functools
import math

import jax
import jax.numpy as jnp
import ml_dtypes
import numpy as np
from jax import lax
from jax.experimental import pallas as pl
from jax.experimental.pallas import tpu as pltpu
from jax.sharding import PartitionSpec as P

TS = 384
STRIP = 256
OUTC = 128
CHUNK = 16
VMEM_BYTES = 40 * 1024 * 1024


def cos_sin(freqs, places, modulus):
    residue = freqs[:, None] * places[None, :] % modulus
    lowest = np.minimum(residue, modulus - residue)
    flipped = np.where(residue > modulus - residue, -1.0, 1.0).astype(np.float32)
    angle = lowest.astype(np.float32) * np.float32(2.0 * math.pi / modulus)
    sine = np.where(2 * lowest == modulus, np.float32(0.0), flipped * np.sin(angle))
    return np.cos(angle).astype(np.float32), sine.astype(np.float32)


def round_up(value, multiple):
    return -(-value // multiple) * multiple


@functools.lru_cache(maxsize=None)
def tables(width_rows, width_cols):
    half = width_cols // 2
    rows = width_rows // 2 + 1
    padded = round_up(rows, CHUNK)
    bf16 = ml_dtypes.bfloat16
    places = np.arange(width_cols)
    cos_v, sin_v = cos_sin(np.arange(half + 1), places, width_cols)
    packed_sin = sin_v[:half].copy()
    forward_sin = -packed_sin
    forward_sin[0] = cos_v[half]
    packed_sin[0] = cos_v[half]
    col = np.concatenate([cos_v[:half], forward_sin], 0).T.astype(bf16)
    back = (2.0 * np.concatenate([cos_v[:half], packed_sin], 0)[:, :OUTC].astype(bf16).astype(np.float32)).astype(bf16)
    cos_u, sin_u = cos_sin(np.arange(rows), np.arange(width_rows), width_rows)
    row = np.zeros((2 * padded, width_rows), np.float32)
    row[:rows] = cos_u
    row[padded : padded + rows] = -sin_u
    row = row.astype(bf16)
    weight = np.ones((rows, 1), np.float32)
    weight[0] = weight[-1] = 0.5
    out = np.zeros((2 * padded, STRIP), np.float32)
    out[:rows] = cos_u[:, :STRIP].astype(bf16).astype(np.float32) * weight
    out[padded : padded + rows] = sin_u[:, :STRIP].astype(bf16).astype(np.float32) * weight
    out = np.ascontiguousarray(out.T).astype(bf16)
    row_sum = row[:, :TS].astype(np.float32).sum(1, keepdims=True)
    col_sum = col[:TS].astype(np.float32).sum(0, keepdims=True)
    return col, row, back, out, row_sum, col_sum


def swapped(value, axis, step):
    count = lax.axis_size(axis)
    return lax.ppermute(value, axis, [(source, source ^ step) for source in range(count)])


def spread_out(value, axis):
    held, step = {0: value}, lax.axis_size(axis) // 2
    while step > 1:
        held |= {index ^ step: swapped(block, axis, step) for index, block in held.items()}
        step //= 2
    return [held[index] for index in sorted(held)[1:]]


def first_column(shape):
    return lax.broadcasted_iota(jnp.int32, shape, 1) == 0


def both_signs(cc, cs, sc, ss, first):
    plus_re = cc - jnp.where(first, 0.0, ss)
    plus_im = jnp.where(first, 0.0, cs) + sc
    minus_re = jnp.where(first, cs, cc + ss)
    minus_im = jnp.where(first, ss, cs - sc)
    return plus_re, plus_im, minus_re, minus_im


def quadrants(load, r, padded, half, first):
    up, down = load(slice(r, r + CHUNK)), load(slice(padded + r, padded + r + CHUNK))
    return both_signs(up[:, :half], up[:, half:], down[:, :half], down[:, half:], first)


def dot(left, right):
    return jnp.dot(left, right, preferred_element_type=jnp.float32)


def moments(block):
    wide = block.astype(jnp.float32)
    return jnp.sum(wide, axis=0, keepdims=True), jnp.sum(wide * wide, axis=0, keepdims=True)


def early_kernel(
    tile_ref, ctf_ref, strip_b, tpl_b, strip_hbm, tpl_hbm, col_hbm, row_hbm, deep_hbm,
    column_ref, partial_ref, raw_ref, shape_ref, moment_ref,
    strip_a, tpl_a, col_ref, row_ref, deep_ref, order_ref, sems,
):
    tile = tile_ref[0]
    bit, pair = tile & 1, tile >> 1
    padded, half = row_ref.shape[0] // 2, col_ref.shape[1] // 2
    pending = {}

    def fetch(name, source, target, pieces):
        step = target.shape[0] // pieces
        pending[name] = []
        for k in range(pieces):
            number = sum(map(len, pending.values()))
            rows = pl.ds(k * step, step)
            copy = pltpu.make_async_copy(source.at[rows], target.at[rows], sems.at[number])
            copy.start()
            pending[name].append(copy)

    def ready(name):
        for copy in pending[name]:
            copy.wait()

    fetch("strip", strip_hbm, strip_a, 1)
    fetch("col", col_hbm, col_ref, 2)
    fetch("row", row_hbm, row_ref, 3)
    fetch("tpl", tpl_hbm, tpl_a, 1)
    pending["deep"] = [pltpu.make_async_copy(deep_hbm.at[pair], deep_ref, sems.at[7])]
    pending["deep"][0].start()

    ready("strip")
    ready("col")
    for j, strip in enumerate((strip_a, strip_b)):
        start = pl.multiple_of((bit ^ j) * STRIP, STRIP)
        column_ref[pl.ds(start, STRIP), :] = dot(strip[...], col_ref[...]).astype(jnp.bfloat16)
    ready("row")
    partial_ref[0] = dot(row_ref[:, : 2 * STRIP], column_ref[...])
    partial_ref[1] = dot(row_ref[:, :STRIP], column_ref[STRIP:, :])
    ready("tpl")
    mine, depth = raw_ref.shape[0], tpl_a.shape[1]
    for index in range(mine):
        for j, block in enumerate((tpl_a, tpl_b)):
            start = pl.multiple_of((bit ^ j) * depth, depth)
            order_ref[index, pl.ds(start, depth), :] = block[bit * mine + index].astype(order_ref.dtype)
    raw_ref[...] = order_ref[...].astype(jnp.bfloat16)
    ready("deep")
    for index in range(mine):
        for k, moment in enumerate(moments(raw_ref[index])):
            moment_ref[2 * index + k : 2 * index + k + 1, :] = moment
        shape_ref[index] = dot(deep_ref[...], dot(raw_ref[index], col_ref[:TS, :]).astype(jnp.bfloat16))


def ctf_kernel(half, width_rows, tile_ref, group_a, group_b, defocus_ref, ctf_ref):
    bit = tile_ref[0] & 1
    padded = ctf_ref.shape[2]
    u = lax.broadcasted_iota(jnp.int32, (8, round_up(padded, 128)), 1).astype(jnp.float32) / width_rows
    column = lax.broadcasted_iota(jnp.int32, (8, half), 1)
    wrapped = (lax.broadcasted_iota(jnp.int32, (8, half), 0) == 1) & (column == 0)
    v = jnp.where(wrapped, half, column).astype(jnp.float32) / (2 * half)
    for k in range(2):
        turn = jnp.float32(math.pi) * defocus_ref[jnp.where(bit == k, group_a[0], group_b[0])]
        phase_u, phase_v = turn * (u * u) + 0.07, turn * (v * v)
        sin_u, cos_u = jnp.sin(phase_u).T[:padded, :1], jnp.cos(phase_u).T[:padded, :1]
        sin_v, cos_v = jnp.sin(phase_v), jnp.cos(phase_v)
        for side in range(2):
            for r in range(0, padded, CHUNK):
                up = slice(r, r + CHUNK)
                ctf_ref[k, side, up] = -(
                    sin_u[up] * cos_v[side : side + 1] + cos_u[up] * sin_v[side : side + 1]
                )


def spectrum_kernel(count, tile_ref, *refs):
    others = refs[: count - 2]
    (column_ref, partial_ref, ctf_ref, col_ref, row_ref, weighted_ref) = refs[count - 2 : count + 4]
    part_ref, cross_ref, work_ref, power_ref = refs[count + 4 :]
    padded, half = row_ref.shape[0] // 2, col_ref.shape[1] // 2
    width_rows, width_cols = row_ref.shape[1], col_ref.shape[0]
    tile = tile_ref[0]
    bit = tile & 1
    pairs = count // 2
    first = first_column((CHUNK, half))

    def rows_of(pair, offset, length):
        return pl.ds(pl.multiple_of(pair * (2 * STRIP), 2 * STRIP) + offset, length)

    for j in range(2, count):
        start = pl.multiple_of((tile ^ j) * STRIP, STRIP)
        part_ref[pl.ds(start, STRIP), :] = dot(others[j - 2][...], col_ref[...]).astype(jnp.bfloat16)
    if pairs > 1:
        part_ref[rows_of(tile >> 1, 0, 2 * STRIP), :] = column_ref[...]

    def add_power(loads, fresh):
        for r in range(0, padded, CHUNK):
            up = slice(r, r + CHUNK)
            plus, minus = 0.0, 0.0
            for load in loads:
                signs = quadrants(load, r, padded, half, first)
                plus = plus + (signs[0] * signs[0] + signs[1] * signs[1])
                minus = minus + (signs[2] * signs[2] + signs[3] * signs[3])
            power_ref[0, up] = plus if fresh else power_ref[0, up] + plus
            power_ref[1, up] = minus if fresh else power_ref[1, up] + minus

    own = tile >> 1

    @pl.when(own + 1 < pairs)
    def _():
        cross_ref[0] = dot(row_ref[:, 2 * STRIP :], part_ref[rows_of(own + 1, 0, width_rows - 2 * STRIP), :])
        cross_ref[1] = dot(row_ref[:, STRIP:], part_ref[rows_of(own + 1, 0, width_rows - STRIP), :])
        add_power([lambda s, k=k: partial_ref[k, s] + cross_ref[k, s] for k in range(2)], True)

    @pl.when(own + 1 == pairs)
    def _():
        add_power([lambda s, k=k: partial_ref[k, s] for k in range(2)], True)

    for j in range(1, pairs):
        pair = own ^ j

        @pl.when(pair + 1 < pairs)
        def _():
            work_ref[0] = dot(row_ref[...], part_ref[rows_of(pair, 0, width_rows), :])
            work_ref[1] = dot(row_ref[...], part_ref[rows_of(pair, STRIP, width_rows), :])

        @pl.when(pair + 1 == pairs)
        def _():
            work_ref[0] = dot(row_ref[:, : 2 * STRIP], part_ref[rows_of(pair, 0, 2 * STRIP), :])
            work_ref[1] = dot(row_ref[:, :STRIP], part_ref[rows_of(pair, STRIP, STRIP), :])

        add_power([lambda s, k=k: work_ref[k, s] for k in range(2)], False)

    total = jnp.zeros((CHUNK, half), jnp.float32)
    for r in range(0, padded, CHUNK):
        total = total + (power_ref[0, r : r + CHUNK] + power_ref[1, r : r + CHUNK])
    last = width_rows // 2
    ends = (power_ref[0, 0:1] + power_ref[1, 0:1]) + (power_ref[0, last : last + 1] + power_ref[1, last : last + 1])
    mean = (2.0 * jnp.sum(total, keepdims=True) - jnp.sum(ends, keepdims=True)) / (count * width_rows * width_cols)

    def weigh(loads):
        for r in range(0, padded, CHUNK):
            up = slice(r, r + CHUNK)
            gains = [lax.rsqrt(power_ref[side, up] * (1.0 / count) + mean) for side in range(2)]
            for k, load in enumerate(loads):
                signs = quadrants(load, r, padded, half, first)
                for side in range(2):
                    gain = gains[side] * ctf_ref[k, side, up]
                    weighted_ref[k, 2 * side, up] = signs[2 * side] * gain
                    weighted_ref[k, 2 * side + 1, up] = signs[2 * side + 1] * gain

    @pl.when(own + 1 < pairs)
    def _():
        weigh([lambda s, k=k: partial_ref[k, s] + cross_ref[k, s] for k in range(2)])

    @pl.when(own + 1 == pairs)
    def _():
        weigh([lambda s, k=k: partial_ref[k, s] for k in range(2)])


def score_kernel(count, tile_ref, *refs):
    pairs = count // 2
    others = refs[: pairs - 1]
    (weighted_ref, shape_ref, moment_ref, col_ref, deep_ref, back_ref, out_ref, row_sum_ref, col_sum_ref) = refs[
        pairs - 1 : pairs + 8
    ]
    score_ref, quad_ref, product_ref = refs[pairs + 8 :]
    padded, half = deep_ref.shape[1] // 2, col_ref.shape[1] // 2
    scale = 1.0 / ((STRIP + TS) * col_ref.shape[0])
    first = first_column((CHUNK, half))
    pieces, mine = score_ref.shape[:2]
    own = tile_ref[0] >> 1
    for index in range(mine):
        sums, squares = (moment_ref[2 * index + k : 2 * index + k + 1, :] for k in range(2))
        for j in range(1, pairs):
            raw = others[j - 1][index]
            late = dot(deep_ref[own ^ j], dot(raw, col_ref[:TS, :]).astype(jnp.bfloat16))
            quad_ref[...] = late if j == 1 else quad_ref[...] + late
            more = moments(raw)
            sums, squares = sums + more[0], squares + more[1]
        mean = jnp.sum(sums, keepdims=True) / (TS * TS)
        spread = jnp.sqrt(jnp.sum(squares, keepdims=True) / (TS * TS) - mean * mean + 1e-05)
        col_sum = mean * col_sum_ref[...]

        def load(s):
            known = shape_ref[index, s] + quad_ref[s] if pairs > 1 else shape_ref[index, s]
            return known - row_sum_ref[s, :] * col_sum

        for r in range(0, padded, CHUNK):
            up, down = slice(r, r + CHUNK), slice(padded + r, padded + r + CHUNK)
            a, b, c, d = quadrants(load, r, padded, half, first)
            for k in range(2):
                p, q, s, t = (weighted_ref[k, m, up] for m in range(4))
                plus_re = p * a + q * b
                plus_im = q * a - p * b
                minus_re = s * c + t * d
                minus_im = t * c - s * d
                product_ref[k, up, :half] = (plus_re + jnp.where(first, 0.0, minus_re)).astype(jnp.bfloat16)
                product_ref[k, up, half:] = jnp.where(first, minus_re, -(plus_im + minus_im)).astype(jnp.bfloat16)
                product_ref[k, down, :half] = (jnp.where(first, 0.0, minus_im) - plus_im).astype(jnp.bfloat16)
                product_ref[k, down, half:] = jnp.where(first, -minus_im, minus_re - plus_re).astype(jnp.bfloat16)
        for k in range(2):
            back = dot(product_ref[k], back_ref[...]).astype(jnp.bfloat16)
            score = (dot(out_ref[...], back) * (scale / spread)).reshape(pieces // 2, 2 * STRIP // pieces, OUTC)
            score_ref[k * (pieces // 2) : (k + 1) * (pieces // 2), index] = score.astype(jnp.bfloat16)


def on_device(kernel, scalars, operands, tables_in_hbm, scratch, result, flops):
    vmem, smem, hbm = (pl.BlockSpec(memory_space=space) for space in (pltpu.VMEM, pltpu.SMEM, pltpu.HBM))
    return pl.pallas_call(
        kernel,
        out_shape=result,
        in_specs=[smem] * len(scalars) + [vmem] * len(operands) + [hbm] * len(tables_in_hbm),
        out_specs=jax.tree.map(lambda _: vmem, result),
        scratch_shapes=scratch,
        compiler_params=pltpu.CompilerParams(vmem_limit_bytes=VMEM_BYTES),
        cost_estimate=pl.CostEstimate(flops=flops, bytes_accessed=0, transcendentals=0),
    )(*scalars, *operands, *tables_in_hbm)


def local(micrograph, templates, defocus, group_of_tile):
    width_cols = micrograph.shape[1]
    width_rows = STRIP + TS
    tpl_count, depth = templates.shape[:2]
    count = lax.axis_size("tile")
    orient_count = lax.axis_size("orient")
    col, row, back, out, row_sum, col_sum = tables(width_rows, width_cols)
    deep = np.stack(np.split(row[:, :TS], count // 2, axis=1))
    padded, half = row.shape[0] // 2, width_cols // 2
    tile = lax.axis_index("tile").astype(jnp.int32).reshape(1)
    plane, quads = (padded, half), (2 * padded, width_cols)
    f32, bf16 = jnp.float32, jnp.bfloat16
    mine = tpl_count // 2
    pass_flops = 2 * quads[0] * quads[1] * STRIP

    strips = spread_out(micrograph, "tile")
    held = [micrograph, templates, col, row, deep]
    ctf = on_device(
        functools.partial(ctf_kernel, half, width_rows),
        [tile, group_of_tile, swapped(group_of_tile, "tile", 1), defocus],
        [],
        [],
        [],
        jax.ShapeDtypeStruct((2, 2, *plane), f32),
        24 * pass_flops,
    )
    early = on_device(
        early_kernel,
        [tile],
        [ctf, swapped(micrograph, "tile", 1), swapped(templates, "tile", 1)],
        held,
        [pltpu.VMEM(a.shape if a is not deep else a.shape[1:], a.dtype) for a in held]
        + [
            pltpu.VMEM((mine, 2 * depth, TS), bf16 if depth % 16 == 0 else f32),
            pltpu.SemaphoreType.DMA((10,)),
        ],
        (
            jax.ShapeDtypeStruct((2 * STRIP, width_cols), bf16),
            jax.ShapeDtypeStruct((2, *quads), f32),
            jax.ShapeDtypeStruct((mine, 2 * depth, TS), bf16),
            jax.ShapeDtypeStruct((mine, *quads), f32),
            jax.ShapeDtypeStruct((round_up(2 * mine, 8), TS), f32),
        ),
        12 * pass_flops,
    )
    column, partial, raw, shape, moment = early
    strips, column = lax.optimization_barrier((strips, column))
    pieces = spread_out(raw, "tile")
    strips = [block for strip in strips for block in (strip, swapped(strip, "tile", 1))]
    weighted = on_device(
        functools.partial(spectrum_kernel, count),
        [tile],
        [*strips, column, partial, ctf, col, row],
        [],
        [
            pltpu.VMEM((count * STRIP, width_cols), bf16),
            pltpu.VMEM((2, *quads), f32),
            pltpu.VMEM((2, *quads), f32),
            pltpu.VMEM((2, *plane), f32),
        ],
        jax.ShapeDtypeStruct((2, 4, *plane), f32),
        14 * pass_flops,
    )
    pieces, weighted = lax.optimization_barrier((pieces, weighted))
    scores = on_device(
        functools.partial(score_kernel, count),
        [tile],
        [*pieces, weighted, shape, moment, col, deep, back, out, row_sum, col_sum],
        [],
        [pltpu.VMEM(quads, f32), pltpu.VMEM((2, *quads), bf16)],
        jax.ShapeDtypeStruct((2 * orient_count, mine, STRIP // orient_count, OUTC), bf16),
        12 * pass_flops,
    )
    chips = [[first + k for k in range(2 * orient_count)] for first in range(0, count * orient_count, 2 * orient_count)]
    received = lax.all_to_all(
        scores, ("tile", "orient"), split_axis=0, concat_axis=0, tiled=True, axis_index_groups=chips
    ).astype(f32)
    orient_total = tpl_count * orient_count
    best = jnp.max(received, axis=(0, 1))
    score_mean = jnp.sum(received, axis=(0, 1)) / orient_total
    score_var = jnp.sum(received * received, axis=(0, 1)) / orient_total - score_mean * score_mean
    return (best, (best - score_mean) / jnp.sqrt(score_var + 1e-05))


def solution(mesh):
    placed = (P("tile", None), P("orient", "tile", None), P(), P("tile"))
    return jax.shard_map(
        local,
        mesh=mesh,
        in_specs=placed,
        out_specs=(P(("tile", "orient"), None), P(("tile", "orient"), None)),
        check_vma=False,
    )
```

time: 40.4 us -> 34 us (0.84)
  waiting for transfers between devices: 6.55 us -> 2.29 us
  other arithmetic: 4.04 us -> 0.69 us
  Pallas kernels: 7.9 us -> 9.73 us
  local copies, waits for them, and re-layouts: 2.29 us -> 0.69 us
  starting transfers between devices: 4.1 us -> 5.35 us
  between operations: 2.09 us -> 1.42 us
  blocking collectives: 13.2 us -> 13.7 us
    ppermute x6, waiting for transfers between devices: 6.55 us -> 2.29 us  [swapped(): lax.ppermute(value, axis, [(source, source ^ step) for source in range(co...]
    neg x1 -> x0, other arithmetic: 3.27 us -> none  [local(): -jnp.sin(jnp.float32(math.pi) * defocus[group_of_tile[0]] * radius + 0.07)]
    pallas_call x2 -> x4, Pallas kernels: 7.9 us -> 9.73 us  [on_device(): pl.pallas_call(kernel, out_shape=result, in_specs=[smem] * len(scalars) +...]
    ppermute x6, starting transfers between devices: 4.1 us -> 5.35 us  [swapped(): lax.ppermute(value, axis, [(source, source ^ step) for source in range(co...]
    dynamic_slice x1 -> x0, local copies, waits for them, and re-layouts: 1.24 us -> none  [local(): defocus[group_of_tile[0]]]
    all_to_all x1, blocking collectives: 13.2 us -> 13.7 us  [local(): lax.all_to_all(scores, ('tile', 'orient'), split_axis=0, concat_axis=0, t...]
    unnamed x16 -> x20, local copies, waits for them, and re-layouts: 1.04 us -> 0.69 us
  transfers between devices with their start and end apart: 6 -> 6, of which waited for: 1 -> 3; matrix products, arithmetic and copies ran while one was open for 11% -> 0% of each run, Pallas kernels for 10% -> 22%
where the time goes in v1:
time: 34 us; the launch traced here: 33.8 us
  blocking collectives  13.7 us (40%)
  Pallas kernels  9.73 us (29%)
  starting transfers between devices  5.35 us (16%)
  waiting for transfers between devices  2.29 us (7%)
  between operations  1.42 us (4%)
  local copies, waits for them, and re-layouts  0.69 us (2%)
  other arithmetic  0.69 us (2%)
    all_to_all x1, blocking collectives, local(): lax.all_to_all(scores, ('tile', 'orient'), split_axis=0, concat_axis=0, t...  13.7 us
    pallas_call x4, Pallas kernels, on_device(): pl.pallas_call(kernel, out_shape=result, in_specs=[smem] * len(scalars) +...  9.73 us
    ppermute x6, starting transfers between devices, swapped(): lax.ppermute(value, axis, [(source, source ^ step) for source in range(co...  5.35 us
    ppermute x6, waiting for transfers between devices, swapped(): lax.ppermute(value, axis, [(source, source ^ step) for source in range(co...  2.29 us
    unnamed x20, local copies, waits for them, and re-layouts  0.69 us
  transfers between devices with their start and end apart: 6, of which 3 were waited for; matrix products, arithmetic and copies ran while one was open for 0% of the time, Pallas kernels for 22%

profile of v1, /device:TPU:0, one launch (start us, length us, event | category | flops | bytes accessed | tf_op | source)
XLA Modules:
  0.0 33.8 jit_solution(5260286155542067032)
XLA Ops:
  0.6 0.5 %collective-permute-start.1 = (bf16[256,512]{1,0:T(8,128)(2,1)}, bf16[256,512]{1,0:T(8,128)(2,1)S(1)}, u32[]{:S(2)}, u32[]{:S(2)}) collective-permute-start(bf16[256,512]{1,0:T(8,128)(2,1)} %strip_hbm.1), channel_id=1, source_target_pairs={{0,8},{8,0},{16,24},{24,16},{1,9},{9,1},{17,25},{25,17},{2,10},{10... | collective-permute-start | bytes 786440 | tf_op jit(solution)/shard_map/ppermute | solution.py:65
  1.1 2.6 %collective-permute-start.4 = (bf16[256,512]{1,0:T(8,128)(2,1)}, bf16[256,512]{1,0:T(8,128)(2,1)S(1)}, u32[]{:S(2)}, u32[]{:S(2)}) collective-permute-start(bf16[256,512]{1,0:T(8,128)(2,1)} %strip_hbm.1), channel_id=1, source_target_pairs={{0,16},{8,24},{16,0},{24,8},{1,17},{9,25},{17,1},{25,9},{2,18},{10... | collective-permute-start | bytes 786440 | tf_op jit(solution)/shard_map/ppermute | solution.py:65
  3.7 0.2 collective-permute-start
  3.9 0.3 %collective-permute-start.2 = (bf16[2,96,384]{2,1,0:T(8,128)(2,1)}, bf16[2,96,384]{2,1,0:T(8,128)(2,1)S(1)}, u32[]{:S(2)}, u32[]{:S(2)}) collective-permute-start(bf16[2,96,384]{2,1,0:T(8,128)(2,1)} %tpl_hbm.1), channel_id=1, source_target_pairs={{0,8},{8,0},{16,24},{24,16},{1,9},{9,1},{17,25},{25,17},{2,10},{10... | collective-permute-start | bytes 442376 | tf_op jit(solution)/shard_map/ppermute | solution.py:65
  4.9 0.2 collective-permute-done.group_b
  5.1 0.7 %copy-done.4 = f32[4]{0:T(128)S(1)} copy-done((f32[4]{0:T(128)S(1)}, f32[4]{0:T(128)}, u32[]{:S(2)}) %copy-start.4) | copy-done | bytes 40
  5.8 0.0 copy-start.5
  5.8 1.9 %shard_map.122.ctf_ref.refs_4_ = f32[2,2,336,256]{3,2,1,0:T(8,128)S(1)} custom-call(s32[1]{0:T(128)} %bitcast.tile_ref, s32[1]{0:T(128)S(6)} %copy.13.group_a, s32[1]{0:T(128)} %collective-permute-done.group_b, f32[4]{0:T(128)S(1)} %copy-done.4), custom_call_target="tpu_custom_call" | custom-call | flops 4227858432 | tf_op jit(solution)/shard_map/pallas_call | solution.py:309
  7.7 0.0 collective-permute-done.2.tpl_b
  7.7 0.0 collective-permute-done.1.strip_b
  7.7 0.0 copy-done
  7.7 0.0 copy-done.1
  7.7 2.4 %shard_map.123 = (bf16[512,512]{1,0:T(8,128)(2,1)S(1)}, f32[2,672,512]{2,1,0:T(8,128)S(1)}, bf16[1,192,384]{2,1,0:T(8,128)(2,1)S(1)}, f32[1,672,512]{2,1,0:T(8,128)S(1)}, f32[8,384]{1,0:T(8,128)S(1)}) custom-call(s32[1]{0:T(128)} %bitcast.tile_ref, f32[2,2,336,256]{3,2,1,0:T(8,128)S(1)} %shard_map.122.ctf_ref.refs_4_, ...), custom_call_target="tpu_custom_call" | custom-call | flops 2113929216 | tf_op jit(solution)/shard_map/pallas_call | solution.py:309
  10.1 0.7 %collective-permute-done.4.refs_0_ = bf16[256,512]{1,0:T(8,128)(2,1)S(1)} collective-permute-done((bf16[256,512]{1,0:T(8,128)(2,1)}, bf16[256,512]{1,0:T(8,128)(2,1)S(1)}, u32[]{:S(2)}, u32[]{:S(2)}) %collective-permute-start.4) | collective-permute-done | bytes 262176 | tf_op jit(solution)/shard_map/ppermute | solution.py:65
  10.8 0.0 collective-permute-start.5
  10.8 1.8 %collective-permute-start.3 = (bf16[1,192,384]{2,1,0:T(8,128)(2,1)S(1)}, bf16[1,192,384]{2,1,0:T(8,128)(2,1)S(1)}, u32[]{:S(2)}, u32[]{:S(2)}) collective-permute-start(bf16[1,192,384]{2,1,0:T(8,128)(2,1)S(1)} %get-tuple-element.11), channel_id=1, source_target_pairs={{0,16},{8,24},{16,0},{24,8},{1,17},{9,25},{17,1},{25,9},{2,18},{10... | collective-permute-start | bytes 442376 | tf_op jit(solution)/shard_map/ppermute | solution.py:65
  12.6 0.0 collective-permute-done.5.refs_1_
  12.6 0.0 copy-start.9
  12.6 3.1 %shard_map.124.refs_1_ = f32[2,4,336,256]{3,2,1,0:T(8,128)S(1)} custom-call(s32[1]{0:T(128)} %bitcast.tile_ref, bf16[256,512]{1,0:T(8,128)(2,1)S(1)} %collective-permute-done.4.refs_0_, bf16[256,512]{1,0:T(8,128)(2,1)S(1)} %collective-permute-done.5.refs_1_, bf16[512,512]{1,0:T(8,128)(2,1)S(1)} %get-tuple-element.14.refs_2_, ...), custom_call_target="tpu_custom_call" | custom-call | flops 2466250752 | tf_op jit(solution)/shard_map/pallas_call | solution.py:309
  15.8 1.3 %collective-permute-done.3.refs_0_ = bf16[1,192,384]{2,1,0:T(8,128)(2,1)S(1)} collective-permute-done((bf16[1,192,384]{2,1,0:T(8,128)(2,1)S(1)}, bf16[1,192,384]{2,1,0:T(8,128)(2,1)S(1)}, u32[]{:S(2)}, u32[]{:S(2)}) %collective-permute-start.3) | collective-permute-done | bytes 147488 | tf_op jit(solution)/shard_map/ppermute | solution.py:65
  17.1 0.0 copy-done.9
  17.1 2.4 %shard_map.125 = bf16[16,1,32,128]{3,2,1,0:T(8,128)(2,1)S(1)} custom-call(s32[1]{0:T(128)} %bitcast.tile_ref, bf16[1,192,384]{2,1,0:T(8,128)(2,1)S(1)} %collective-permute-done.3.refs_0_, f32[2,4,336,256]{3,2,1,0:T(8,128)S(1)} %shard_map.124.refs_1_, f32[1,672,512]{2,1,0:T(8,128)S(1)} %get-tuple-element.18.refs_2_, f32[8,384]{1,0:T(8,128)S(1)} %get-tuple-element.19.refs_3_, ...), custom_call_target="tpu_custom_call" | custom-call | flops 2113929216 | tf_op jit(solution)/shard_map/pallas_call | solution.py:309
  19.5 13.7 %all_to_all.5 = bf16[16,1,32,128]{3,2,1,0:T(8,128)(2,1)S(1)} all-to-all(bf16[16,1,32,128]{3,2,1,0:T(8,128)(2,1)S(1)} %shard_map.125), channel_id=1, replica_groups={{0,1,2,3,4,5,6,7,8,9,10,11,12,13,14,15},{16,17,18,19,20,21,22,23,24,25,..., dimensions={0} | all-to-all | bytes 262144 | tf_op jit(solution)/shard_map/all_to_all | solution.py:394
  33.2 0.6 %rsqrt_multiply_fusion = (f32[32,128]{1,0:T(8,128)}, f32[32,128]{1,0:T(8,128)}) fusion(f32[32,128]{1,0:T(8,128)S(1)} %get-tuple-element.21, f32[32,128]{1,0:T(8,128)S(1)} %get-tuple-element.20, bf16[32,128]{1,0:T(8,128)(2,1)S(1)} %reduce_max.14), kind=kLoop, calls=%fused_computation.3 | loop fusion | flops 32768 | bytes 73728 | tf_op jit(solution)/shard_map/div | solution.py:401
  (16 shorter events, 0.1 us)
Async XLA Ops:
  0.6 7.1 %collective-permute-start.1 = (bf16[256,512]{1,0:T(8,128)(2,1)}, bf16[256,512]{1,0:T(8,128)(2,1)S(1)}, u32[]{:S(2)}, u32[]{:S(2)}) collective-permute-start(bf16[256,512]{1,0:T(8,128)(2,1)} %strip_hbm.1), channel_id=1, source_target_pairs={{0,8},{8,0},{16,24},{24,16},{1,9},{9,1},{17,25},{25,17},{2,10},{10... | collective-permute-start | bytes 786440 | tf_op jit(solution)/shard_map/ppermute | solution.py:65
  1.1 9.7 %collective-permute-start.4 = (bf16[256,512]{1,0:T(8,128)(2,1)}, bf16[256,512]{1,0:T(8,128)(2,1)S(1)}, u32[]{:S(2)}, u32[]{:S(2)}) collective-permute-start(bf16[256,512]{1,0:T(8,128)(2,1)} %strip_hbm.1), channel_id=1, source_target_pairs={{0,16},{8,24},{16,0},{24,8},{1,17},{9,25},{17,1},{25,9},{2,18},{10... | collective-permute-start | bytes 786440 | tf_op jit(solution)/shard_map/ppermute | solution.py:65
  3.7 1.4 %collective-permute-start = (s32[1]{0:T(128)}, s32[1]{0:T(128)}, u32[]{:S(2)}, u32[]{:S(2)}) collective-permute-start(s32[1]{0:T(128)} %param.14), channel_id=1, source_target_pairs={{0,8},{8,0},{16,24},{24,16},{1,9},{9,1},{17,25},{25,17},{2,10},{10... | collective-permute-start | bytes 20 | tf_op jit(solution)/shard_map/ppermute | solution.py:65
  3.9 3.8 %collective-permute-start.2 = (bf16[2,96,384]{2,1,0:T(8,128)(2,1)}, bf16[2,96,384]{2,1,0:T(8,128)(2,1)S(1)}, u32[]{:S(2)}, u32[]{:S(2)}) collective-permute-start(bf16[2,96,384]{2,1,0:T(8,128)(2,1)} %tpl_hbm.1), channel_id=1, source_target_pairs={{0,8},{8,0},{16,24},{24,16},{1,9},{9,1},{17,25},{25,17},{2,10},{10... | collective-permute-start | bytes 442376 | tf_op jit(solution)/shard_map/ppermute | solution.py:65
  5.1 0.7 %copy-start.4 = (f32[4]{0:T(128)S(1)}, f32[4]{0:T(128)}, u32[]{:S(2)}) copy-start(f32[4]{0:T(128)} %defocus_ref.1) | copy-start | bytes 52
  5.8 1.9 %copy-start = (bf16[672,640]{1,0:T(8,128)(2,1)S(1)}, bf16[672,640]{1,0:T(8,128)(2,1)}, u32[]{:S(2)}) copy-start(bf16[672,640]{1,0:T(8,128)(2,1)} %constant.31.clone.row_hbm.refs_6_) | copy-start | bytes 2580484
  5.8 1.9 %copy-start.1 = (bf16[512,512]{1,0:T(8,128)(2,1)S(1)}, bf16[512,512]{1,0:T(8,128)(2,1)}, u32[]{:S(2)}) copy-start(bf16[512,512]{1,0:T(8,128)(2,1)} %constant.30.clone.col_hbm.refs_5_.refs_4_) | copy-start | bytes 1572868
  5.8 2.0 %copy-start.2 = (bf16[256,512]{1,0:T(8,128)(2,1)S(1)}, bf16[256,512]{1,0:T(8,128)(2,1)}, u32[]{:S(2)}) copy-start(bf16[256,512]{1,0:T(8,128)(2,1)} %strip_hbm.1) | copy-start | bytes 786436
  5.8 2.0 %copy-start.3 = (bf16[2,96,384]{2,1,0:T(8,128)(2,1)S(1)}, bf16[2,96,384]{2,1,0:T(8,128)(2,1)}, u32[]{:S(2)}) copy-start(bf16[2,96,384]{2,1,0:T(8,128)(2,1)} %tpl_hbm.1) | copy-start | bytes 442372
  5.8 2.0 %copy-start.5 = (bf16[2,672,192]{2,1,0:T(8,128)(2,1)S(1)}, bf16[2,672,192]{2,1,0:T(8,128)(2,1)}, u32[]{:S(2)}) copy-start(bf16[2,672,192]{2,1,0:T(8,128)(2,1)} %constant.32.clone.deep_hbm.refs_5_) | copy-start | bytes 1548292
  10.8 1.8 %collective-permute-start.5 = (bf16[256,512]{1,0:T(8,128)(2,1)S(1)}, bf16[256,512]{1,0:T(8,128)(2,1)S(1)}, u32[]{:S(2)}, u32[]{:S(2)}) collective-permute-start(bf16[256,512]{1,0:T(8,128)(2,1)S(1)} %collective-permute-done.4.refs_0_), channel_id=1, source_target_pairs={{0,8},{8,0},{16,24},{24,16},{1,9},{9,1},{17,25},{25,17},{2,10},{10... | collective-permute-start | bytes 786440 | tf_op jit(solution)/shard_map/ppermute | solution.py:65
  10.8 6.3 %collective-permute-start.3 = (bf16[1,192,384]{2,1,0:T(8,128)(2,1)S(1)}, bf16[1,192,384]{2,1,0:T(8,128)(2,1)S(1)}, u32[]{:S(2)}, u32[]{:S(2)}) collective-permute-start(bf16[1,192,384]{2,1,0:T(8,128)(2,1)S(1)} %get-tuple-element.11), channel_id=1, source_target_pairs={{0,16},{8,24},{16,0},{24,8},{1,17},{9,25},{17,1},{25,9},{2,18},{10... | collective-permute-start | bytes 442376 | tf_op jit(solution)/shard_map/ppermute | solution.py:65
  12.6 4.5 %copy-start.6 = (bf16[256,672]{1,0:T(8,128)(2,1)S(1)}, bf16[256,672]{1,0:T(8,128)(2,1)}, u32[]{:S(2)}) copy-start(bf16[256,672]{1,0:T(8,128)(2,1)} %constant.34.clone.refs_7_) | copy-start | bytes 1032196
  12.6 4.5 %copy-start.7 = (f32[672,1]{1,0:T(8,128)S(1)}, f32[672,1]{1,0:T(8,128)}, u32[]{:S(2)}) copy-start(f32[672,1]{1,0:T(8,128)} %constant.35.clone.refs_8_) | copy-start | bytes 8068
  12.6 4.5 %copy-start.8 = (bf16[512,128]{1,0:T(8,128)(2,1)S(1)}, bf16[512,128]{1,0:T(8,128)(2,1)}, u32[]{:S(2)}) copy-start(bf16[512,128]{1,0:T(8,128)(2,1)} %constant.33.clone.refs_6_) | copy-start | bytes 393220
  12.6 4.5 %copy-start.9 = (f32[1,512]{1,0:T(1,128)S(1)}, f32[1,512]{1,0:T(1,128)}, u32[]{:S(2)}) copy-start(f32[1,512]{1,0:T(1,128)} %constant.36.clone.refs_9_) | copy-start | bytes 6148

commit v2 on v1

v2 whole, which is shorter than its diff:
```python
import functools
import math

import jax
import jax.numpy as jnp
import ml_dtypes
import numpy as np
from jax import lax
from jax.experimental import pallas as pl
from jax.experimental.pallas import tpu as pltpu
from jax.sharding import PartitionSpec as P

TS = 384
STRIP = 256
OUTC = 128
CHUNK = 16
VMEM_BYTES = 24 * 1024 * 1024


def cos_sin(freqs, places, modulus):
    residue = freqs[:, None] * places[None, :] % modulus
    lowest = np.minimum(residue, modulus - residue)
    flipped = np.where(residue > modulus - residue, -1.0, 1.0).astype(np.float32)
    angle = lowest.astype(np.float32) * np.float32(2.0 * math.pi / modulus)
    sine = np.where(2 * lowest == modulus, np.float32(0.0), flipped * np.sin(angle))
    return np.cos(angle).astype(np.float32), sine.astype(np.float32)


def round_up(value, multiple):
    return -(-value // multiple) * multiple


@functools.lru_cache(maxsize=None)
def tables(width_rows, width_cols):
    half = width_cols // 2
    rows = width_rows // 2 + 1
    padded = round_up(rows, CHUNK)
    bf16 = ml_dtypes.bfloat16
    places = np.arange(width_cols)
    cos_v, sin_v = cos_sin(np.arange(half + 1), places, width_cols)
    packed_sin = sin_v[:half].copy()
    forward_sin = -packed_sin
    forward_sin[0] = cos_v[half]
    packed_sin[0] = cos_v[half]
    col = np.concatenate([cos_v[:half], forward_sin], 0).T.astype(bf16)
    back = (2.0 * np.concatenate([cos_v[:half], packed_sin], 0)[:, :OUTC].astype(bf16).astype(np.float32)).astype(bf16)
    cos_u, sin_u = cos_sin(np.arange(rows), np.arange(width_rows), width_rows)
    row = np.zeros((2 * padded, width_rows), np.float32)
    row[:rows] = cos_u
    row[padded : padded + rows] = -sin_u
    row = row.astype(bf16)
    weight = np.ones((rows, 1), np.float32)
    weight[0] = weight[-1] = 0.5
    out = np.zeros((2 * padded, STRIP), np.float32)
    out[:rows] = cos_u[:, :STRIP].astype(bf16).astype(np.float32) * weight
    out[padded : padded + rows] = sin_u[:, :STRIP].astype(bf16).astype(np.float32) * weight
    out = np.ascontiguousarray(out.T).astype(bf16)
    row_sum = row[:, :TS].astype(np.float32).sum(1, keepdims=True)
    col_sum = col[:TS].astype(np.float32).sum(0, keepdims=True)
    return col, row, back, out, row_sum, col_sum


def swapped(value, axis, step):
    count = lax.axis_size(axis)
    return lax.ppermute(value, axis, [(source, source ^ step) for source in range(count)])


def spread_out(value, axis):
    held, step = {0: value}, lax.axis_size(axis) // 2
    while step > 1:
        held |= {index ^ step: swapped(block, axis, step) for index, block in held.items()}
        step //= 2
    return [held[index] for index in sorted(held)[1:]]


def with_partners(blocks, axis):
    return [block for held in blocks for block in (held, swapped(held, axis, 1))]


def dot(left, right):
    return jnp.dot(left, right, preferred_element_type=jnp.float32)


def first_column(shape):
    return lax.broadcasted_iota(jnp.int32, shape, 1) == 0


def quadrants(load, r, padded, half, first):
    up, down = load(slice(r, r + CHUNK)), load(slice(padded + r, padded + r + CHUNK))
    cc, cs, sc, ss = up[:, :half], up[:, half:], down[:, :half], down[:, half:]
    plus_re = cc - jnp.where(first, 0.0, ss)
    plus_im = jnp.where(first, 0.0, cs) + sc
    minus_re = jnp.where(first, cs, cc + ss)
    minus_im = jnp.where(first, ss, cs - sc)
    return plus_re, plus_im, minus_re, minus_im


def template_pair(blocks, bit, raw_ref, index):
    depth = blocks[0].shape[1]
    sums = squares = 0.0
    for j in range(2):
        block = blocks[j][index]
        wide = block.astype(jnp.float32)
        sums = sums + jnp.sum(wide, axis=0, keepdims=True)
        squares = squares + jnp.sum(wide * wide, axis=0, keepdims=True)
        start = pl.multiple_of((bit ^ j) * depth, depth)
        raw_ref[index, pl.ds(start, depth), :] = block.astype(raw_ref.dtype)
    return sums, squares


def ctf_kernel(half, width_rows, tile_ref, group_a, group_b, defocus_ref, ctf_ref):
    padded = ctf_ref.shape[2]
    u = lax.broadcasted_iota(jnp.int32, (8, round_up(padded, 128)), 1).astype(jnp.float32) / width_rows
    column = lax.broadcasted_iota(jnp.int32, (8, half), 1)
    wrapped = (lax.broadcasted_iota(jnp.int32, (8, half), 0) == 1) & (column == 0)
    v = jnp.where(wrapped, half, column).astype(jnp.float32) / (2 * half)
    for k in range(2):
        group = jnp.where((tile_ref[0] & 1) == k, group_a[0], group_b[0])
        turn = jnp.float32(math.pi) * defocus_ref[group]
        phase_u, phase_v = turn * (u * u) + 0.07, turn * (v * v)
        sin_u, cos_u = jnp.sin(phase_u).T[:padded, :1], jnp.cos(phase_u).T[:padded, :1]
        sin_v, cos_v = jnp.sin(phase_v), jnp.cos(phase_v)
        for r in range(0, padded, CHUNK):
            up = slice(r, r + CHUNK)
            for side in range(2):
                row = slice(side, side + 1)
                ctf_ref[k, side, up] = -(sin_u[up] * cos_v[row] + cos_u[up] * sin_v[row])


def template_pair(blocks, bit, raw_ref, index, mine):
    depth = blocks[0].shape[1]
    sums = squares = 0.0
    for j in range(2):
        block = blocks[j][bit * mine + index]
        wide = block.astype(jnp.float32)
        sums = sums + jnp.sum(wide, axis=0, keepdims=True)
        squares = squares + jnp.sum(wide * wide, axis=0, keepdims=True)
        start = pl.multiple_of((bit ^ j) * depth, depth)
        raw_ref[pl.ds(start, depth), :] = block.astype(raw_ref.dtype)
    return sums, squares


def early_kernel(
    tile_ref, strip_a, strip_b, tpl_a, tpl_b, col_ref, row_ref, deep_ref,
    column_ref, *outs
):
    tile = tile_ref[0]
    bit = tile & 1
    shape_ref, moment_ref, raw_ref = outs[-3:]
    for j, strip in enumerate((strip_a, strip_b)):
        start = pl.multiple_of((bit ^ j) * STRIP, STRIP)
        column_ref[pl.ds(start, STRIP), :] = dot(strip[...], col_ref[...]).astype(jnp.bfloat16)
    if len(outs) == 4:
        outs[0][0] = dot(row_ref[:, : 2 * STRIP], column_ref[...])
        outs[0][1] = dot(row_ref[:, :STRIP], column_ref[STRIP:, :])
    else:
        stage_kernel(0, tile_ref, column_ref, row_ref, *outs[:2])
    mine = shape_ref.shape[0]
    for index in range(mine):
        for k, moment in enumerate(template_pair((tpl_a, tpl_b), bit, raw_ref, index, mine)):
            moment_ref[2 * index + k : 2 * index + k + 1, :] = moment
        columns = dot(raw_ref[...].astype(jnp.bfloat16), col_ref[:TS, :]).astype(jnp.bfloat16)
        shape_ref[index] = dot(deep_ref[tile >> 1], columns)


def rows_of(pair, offset, length):
    return pl.ds(pl.multiple_of(pair * (2 * STRIP), 2 * STRIP) + offset, length)


def add_power(power_ref, loads, half, first, fresh):
    padded = power_ref.shape[1]
    for r in range(0, padded, CHUNK):
        up = slice(r, r + CHUNK)
        plus = 0.0 if fresh else power_ref[0, up]
        minus = 0.0 if fresh else power_ref[1, up]
        for load in loads:
            signs = quadrants(load, r, padded, half, first)
            plus = plus + (signs[0] * signs[0] + signs[1] * signs[1])
            minus = minus + (signs[2] * signs[2] + signs[3] * signs[3])
        power_ref[0, up] = plus
        power_ref[1, up] = minus


def other_kernel(count, tile_ref, *refs):
    others = refs[: count - 2]
    column_ref, col_ref, row_ref, part_ref, power_ref, work_ref = refs[count - 2 :]
    half, width_rows = col_ref.shape[1] // 2, row_ref.shape[1]
    tile = tile_ref[0]
    own, pairs = tile >> 1, count // 2
    first = first_column((CHUNK, half))
    for j in range(2, count):
        start = pl.multiple_of((tile ^ j) * STRIP, STRIP)
        part_ref[pl.ds(start, STRIP), :] = dot(others[j - 2][...], col_ref[...]).astype(jnp.bfloat16)
    part_ref[rows_of(own, 0, 2 * STRIP), :] = column_ref[...]
    for j in range(1, pairs):
        pair = own ^ j

        @pl.when(pair + 1 < pairs)
        def _():
            work_ref[0] = dot(row_ref[...], part_ref[rows_of(pair, 0, width_rows), :])
            work_ref[1] = dot(row_ref[...], part_ref[rows_of(pair, STRIP, width_rows), :])

        @pl.when(pair + 1 == pairs)
        def _():
            work_ref[0] = dot(row_ref[:, : 2 * STRIP], part_ref[rows_of(pair, 0, 2 * STRIP), :])
            work_ref[1] = dot(row_ref[:, :STRIP], part_ref[rows_of(pair, STRIP, STRIP), :])

        add_power(power_ref, [lambda s, k=k: work_ref[k, s] for k in range(2)], half, first, j == 1)
    if pairs == 1:
        power_ref[...] = jnp.zeros(power_ref.shape, jnp.float32)


def own_kernel(count, tile_ref, part_ref, partial_ref, others_ref, ctf_ref, row_ref, weighted_ref, cross_ref, power_ref):
    padded, half = power_ref.shape[1:]
    width_rows, width_cols = row_ref.shape[1], 2 * half
    own, pairs = tile_ref[0] >> 1, count // 2
    first = first_column((CHUNK, half))

    def finish(loads):
        total = jnp.zeros((CHUNK, half), jnp.float32)
        for r in range(0, padded, CHUNK):
            up = slice(r, r + CHUNK)
            plus, minus = others_ref[0, up], others_ref[1, up]
            for load in loads:
                signs = quadrants(load, r, padded, half, first)
                plus = plus + (signs[0] * signs[0] + signs[1] * signs[1])
                minus = minus + (signs[2] * signs[2] + signs[3] * signs[3])
            power_ref[0, up] = plus
            power_ref[1, up] = minus
            total = total + (plus + minus)
        last = width_rows // 2
        ends = [power_ref[0, r : r + 1] + power_ref[1, r : r + 1] for r in (0, last)]
        whole = 2.0 * jnp.sum(total, keepdims=True) - jnp.sum(ends[0] + ends[1], keepdims=True)
        mean = whole / (count * width_rows * width_cols)
        for r in range(0, padded, CHUNK):
            up = slice(r, r + CHUNK)
            gains = [lax.rsqrt(power_ref[k, up] * (1.0 / count) + mean) for k in range(2)]
            for k, load in enumerate(loads):
                signs = quadrants(load, r, padded, half, first)
                for side in range(2):
                    gain = gains[side] * ctf_ref[k, side, up]
                    weighted_ref[k, 2 * side, up] = signs[2 * side] * gain
                    weighted_ref[k, 2 * side + 1, up] = signs[2 * side + 1] * gain

    @pl.when(own + 1 < pairs)
    def _():
        cross_ref[0] = dot(row_ref[:, 2 * STRIP :], part_ref[rows_of(own + 1, 0, width_rows - 2 * STRIP), :])
        cross_ref[1] = dot(row_ref[:, STRIP:], part_ref[rows_of(own + 1, 0, width_rows - STRIP), :])
        finish([lambda s, k=k: partial_ref[k, s] + cross_ref[k, s] for k in range(2)])

    @pl.when(own + 1 == pairs)
    def _():
        finish([lambda s, k=k: partial_ref[k, s] for k in range(2)])


def span(strip, blocks):
    start = max(strip, blocks[0])
    stop = min((strip + 1) * STRIP + TS, (blocks[-1] + 1) * STRIP)
    return slice(start * STRIP - strip * STRIP, stop - strip * STRIP), slice(
        (start - blocks[0]) * STRIP, stop - blocks[0] * STRIP
    )


def reached(blocks):
    return [s for s in range(4) if s <= blocks[-1] and (s + 1) * STRIP + TS > blocks[0] * STRIP]


def sources(tile):
    sets = [[tile & 2, tile & 2 | 1], [tile ^ 2], [tile ^ 3]]
    strips = [reached(blocks) for blocks in sets]
    return sets, strips, [[k for k in range(3) if s in strips[k]] for s in range(4)]


def summed(refs, strip, which):
    def load(rows):
        parts = [refs[k][strip, rows] for k in which]
        return functools.reduce(lambda left, right: left + right, parts)

    return load


def gather_power(source_ref, power_ref, loads, half, first):
    for r in range(0, power_ref.shape[1], CHUNK):
        up = slice(r, r + CHUNK)
        plus, minus = (0.0, 0.0) if source_ref is None else (source_ref[0, up], source_ref[1, up])
        for load in loads:
            signs = quadrants(load, r, power_ref.shape[1], half, first)
            plus = plus + (signs[0] * signs[0] + signs[1] * signs[1])
            minus = minus + (signs[2] * signs[2] + signs[3] * signs[3])
        if not loads and source_ref is None:
            plus = minus = jnp.zeros((CHUNK, half), jnp.float32)
        power_ref[0, up] = plus
        power_ref[1, up] = minus


def stage_kernel(stage, tile_ref, *refs):
    earlier, refs = refs[:stage], refs[stage:]
    previous, refs = (refs[0], refs[1:]) if stage else (None, refs)
    if stage:
        low_ref, high_ref, row_ref, quad_ref, power_ref, block_ref = refs
        block_ref[: low_ref.shape[0], :] = low_ref[...]
        block_ref[low_ref.shape[0] :, :] = high_ref[...]
    else:
        block_ref, row_ref, quad_ref, power_ref = refs
    half = quad_ref.shape[2] // 2
    first = first_column((CHUNK, half))
    quads = [*earlier, quad_ref]
    for case in range(4):

        @pl.when(tile_ref[0] == case)
        def _():
            sets, strips, needs = sources(case)
            for s in strips[stage]:
                columns, rows = span(s, sets[stage])
                quad_ref[s] = dot(row_ref[:, columns], block_ref[rows, :])
            done = [s for s in range(4) if max(needs[s]) == stage]
            gather_power(previous, power_ref, [summed(quads, s, needs[s]) for s in done], half, first)


def column_kernel(strip_ref, col_ref, *halves):
    size = halves[0].shape[0]
    for k, half_ref in enumerate(halves):
        half_ref[...] = dot(strip_ref[k * size : (k + 1) * size, :], col_ref[...]).astype(jnp.bfloat16)


def whiten_kernel(tile_ref, first_ref, second_ref, third_ref, power_ref, ctf_ref, weighted_ref):
    padded, half = power_ref.shape[1:]
    width_rows, width_cols = STRIP + TS, 2 * half
    first = first_column((CHUNK, half))
    total = jnp.zeros((CHUNK, half), jnp.float32)
    for r in range(0, padded, CHUNK):
        total = total + (power_ref[0, r : r + CHUNK] + power_ref[1, r : r + CHUNK])
    last = width_rows // 2
    ends = [power_ref[0, r : r + 1] + power_ref[1, r : r + 1] for r in (0, last)]
    whole = 2.0 * jnp.sum(total, keepdims=True) - jnp.sum(ends[0] + ends[1], keepdims=True)
    mean = whole / (4 * width_rows * width_cols)
    for case in range(4):

        @pl.when(tile_ref[0] == case)
        def _():
            needs = sources(case)[2]
            loads = [summed((first_ref, second_ref, third_ref), s, needs[s]) for s in (case & 2, case & 2 | 1)]
            for r in range(0, padded, CHUNK):
                up = slice(r, r + CHUNK)
                gains = [lax.rsqrt(power_ref[k, up] * 0.25 + mean) for k in range(2)]
                for k, load in enumerate(loads):
                    signs = quadrants(load, r, padded, half, first)
                    for side in range(2):
                        gain = gains[side] * ctf_ref[k, side, up]
                        weighted_ref[k, 2 * side, up] = signs[2 * side] * gain
                        weighted_ref[k, 2 * side + 1, up] = signs[2 * side + 1] * gain


def score_kernel(count, tile_ref, *refs):
    others = refs[: count - 2]
    (weighted_ref, shape_ref, moment_ref, col_ref, deep_ref, back_ref, out_ref, row_sum_ref, col_sum_ref) = refs[
        count - 2 : count + 7
    ]
    score_ref, raw_ref, quad_ref, product_ref = refs[count + 7 :]
    padded, half = deep_ref.shape[1] // 2, col_ref.shape[1] // 2
    scale = 1.0 / ((STRIP + TS) * col_ref.shape[0])
    first = first_column((CHUNK, half))
    pieces, mine = score_ref.shape[:2]
    tile = tile_ref[0]
    pairs = count // 2
    for index in range(mine):
        sums, squares = (moment_ref[2 * index + k : 2 * index + k + 1, :] for k in range(2))
        for j in range(1, pairs):
            more = template_pair(others[2 * j - 2 : 2 * j], tile & 1, raw_ref, index, mine)
            sums, squares = sums + more[0], squares + more[1]
            columns = dot(raw_ref[...].astype(jnp.bfloat16), col_ref[:TS, :]).astype(jnp.bfloat16)
            late = dot(deep_ref[(tile >> 1) ^ j], columns)
            quad_ref[...] = late if j == 1 else quad_ref[...] + late
        mean = jnp.sum(sums, keepdims=True) / (TS * TS)
        spread = jnp.sqrt(jnp.sum(squares, keepdims=True) / (TS * TS) - mean * mean + 1e-05)
        col_sum = mean * col_sum_ref[...]

        def load(s):
            known = shape_ref[index, s] + quad_ref[s] if pairs > 1 else shape_ref[index, s]
            return known - row_sum_ref[s, :] * col_sum

        for r in range(0, padded, CHUNK):
            up, down = slice(r, r + CHUNK), slice(padded + r, padded + r + CHUNK)
            a, b, c, d = quadrants(load, r, padded, half, first)
            for k in range(2):
                p, q, s, t = (weighted_ref[k, m, up] for m in range(4))
                plus_re = p * a + q * b
                plus_im = q * a - p * b
                minus_re = s * c + t * d
                minus_im = t * c - s * d
                product_ref[k, up, :half] = (plus_re + jnp.where(first, 0.0, minus_re)).astype(jnp.bfloat16)
                product_ref[k, up, half:] = jnp.where(first, minus_re, -(plus_im + minus_im)).astype(jnp.bfloat16)
                product_ref[k, down, :half] = (jnp.where(first, 0.0, minus_im) - plus_im).astype(jnp.bfloat16)
                product_ref[k, down, half:] = jnp.where(first, -minus_im, minus_re - plus_re).astype(jnp.bfloat16)
        for k in range(2):
            back = dot(product_ref[k], back_ref[...]).astype(jnp.bfloat16)
            score = (dot(out_ref[...], back) * (scale / spread)).reshape(pieces // 2, 2 * STRIP // pieces, OUTC)
            score_ref[k * (pieces // 2) : (k + 1) * (pieces // 2), index] = score.astype(jnp.bfloat16)


def on_device(kernel, scalars, operands, scratch, result, cost):
    vmem, smem = pl.BlockSpec(memory_space=pltpu.VMEM), pl.BlockSpec(memory_space=pltpu.SMEM)
    return pl.pallas_call(
        kernel,
        out_shape=result,
        in_specs=[smem] * len(scalars) + [vmem] * len(operands),
        out_specs=jax.tree.map(lambda _: vmem, result),
        scratch_shapes=scratch,
        compiler_params=pltpu.CompilerParams(vmem_limit_bytes=VMEM_BYTES),
        cost_estimate=None if cost is None else pl.CostEstimate(flops=cost, bytes_accessed=0, transcendentals=0),
    )(*scalars, *operands)


def local(micrograph, templates, defocus, group_of_tile):
    width_cols = micrograph.shape[1]
    width_rows = STRIP + TS
    tpl_count, depth = templates.shape[:2]
    count = lax.axis_size("tile")
    orient_count = lax.axis_size("orient")
    col, row, back, out, row_sum, col_sum = tables(width_rows, width_cols)
    deep = np.stack(np.split(row[:, :TS], count // 2, axis=1))
    padded, half = row.shape[0] // 2, width_cols // 2
    tile = lax.axis_index("tile").astype(jnp.int32).reshape(1)
    plane, quads = (padded, half), (2 * padded, width_cols)
    f32, bf16 = jnp.float32, jnp.bfloat16
    mine = tpl_count // 2
    raw = pltpu.VMEM((2 * depth, TS), bf16 if depth % 16 == 0 else f32)
    pass_flops = 2 * quads[0] * quads[1] * STRIP

    strips = spread_out(micrograph, "tile")
    pieces = spread_out(templates, "tile")
    ctf = on_device(
        functools.partial(ctf_kernel, half, width_rows),
        [tile, group_of_tile, swapped(group_of_tile, "tile", 1), defocus],
        [],
        [],
        jax.ShapeDtypeStruct((2, 2, *plane), f32),
        12 * pass_flops,
    )
    early_in = [micrograph, swapped(micrograph, "tile", 1), templates, swapped(templates, "tile", 1), col, row, deep]
    early_out = [
        jax.ShapeDtypeStruct((mine, *quads), f32),
        jax.ShapeDtypeStruct((round_up(2 * mine, 8), TS), f32),
    ]
    columns_out = jax.ShapeDtypeStruct((2 * STRIP, width_cols), bf16)
    all_quads, power_out = jax.ShapeDtypeStruct((4, *quads), f32), jax.ShapeDtypeStruct((2, *plane), f32)
    weighted_out = jax.ShapeDtypeStruct((2, 4, *plane), f32)
    if count == 4:
        column, quads_0, power, shape, moment = on_device(
            early_kernel, [tile], early_in, [raw], (columns_out, all_quads, power_out, *early_out), None
        )
        strips, power, ctf = lax.optimization_barrier((strips, power, ctf))
        half_out = jax.ShapeDtypeStruct((STRIP // 2, width_cols), bf16)
        block = pltpu.VMEM((STRIP, width_cols), bf16)
        halves = on_device(column_kernel, [], [strips[0], col], [], (half_out, half_out), None)
        received = [swapped(part, "tile", 1) for part in halves]
        quads_1, power = on_device(
            functools.partial(stage_kernel, 1), [tile], [quads_0, power, *halves, row], [block], (all_quads, power_out), None
        )
        quads_2, power = on_device(
            functools.partial(stage_kernel, 2),
            [tile],
            [quads_0, quads_1, power, *received, row],
            [block],
            (all_quads, power_out),
            None,
        )
        pieces, power = lax.optimization_barrier((pieces, power))
        pieces = with_partners(pieces, "tile")
        weighted = on_device(
            whiten_kernel, [tile], [quads_0, quads_1, quads_2, power, ctf], [], weighted_out, None
        )
    else:
        column, partial, shape, moment = on_device(
            early_kernel,
            [tile],
            early_in,
            [raw],
            (columns_out, jax.ShapeDtypeStruct((2, *quads), f32), *early_out),
            None,
        )
        strips, column, ctf = lax.optimization_barrier((strips, column, ctf))
        part, power = on_device(
            functools.partial(other_kernel, count),
            [tile],
            [*with_partners(strips, "tile"), column, col, row],
            [pltpu.VMEM((2, *quads), f32)],
            (jax.ShapeDtypeStruct((count * STRIP, width_cols), bf16), power_out),
            None,
        )
        pieces, power = lax.optimization_barrier((pieces, power))
        pieces = with_partners(pieces, "tile")
        weighted = on_device(
            functools.partial(own_kernel, count),
            [tile],
            [part, partial, power, ctf, row],
            [pltpu.VMEM((2, *quads), f32), pltpu.VMEM((2, *plane), f32)],
            weighted_out,
            None,
        )
    scores = on_device(
        functools.partial(score_kernel, count),
        [tile],
        [*pieces, weighted, shape, moment, col, deep, back, out, row_sum, col_sum],
        [raw, pltpu.VMEM(quads, f32), pltpu.VMEM((2, *quads), bf16)],
        jax.ShapeDtypeStruct((2 * orient_count, mine, STRIP // orient_count, OUTC), bf16),
        None,
    )
    chips = [[first + k for k in range(2 * orient_count)] for first in range(0, count * orient_count, 2 * orient_count)]
    received = lax.all_to_all(
        scores, ("tile", "orient"), split_axis=0, concat_axis=0, tiled=True, axis_index_groups=chips
    ).astype(f32)
    orient_total = tpl_count * orient_count
    best = jnp.max(received, axis=(0, 1))
    score_mean = jnp.sum(received, axis=(0, 1)) / orient_total
    score_var = jnp.sum(received * received, axis=(0, 1)) / orient_total - score_mean * score_mean
    return (best, (best - score_mean) / jnp.sqrt(score_var + 1e-05))


def solution(mesh):
    placed = (P("tile", None), P("orient", "tile", None), P(), P("tile"))
    return jax.shard_map(
        local,
        mesh=mesh,
        in_specs=placed,
        out_specs=(P(("tile", "orient"), None), P(("tile", "orient"), None)),
        check_vma=False,
    )
```

time: 34 us -> 32.9 us (0.968)
  waiting for transfers between devices: 2.29 us -> 1.4 us
  starting transfers between devices: 5.35 us -> 4.68 us
    ppermute x6 -> x8, waiting for transfers between devices: 2.29 us -> 1.4 us  [swapped(): lax.ppermute(value, axis, [(source, source ^ step) for source in range(co...]
    ppermute x6 -> x8, starting transfers between devices: 5.35 us -> 4.68 us  [swapped(): lax.ppermute(value, axis, [(source, source ^ step) for source in range(co...]
    pallas_call x4 -> x7, Pallas kernels: 9.73 us -> 9.74 us  [on_device(): pl.pallas_call(kernel, out_shape=result, in_specs=[smem] * len(scalars) +...]
  transfers between devices with their start and end apart: 6 -> 8, of which waited for: 3 -> 4; matrix products, arithmetic and copies ran while one was open for 0% -> 0% of each run, Pallas kernels for 22% -> 23%
where the time goes in v2:
time: 32.9 us; the launch traced here: 32.6 us
  blocking collectives  13.9 us (42%)
  Pallas kernels  9.74 us (30%)
  starting transfers between devices  4.68 us (14%)
  between operations  1.47 us (4%)
  waiting for transfers between devices  1.4 us (4%)
  local copies, waits for them, and re-layouts  0.8 us (2%)
  other arithmetic  0.69 us (2%)
    all_to_all x1, blocking collectives, local(): lax.all_to_all(scores, ('tile', 'orient'), split_axis=0, concat_axis=0, t...  13.9 us
    pallas_call x7, Pallas kernels, on_device(): pl.pallas_call(kernel, out_shape=result, in_specs=[smem] * len(scalars) +...  9.74 us
    ppermute x8, starting transfers between devices, swapped(): lax.ppermute(value, axis, [(source, source ^ step) for source in range(co...  4.68 us
    ppermute x8, waiting for transfers between devices, swapped(): lax.ppermute(value, axis, [(source, source ^ step) for source in range(co...  1.4 us
    unnamed x20, local copies, waits for them, and re-layouts  0.8 us
  transfers between devices with their start and end apart: 8, of which 4 were waited for; matrix products, arithmetic and copies ran while one was open for 0% of the time, Pallas kernels for 23%

profile of v2, /device:TPU:0, one launch (start us, length us, event | category | flops | bytes accessed | tf_op | source)
XLA Modules:
  0.0 32.6 jit_solution(6952070184957248126)
XLA Ops:
  0.7 0.5 %collective-permute-start.1 = (bf16[256,512]{1,0:T(8,128)(2,1)}, bf16[256,512]{1,0:T(8,128)(2,1)S(1)}, u32[]{:S(2)}, u32[]{:S(2)}) collective-permute-start(bf16[256,512]{1,0:T(8,128)(2,1)} %strip_a.1), channel_id=1, source_target_pairs={{0,8},{8,0},{16,24},{24,16},{1,9},{9,1},{17,25},{25,17},{2,10},{10... | collective-permute-start | bytes 786440 | tf_op jit(solution)/shard_map/ppermute | solution.py:65
  1.2 2.6 %collective-permute-start.3 = (bf16[256,512]{1,0:T(8,128)(2,1)}, bf16[256,512]{1,0:T(8,128)(2,1)S(1)}, u32[]{:S(2)}, u32[]{:S(2)}) collective-permute-start(bf16[256,512]{1,0:T(8,128)(2,1)} %strip_a.1), channel_id=1, source_target_pairs={{0,16},{8,24},{16,0},{24,8},{1,17},{9,25},{17,1},{25,9},{2,18},{10... | collective-permute-start | bytes 786440 | tf_op jit(solution)/shard_map/ppermute | solution.py:65
  3.8 0.1 collective-permute-start
  3.9 0.1 collective-permute-start.2
  4.0 0.4 %collective-permute-start.4 = (s32[1]{0:T(128)}, s32[1]{0:T(128)}, u32[]{:S(2)}, u32[]{:S(2)}) collective-permute-start(s32[1]{0:T(128)} %param.14), channel_id=1, source_target_pairs={{0,8},{8,0},{16,24},{24,16},{1,9},{9,1},{17,25},{25,17},{2,10},{10... | collective-permute-start | bytes 20 | tf_op jit(solution)/shard_map/ppermute | solution.py:65
  5.0 0.3 collective-permute-done.4.group_b
  5.3 0.7 %copy-done.9 = f32[4]{0:T(128)S(1)} copy-done((f32[4]{0:T(128)S(1)}, f32[4]{0:T(128)}, u32[]{:S(2)}) %copy-start.9) | copy-done | bytes 40
  6.0 1.7 %shard_map.123.ctf_ref = f32[2,2,336,256]{3,2,1,0:T(8,128)S(1)} custom-call(s32[1]{0:T(128)} %bitcast.tile_ref, s32[1]{0:T(128)S(6)} %copy.13.group_a, s32[1]{0:T(128)} %collective-permute-done.4.group_b, f32[4]{0:T(128)S(1)} %copy-done.9), custom_call_target="tpu_custom_call" | custom-call | flops 2113929216 | tf_op jit(solution)/shard_map/pallas_call | solution.py:403
  7.8 2.5 %shard_map.122 = (bf16[512,512]{1,0:T(8,128)(2,1)}, f32[4,672,512]{2,1,0:T(8,128)S(1)}, f32[2,336,256]{2,1,0:T(8,128)S(1)}, f32[1,672,512]{2,1,0:T(8,128)S(1)}, f32[8,384]{1,0:T(8,128)S(1)}) custom-call(s32[1]{0:T(128)} %bitcast.tile_ref, bf16[256,512]{1,0:T(8,128)(2,1)S(1)} %copy-done.5, bf16[256,512]{1,0:T(8,128)(2,1)S(1)} %collective-permute-done.1.strip_b, ...), custom_call_target="tpu_custom_call" | custom-call | tf_op jit(solution)/shard_map/pallas_call | solution.py:403
  10.2 0.9 %collective-permute-done.3.strip_ref = bf16[256,512]{1,0:T(8,128)(2,1)S(1)} collective-permute-done((bf16[256,512]{1,0:T(8,128)(2,1)}, bf16[256,512]{1,0:T(8,128)(2,1)S(1)}, u32[]{:S(2)}, u32[]{:S(2)}) %collective-permute-start.3) | collective-permute-done | bytes 262176 | tf_op jit(solution)/shard_map/ppermute | solution.py:65
  11.1 0.3 shard_map.124
  11.5 0.1 collective-permute-start.5
  11.5 0.5 %collective-permute-start.6 = (bf16[128,512]{1,0:T(8,128)(2,1)S(1)}, bf16[128,512]{1,0:T(8,128)(2,1)S(1)}, u32[]{:S(2)}, u32[]{:S(2)}) collective-permute-start(bf16[128,512]{1,0:T(8,128)(2,1)S(1)} %get-tuple-element.22.refs_3_), channel_id=1, source_target_pairs={{0,8},{8,0},{16,24},{24,16},{1,9},{9,1},{17,25},{25,17},{2,10},{10... | collective-permute-start | bytes 393224 | tf_op jit(solution)/shard_map/ppermute | solution.py:65
  12.0 0.9 %shard_map.125 = (f32[4,672,512]{2,1,0:T(8,128)S(1)}, f32[2,336,256]{2,1,0:T(8,128)S(1)}) custom-call(s32[1]{0:T(128)} %bitcast.tile_ref, f32[4,672,512]{2,1,0:T(8,128)S(1)} %get-tuple-element.17.refs_0_.first_ref, f32[2,336,256]{2,1,0:T(8,128)S(1)} %get-tuple-element.19.refs_1_, bf16[128,512]{1,0:T(8,128)(2,1)S(1)} %get-tuple-element.21.refs_2_, ...), custom_call_target="tpu_custom_call" | custom-call | tf_op jit(solution)/shard_map/pallas_call | solution.py:403
  12.9 0.1 collective-permute-done.6.refs_4_
  13.1 1.2 %shard_map.126 = (f32[4,672,512]{2,1,0:T(8,128)S(1)}, f32[2,336,256]{2,1,0:T(8,128)S(1)}) custom-call(s32[1]{0:T(128)} %bitcast.tile_ref, f32[4,672,512]{2,1,0:T(8,128)S(1)} %get-tuple-element.17.refs_0_.first_ref, f32[4,672,512]{2,1,0:T(8,128)S(1)} %get-tuple-element.23.refs_1_.second_ref, f32[2,336,256]{2,1,0:T(8,128)S(1)} %get-tuple-element.24.refs_2_, ...), custom_call_target="tpu_custom_call" | custom-call | tf_op jit(solution)/shard_map/pallas_call | solution.py:403
  14.3 0.4 %collective-permute-start.7 = (bf16[2,96,384]{2,1,0:T(8,128)(2,1)S(1)}, bf16[2,96,384]{2,1,0:T(8,128)(2,1)S(1)}, u32[]{:S(2)}, u32[]{:S(2)}) collective-permute-start(bf16[2,96,384]{2,1,0:T(8,128)(2,1)S(1)} %collective-permute-done.refs_0_), channel_id=1, source_target_pairs={{0,8},{8,0},{16,24},{24,16},{1,9},{9,1},{17,25},{25,17},{2,10},{10... | collective-permute-start | bytes 442376 | tf_op jit(solution)/shard_map/ppermute | solution.py:65
  14.7 0.9 %shard_map.127.refs_2_ = f32[2,4,336,256]{3,2,1,0:T(8,128)S(1)} custom-call(s32[1]{0:T(128)} %bitcast.tile_ref, f32[4,672,512]{2,1,0:T(8,128)S(1)} %get-tuple-element.17.refs_0_.first_ref, f32[4,672,512]{2,1,0:T(8,128)S(1)} %get-tuple-element.23.refs_1_.second_ref, f32[4,672,512]{2,1,0:T(8,128)S(1)} %get-tuple-element.27.third_ref, ...), custom_call_target="tpu_custom_call" | custom-call | tf_op jit(solution)/shard_map/pallas_call | solution.py:403
  15.7 0.1 collective-permute-done.7.refs_1_
  15.7 0.1 copy-done.4
  15.8 0.0 copy-done.7
  15.8 2.2 %shard_map.128 = bf16[16,1,32,128]{3,2,1,0:T(8,128)(2,1)S(1)} custom-call(s32[1]{0:T(128)} %bitcast.tile_ref, bf16[2,96,384]{2,1,0:T(8,128)(2,1)S(1)} %collective-permute-done.refs_0_, bf16[2,96,384]{2,1,0:T(8,128)(2,1)S(1)} %collective-permute-done.7.refs_1_, f32[2,4,336,256]{3,2,1,0:T(8,128)S(1)} %shard_map.127.refs_2_, ...), custom_call_target="tpu_custom_call" | custom-call | tf_op jit(solution)/shard_map/pallas_call | solution.py:403
  18.1 13.9 %all_to_all.5 = bf16[16,1,32,128]{3,2,1,0:T(8,128)(2,1)S(1)} all-to-all(bf16[16,1,32,128]{3,2,1,0:T(8,128)(2,1)S(1)} %shard_map.128), channel_id=1, replica_groups={{0,1,2,3,4,5,6,7,8,9,10,11,12,13,14,15},{16,17,18,19,20,21,22,23,24,25,..., dimensions={0} | all-to-all | bytes 262144 | tf_op jit(solution)/shard_map/all_to_all | solution.py:510
  32.0 0.6 %rsqrt_multiply_fusion = (f32[32,128]{1,0:T(8,128)}, f32[32,128]{1,0:T(8,128)}) fusion(f32[32,128]{1,0:T(8,128)S(1)} %get-tuple-element.33, f32[32,128]{1,0:T(8,128)S(1)} %get-tuple-element.32, bf16[32,128]{1,0:T(8,128)(2,1)S(1)} %reduce_max.14), kind=kLoop, calls=%fused_computation.3 | loop fusion | flops 32768 | bytes 73728 | tf_op jit(solution)/shard_map/div | solution.py:517
  (23 shorter events, 0.1 us)
Async XLA Ops:
  0.6 7.1 %copy-start = (bf16[672,640]{1,0:T(8,128)(2,1)S(1)}, bf16[672,640]{1,0:T(8,128)(2,1)}, u32[]{:S(2)}) copy-start(bf16[672,640]{1,0:T(8,128)(2,1)} %constant.31.clone.row_ref.refs_4_.refs_5_) | copy-start | bytes 2580484
  0.6 7.1 %copy-start.1 = (bf16[512,512]{1,0:T(8,128)(2,1)S(1)}, bf16[512,512]{1,0:T(8,128)(2,1)}, u32[]{:S(2)}) copy-start(bf16[512,512]{1,0:T(8,128)(2,1)} %constant.30.clone.col_ref.refs_5_) | copy-start | bytes 1572868
  0.7 7.1 %copy-start.2 = (bf16[2,672,192]{2,1,0:T(8,128)(2,1)S(1)}, bf16[2,672,192]{2,1,0:T(8,128)(2,1)}, u32[]{:S(2)}) copy-start(bf16[2,672,192]{2,1,0:T(8,128)(2,1)} %constant.32.clone.deep_ref.refs_6_) | copy-start | bytes 1548292
  0.7 7.1 %copy-start.5 = (bf16[256,512]{1,0:T(8,128)(2,1)S(1)}, bf16[256,512]{1,0:T(8,128)(2,1)}, u32[]{:S(2)}) copy-start(bf16[256,512]{1,0:T(8,128)(2,1)} %strip_a.1) | copy-start | bytes 786436
  0.7 7.1 %copy-start.6 = (bf16[2,96,384]{2,1,0:T(8,128)(2,1)S(1)}, bf16[2,96,384]{2,1,0:T(8,128)(2,1)}, u32[]{:S(2)}) copy-start(bf16[2,96,384]{2,1,0:T(8,128)(2,1)} %tpl_a.1) | copy-start | bytes 442372
  0.7 7.0 %collective-permute-start.1 = (bf16[256,512]{1,0:T(8,128)(2,1)}, bf16[256,512]{1,0:T(8,128)(2,1)S(1)}, u32[]{:S(2)}, u32[]{:S(2)}) collective-permute-start(bf16[256,512]{1,0:T(8,128)(2,1)} %strip_a.1), channel_id=1, source_target_pairs={{0,8},{8,0},{16,24},{24,16},{1,9},{9,1},{17,25},{25,17},{2,10},{10... | collective-permute-start | bytes 786440 | tf_op jit(solution)/shard_map/ppermute | solution.py:65
  1.2 9.9 %collective-permute-start.3 = (bf16[256,512]{1,0:T(8,128)(2,1)}, bf16[256,512]{1,0:T(8,128)(2,1)S(1)}, u32[]{:S(2)}, u32[]{:S(2)}) collective-permute-start(bf16[256,512]{1,0:T(8,128)(2,1)} %strip_a.1), channel_id=1, source_target_pairs={{0,16},{8,24},{16,0},{24,8},{1,17},{9,25},{17,1},{25,9},{2,18},{10... | collective-permute-start | bytes 786440 | tf_op jit(solution)/shard_map/ppermute | solution.py:65
  3.8 10.5 %collective-permute-start = (bf16[2,96,384]{2,1,0:T(8,128)(2,1)}, bf16[2,96,384]{2,1,0:T(8,128)(2,1)S(1)}, u32[]{:S(2)}, u32[]{:S(2)}) collective-permute-start(bf16[2,96,384]{2,1,0:T(8,128)(2,1)} %tpl_a.1), channel_id=1, source_target_pairs={{0,16},{8,24},{16,0},{24,8},{1,17},{9,25},{17,1},{25,9},{2,18},{10... | collective-permute-start | bytes 442376 | tf_op jit(solution)/shard_map/ppermute | solution.py:65
  3.9 3.9 %collective-permute-start.2 = (bf16[2,96,384]{2,1,0:T(8,128)(2,1)}, bf16[2,96,384]{2,1,0:T(8,128)(2,1)S(1)}, u32[]{:S(2)}, u32[]{:S(2)}) collective-permute-start(bf16[2,96,384]{2,1,0:T(8,128)(2,1)} %tpl_a.1), channel_id=1, source_target_pairs={{0,8},{8,0},{16,24},{24,16},{1,9},{9,1},{17,25},{25,17},{2,10},{10... | collective-permute-start | bytes 442376 | tf_op jit(solution)/shard_map/ppermute | solution.py:65
  4.0 1.4 %collective-permute-start.4 = (s32[1]{0:T(128)}, s32[1]{0:T(128)}, u32[]{:S(2)}, u32[]{:S(2)}) collective-permute-start(s32[1]{0:T(128)} %param.14), channel_id=1, source_target_pairs={{0,8},{8,0},{16,24},{24,16},{1,9},{9,1},{17,25},{25,17},{2,10},{10... | collective-permute-start | bytes 20 | tf_op jit(solution)/shard_map/ppermute | solution.py:65
  5.3 0.7 %copy-start.9 = (f32[4]{0:T(128)S(1)}, f32[4]{0:T(128)}, u32[]{:S(2)}) copy-start(f32[4]{0:T(128)} %defocus_ref.1) | copy-start | bytes 52
  11.5 1.5 %collective-permute-start.5 = (bf16[128,512]{1,0:T(8,128)(2,1)S(1)}, bf16[128,512]{1,0:T(8,128)(2,1)S(1)}, u32[]{:S(2)}, u32[]{:S(2)}) collective-permute-start(bf16[128,512]{1,0:T(8,128)(2,1)S(1)} %get-tuple-element.21.refs_2_), channel_id=1, source_target_pairs={{0,8},{8,0},{16,24},{24,16},{1,9},{9,1},{17,25},{25,17},{2,10},{10... | collective-permute-start | bytes 393224 | tf_op jit(solution)/shard_map/ppermute | solution.py:65
  11.5 1.5 %collective-permute-start.6 = (bf16[128,512]{1,0:T(8,128)(2,1)S(1)}, bf16[128,512]{1,0:T(8,128)(2,1)S(1)}, u32[]{:S(2)}, u32[]{:S(2)}) collective-permute-start(bf16[128,512]{1,0:T(8,128)(2,1)S(1)} %get-tuple-element.22.refs_3_), channel_id=1, source_target_pairs={{0,8},{8,0},{16,24},{24,16},{1,9},{9,1},{17,25},{25,17},{2,10},{10... | collective-permute-start | bytes 393224 | tf_op jit(solution)/shard_map/ppermute | solution.py:65
  14.3 1.4 %collective-permute-start.7 = (bf16[2,96,384]{2,1,0:T(8,128)(2,1)S(1)}, bf16[2,96,384]{2,1,0:T(8,128)(2,1)S(1)}, u32[]{:S(2)}, u32[]{:S(2)}) collective-permute-start(bf16[2,96,384]{2,1,0:T(8,128)(2,1)S(1)} %collective-permute-done.refs_0_), channel_id=1, source_target_pairs={{0,8},{8,0},{16,24},{24,16},{1,9},{9,1},{17,25},{25,17},{2,10},{10... | collective-permute-start | bytes 442376 | tf_op jit(solution)/shard_map/ppermute | solution.py:65
  14.7 1.0 %copy-start.3 = (bf16[256,672]{1,0:T(8,128)(2,1)S(1)}, bf16[256,672]{1,0:T(8,128)(2,1)}, u32[]{:S(2)}) copy-start(bf16[256,672]{1,0:T(8,128)(2,1)} %constant.34.clone.refs_8_) | copy-start | bytes 1032196
  14.7 1.1 %copy-start.4 = (f32[672,1]{1,0:T(8,128)S(1)}, f32[672,1]{1,0:T(8,128)}, u32[]{:S(2)}) copy-start(f32[672,1]{1,0:T(8,128)} %constant.35.clone.refs_9_) | copy-start | bytes 8068
  14.7 1.1 %copy-start.7 = (bf16[512,128]{1,0:T(8,128)(2,1)S(1)}, bf16[512,128]{1,0:T(8,128)(2,1)}, u32[]{:S(2)}) copy-start(bf16[512,128]{1,0:T(8,128)(2,1)} %constant.33.clone.refs_7_) | copy-start | bytes 393220
  14.7 1.1 %copy-start.8 = (f32[1,512]{1,0:T(1,128)S(1)}, f32[1,512]{1,0:T(1,128)}, u32[]{:S(2)}) copy-start(f32[1,512]{1,0:T(1,128)} %constant.36.clone.refs_10_) | copy-start | bytes 6148

commit v3 on v2

v3 whole, which is shorter than its diff:
```python
import functools
import math

import jax
import jax.numpy as jnp
import ml_dtypes
import numpy as np
from jax import lax
from jax.experimental import pallas as pl
from jax.experimental.pallas import tpu as pltpu
from jax.sharding import PartitionSpec as P

TS = 384
STRIP = 256
OUTC = 128
CHUNK = 16
LANES = 256
VMEM_BYTES = 24 * 1024 * 1024


def cos_sin(freqs, places, modulus):
    residue = freqs[:, None] * places[None, :] % modulus
    lowest = np.minimum(residue, modulus - residue)
    flipped = np.where(residue > modulus - residue, -1.0, 1.0).astype(np.float32)
    angle = lowest.astype(np.float32) * np.float32(2.0 * math.pi / modulus)
    sine = np.where(2 * lowest == modulus, np.float32(0.0), flipped * np.sin(angle))
    return np.cos(angle).astype(np.float32), sine.astype(np.float32)


def round_up(value, multiple):
    return -(-value // multiple) * multiple


@functools.lru_cache(maxsize=None)
def tables(width_rows, width_cols):
    half = width_cols // 2
    rows = width_rows // 2 + 1
    padded = round_up(rows, CHUNK)
    bf16 = ml_dtypes.bfloat16
    places = np.arange(width_cols)
    cos_v, sin_v = cos_sin(np.arange(half + 1), places, width_cols)
    packed_sin = sin_v[:half].copy()
    forward_sin = -packed_sin
    forward_sin[0] = cos_v[half]
    packed_sin[0] = cos_v[half]
    col = np.concatenate([cos_v[:half], forward_sin], 0).T.astype(bf16)
    back = (2.0 * np.concatenate([cos_v[:half], packed_sin], 0)[:, :OUTC].astype(bf16).astype(np.float32)).astype(bf16)
    cos_u, sin_u = cos_sin(np.arange(rows), np.arange(width_rows), width_rows)
    row = np.zeros((2 * padded, width_rows), np.float32)
    row[:rows] = cos_u
    row[padded : padded + rows] = -sin_u
    row = row.astype(bf16)
    weight = np.ones((rows, 1), np.float32)
    weight[0] = weight[-1] = 0.5
    out = np.zeros((2 * padded, STRIP), np.float32)
    out[:rows] = cos_u[:, :STRIP].astype(bf16).astype(np.float32) * weight
    out[padded : padded + rows] = sin_u[:, :STRIP].astype(bf16).astype(np.float32) * weight
    tall = round_up(padded, 128)
    out = np.concatenate([np.pad(part, ((0, tall - padded), (0, 0))) for part in (out[:padded], out[padded:])])
    out = np.ascontiguousarray(out.T).astype(bf16)
    row_sum = row[:, :TS].astype(np.float32).sum(1, keepdims=True)
    col_sum = col[:TS].astype(np.float32).sum(0, keepdims=True)
    return col, row, back, out, row_sum, col_sum


def swapped(value, axis, step):
    count = lax.axis_size(axis)
    return lax.ppermute(value, axis, [(source, source ^ step) for source in range(count)])


def spread_out(value, axis):
    held, step = {0: value}, lax.axis_size(axis) // 2
    while step > 1:
        held |= {index ^ step: swapped(block, axis, step) for index, block in held.items()}
        step //= 2
    return [held[index] for index in sorted(held)[1:]]


def with_partners(blocks, axis):
    return [block for held in blocks for block in (held, swapped(held, axis, 1))]


def dot(left, right):
    return jnp.dot(left, right, preferred_element_type=jnp.float32)


def tiles(padded, half):
    return [(slice(r, r + CHUNK), lane) for r in range(0, padded, CHUNK) for lane in (0,)]


def lanes(lane):
    return slice(lane, lane + LANES)


def where_first(lane, special, usual):
    if lane:
        return usual
    return jnp.where(lax.broadcasted_iota(jnp.int32, usual.shape, 1) == 0, special, usual)


def quadrants(load, rows, lane, padded, half):
    down = slice(padded + rows.start, padded + rows.stop)
    left, right = lanes(lane), lanes(half + lane)
    cc, cs, sc, ss = load(rows, left), load(rows, right), load(down, left), load(down, right)
    plus_re = cc - where_first(lane, 0.0, ss)
    plus_im = where_first(lane, 0.0, cs) + sc
    minus_re = where_first(lane, cs, cc + ss)
    minus_im = where_first(lane, ss, cs - sc)
    return plus_re, plus_im, minus_re, minus_im


def squared(signs):
    return signs[0] * signs[0] + signs[1] * signs[1], signs[2] * signs[2] + signs[3] * signs[3]


def sum_power(source_ref, power_ref, loads):
    padded, half = power_ref.shape[1:]
    total = 0.0
    for rows, lane in tiles(padded, half):
        at = lanes(lane)
        zero = jnp.zeros((CHUNK, LANES), jnp.float32)
        plus, minus = (zero, zero) if source_ref is None else (source_ref[0, rows, at], source_ref[1, rows, at])
        for load in loads:
            more = squared(quadrants(load, rows, lane, padded, half))
            plus, minus = plus + more[0], minus + more[1]
        power_ref[0, rows, at] = plus
        power_ref[1, rows, at] = minus
        total = total + (plus + minus)
    return total


def mean_power(total, power_ref, count, width_rows):
    last = width_rows // 2
    ends = [power_ref[0, r : r + 1] + power_ref[1, r : r + 1] for r in (0, last)]
    whole = 2.0 * jnp.sum(total, keepdims=True) - jnp.sum(ends[0] + ends[1], keepdims=True)
    return whole / (count * width_rows * 2 * power_ref.shape[2])


def whiten(power_ref, mean, count, ctf_ref, loads, weighted_ref):
    padded, half = power_ref.shape[1:]
    for rows, lane in tiles(padded, half):
        at = lanes(lane)
        gains = [lax.rsqrt(power_ref[side, rows, at] * (1.0 / count) + mean) for side in range(2)]
        for k, load in enumerate(loads):
            signs = quadrants(load, rows, lane, padded, half)
            for side in range(2):
                gain = gains[side] * ctf_ref[k, side, rows, at]
                weighted_ref[k, 2 * side, rows, at] = signs[2 * side] * gain
                weighted_ref[k, 2 * side + 1, rows, at] = signs[2 * side + 1] * gain


def ctf_kernel(half, width_rows, tile_ref, group_a, group_b, defocus_ref, ctf_ref):
    padded = ctf_ref.shape[2]
    u = lax.broadcasted_iota(jnp.int32, (8, round_up(padded, 128)), 1).astype(jnp.float32) / width_rows
    column = lax.broadcasted_iota(jnp.int32, (8, half), 1)
    wrapped = (lax.broadcasted_iota(jnp.int32, (8, half), 0) == 1) & (column == 0)
    v = jnp.where(wrapped, half, column).astype(jnp.float32) / (2 * half)
    for k in range(2):
        group = jnp.where((tile_ref[0] & 1) == k, group_a[0], group_b[0])
        turn = jnp.float32(math.pi) * defocus_ref[group]
        phase_u, phase_v = turn * (u * u) + 0.07, turn * (v * v)
        sin_u, cos_u = jnp.sin(phase_u).T[:padded, :1], jnp.cos(phase_u).T[:padded, :1]
        sin_v, cos_v = jnp.sin(phase_v), jnp.cos(phase_v)
        for r in range(0, padded, CHUNK):
            up = slice(r, r + CHUNK)
            for side in range(2):
                row = slice(side, side + 1)
                ctf_ref[k, side, up] = -(sin_u[up] * cos_v[row] + cos_u[up] * sin_v[row])


def pair_kernel(tile_ref, tpl_a, tpl_b, raw_ref, order_ref):
    bit, depth = tile_ref[0] & 1, tpl_a.shape[1]
    for index in range(raw_ref.shape[0]):
        for j, block in enumerate((tpl_a, tpl_b)):
            rows = pl.ds(pl.multiple_of((bit ^ j) * depth, depth), depth)
            order_ref[index, rows, :] = block[bit * raw_ref.shape[0] + index].astype(order_ref.dtype)
    raw_ref[...] = order_ref[...].astype(raw_ref.dtype)


def moments(block):
    wide = block.astype(jnp.float32)
    return jnp.sum(wide, axis=0, keepdims=True), jnp.sum(wide * wide, axis=0, keepdims=True)


def early_kernel(
    tile_ref, strip_a, strip_b, raw_ref, col_ref, row_ref, deep_ref, column_ref, *outs
):
    tile = tile_ref[0]
    bit = tile & 1
    shape_ref, moment_ref = outs[-2:]
    for j, strip in enumerate((strip_a, strip_b)):
        start = pl.multiple_of((bit ^ j) * STRIP, STRIP)
        column_ref[pl.ds(start, STRIP), :] = dot(strip[...], col_ref[...]).astype(jnp.bfloat16)
    if len(outs) == 3:
        outs[0][0] = dot(row_ref[:, : 2 * STRIP], column_ref[...])
        outs[0][1] = dot(row_ref[:, :STRIP], column_ref[STRIP:, :])
    else:
        stage_kernel(0, tile_ref, column_ref, row_ref, *outs[:2])
    for index in range(shape_ref.shape[0]):
        for k, moment in enumerate(moments(raw_ref[index])):
            moment_ref[2 * index + k : 2 * index + k + 1, :] = moment
        columns = dot(raw_ref[index], col_ref[:TS, :]).astype(jnp.bfloat16)
        shape_ref[index] = dot(deep_ref[tile >> 1], columns)


def rows_of(pair, offset, length):
    return pl.ds(pl.multiple_of(pair * (2 * STRIP), 2 * STRIP) + offset, length)


def other_kernel(count, tile_ref, *refs):
    others = refs[: count - 2]
    column_ref, col_ref, row_ref, part_ref, power_ref, work_ref = refs[count - 2 :]
    width_rows = row_ref.shape[1]
    tile = tile_ref[0]
    own, pairs = tile >> 1, count // 2
    for j in range(2, count):
        start = pl.multiple_of((tile ^ j) * STRIP, STRIP)
        part_ref[pl.ds(start, STRIP), :] = dot(others[j - 2][...], col_ref[...]).astype(jnp.bfloat16)
    part_ref[rows_of(own, 0, 2 * STRIP), :] = column_ref[...]
    for j in range(1, pairs):
        pair = own ^ j

        @pl.when(pair + 1 < pairs)
        def _():
            work_ref[0] = dot(row_ref[...], part_ref[rows_of(pair, 0, width_rows), :])
            work_ref[1] = dot(row_ref[...], part_ref[rows_of(pair, STRIP, width_rows), :])

        @pl.when(pair + 1 == pairs)
        def _():
            work_ref[0] = dot(row_ref[:, : 2 * STRIP], part_ref[rows_of(pair, 0, 2 * STRIP), :])
            work_ref[1] = dot(row_ref[:, :STRIP], part_ref[rows_of(pair, STRIP, STRIP), :])

        loads = [lambda rows, at, k=k: work_ref[k, rows, at] for k in range(2)]
        sum_power(None if j == 1 else power_ref, power_ref, loads)
    if pairs == 1:
        power_ref[...] = jnp.zeros(power_ref.shape, jnp.float32)


def own_kernel(count, tile_ref, part_ref, partial_ref, others_ref, ctf_ref, row_ref, weighted_ref, cross_ref, power_ref):
    width_rows = row_ref.shape[1]
    own, pairs = tile_ref[0] >> 1, count // 2

    def finish(loads):
        total = sum_power(others_ref, power_ref, loads)
        whiten(power_ref, mean_power(total, power_ref, count, width_rows), count, ctf_ref, loads, weighted_ref)

    @pl.when(own + 1 < pairs)
    def _():
        cross_ref[0] = dot(row_ref[:, 2 * STRIP :], part_ref[rows_of(own + 1, 0, width_rows - 2 * STRIP), :])
        cross_ref[1] = dot(row_ref[:, STRIP:], part_ref[rows_of(own + 1, 0, width_rows - STRIP), :])
        finish([lambda rows, at, k=k: partial_ref[k, rows, at] + cross_ref[k, rows, at] for k in range(2)])

    @pl.when(own + 1 == pairs)
    def _():
        finish([lambda rows, at, k=k: partial_ref[k, rows, at] for k in range(2)])


def span(strip, blocks):
    start = max(strip, blocks[0])
    stop = min((strip + 1) * STRIP + TS, (blocks[-1] + 1) * STRIP)
    return slice(start * STRIP - strip * STRIP, stop - strip * STRIP), slice(
        (start - blocks[0]) * STRIP, stop - blocks[0] * STRIP
    )


def reached(blocks):
    return [s for s in range(4) if s <= blocks[-1] and (s + 1) * STRIP + TS > blocks[0] * STRIP]


def sources(tile):
    sets = [[tile & 2, tile & 2 | 1], [tile ^ 2], [tile ^ 3]]
    strips = [reached(blocks) for blocks in sets]
    return sets, strips, [[k for k in range(3) if s in strips[k]] for s in range(4)]


def summed(refs, strip, which):
    def load(rows, at):
        parts = [refs[k][strip, rows, at] for k in which]
        return functools.reduce(lambda left, right: left + right, parts)

    return load


def add_blocks(case, stage, block_ref, row_ref, quad_ref):
    sets, strips, _ = sources(case)
    for s in strips[stage]:
        columns, rows = span(s, sets[stage])
        quad_ref[s] = dot(row_ref[:, columns], block_ref[rows, :])


def stage_kernel(stage, tile_ref, *refs):
    earlier, refs = refs[:stage], refs[stage:]
    if stage:
        previous, strip_ref, col_ref, row_ref, quad_ref, power_ref, block_ref = refs
        block_ref[...] = dot(strip_ref[...], col_ref[...]).astype(jnp.bfloat16)
    else:
        previous, (block_ref, row_ref, quad_ref, power_ref) = None, refs
    quads = [*earlier, quad_ref]
    for case in range(4):

        @pl.when(tile_ref[0] == case)
        def _():
            add_blocks(case, stage, block_ref, row_ref, quad_ref)
            needs = sources(case)[2]
            done = [s for s in range(4) if max(needs[s]) == stage]
            sum_power(previous, power_ref, [summed(quads, s, needs[s]) for s in done])


def last_kernel(
    tile_ref, first_ref, second_ref, previous_ref, strip_ref, col_ref, row_ref, ctf_ref,
    weighted_ref, third_ref, power_ref, block_ref,
):
    block_ref[...] = dot(strip_ref[...], col_ref[...]).astype(jnp.bfloat16)
    quads = [first_ref, second_ref, third_ref]
    for case in range(4):

        @pl.when(tile_ref[0] == case)
        def _():
            add_blocks(case, 2, block_ref, row_ref, third_ref)
            needs = sources(case)[2]
            loads = [summed(quads, s, needs[s]) for s in range(4)]
            total = sum_power(previous_ref, power_ref, [loads[s] for s in range(4) if max(needs[s]) == 2])
            mean = mean_power(total, power_ref, 4, STRIP + TS)
            whiten(power_ref, mean, 4, ctf_ref, loads[case & 2 : (case & 2) + 2], weighted_ref)


def score_kernel(count, tile_ref, *refs):
    pairs = count // 2
    others = refs[: pairs - 1]
    (weighted_ref, shape_ref, moment_ref, col_ref, deep_ref, back_ref, out_ref, row_sum_ref, col_sum_ref) = refs[
        pairs - 1 : pairs + 8
    ]
    score_ref, quad_ref, product_ref, y_ref = refs[pairs + 8 :]
    padded, half = deep_ref.shape[1] // 2, col_ref.shape[1] // 2
    scale = 1.0 / ((STRIP + TS) * col_ref.shape[0])
    pieces, mine = score_ref.shape[:2]
    tile = tile_ref[0]
    tall = y_ref.shape[0] // 2
    for h in range(2):
        y_ref[tall * h + padded : tall * (h + 1), :] = jnp.zeros((tall - padded, 2 * OUTC), jnp.bfloat16)
    for index in range(mine):
        sums, squares = (moment_ref[2 * index + k : 2 * index + k + 1, :] for k in range(2))
        for j in range(1, pairs):
            more = moments(others[j - 1][index])
            sums, squares = sums + more[0], squares + more[1]
            columns = dot(others[j - 1][index], col_ref[:TS, :]).astype(jnp.bfloat16)
            late = dot(deep_ref[(tile >> 1) ^ j], columns)
            quad_ref[...] = late if j == 1 else quad_ref[...] + late
        mean = jnp.sum(sums, keepdims=True) / (TS * TS)
        spread = jnp.sqrt(jnp.sum(squares, keepdims=True) / (TS * TS) - mean * mean + 1e-05)
        col_sum = mean * col_sum_ref[...]

        def load(rows, at):
            known = shape_ref[index, rows, at] + quad_ref[rows, at] if pairs > 1 else shape_ref[index, rows, at]
            return known - row_sum_ref[rows, :] * col_sum[:, at]

        for rows, lane in tiles(padded, half):
            a, b, c, d = quadrants(load, rows, lane, padded, half)
            left, right = lanes(lane), lanes(half + lane)
            for k in range(2):
                p, q, s, t = (weighted_ref[k, m, rows, left] for m in range(4))
                plus_re, plus_im = p * a + q * b, q * a - p * b
                minus_re, minus_im = s * c + t * d, t * c - s * d
                up = slice(2 * k * padded + rows.start, 2 * k * padded + rows.stop)
                down = slice(up.start + padded, up.stop + padded)
                parts = (
                    (up, left, plus_re + where_first(lane, 0.0, minus_re)),
                    (up, right, where_first(lane, minus_re, -(plus_im + minus_im))),
                    (down, left, where_first(lane, 0.0, minus_im) - plus_im),
                    (down, right, where_first(lane, -minus_im, minus_re - plus_re)),
                )
                for height, at, value in parts:
                    product_ref[height, at] = value.astype(jnp.bfloat16)
        back = dot(product_ref[...], back_ref[...]).astype(jnp.bfloat16)
        for k in range(2):
            for h in range(2):
                part = back[(2 * k + h) * padded : (2 * k + h + 1) * padded]
                y_ref[tall * h : tall * h + padded, k * OUTC : (k + 1) * OUTC] = part
        score = dot(out_ref[...], y_ref[...]) * (scale / spread)
        for k in range(2):
            strip = score[:, k * OUTC : (k + 1) * OUTC].reshape(pieces // 2, 2 * STRIP // pieces, OUTC)
            score_ref[k * (pieces // 2) : (k + 1) * (pieces // 2), index] = strip.astype(jnp.bfloat16)


def on_device(kernel, scalars, operands, scratch, result, cost):
    vmem, smem = pl.BlockSpec(memory_space=pltpu.VMEM), pl.BlockSpec(memory_space=pltpu.SMEM)
    return pl.pallas_call(
        kernel,
        out_shape=result,
        in_specs=[smem] * len(scalars) + [vmem] * len(operands),
        out_specs=jax.tree.map(lambda _: vmem, result),
        scratch_shapes=scratch,
        compiler_params=pltpu.CompilerParams(vmem_limit_bytes=VMEM_BYTES),
        cost_estimate=None if cost is None else pl.CostEstimate(flops=cost, bytes_accessed=0, transcendentals=0),
    )(*scalars, *operands)


def local(micrograph, templates, defocus, group_of_tile):
    width_cols = micrograph.shape[1]
    width_rows = STRIP + TS
    tpl_count, depth = templates.shape[:2]
    count = lax.axis_size("tile")
    orient_count = lax.axis_size("orient")
    col, row, back, out, row_sum, col_sum = tables(width_rows, width_cols)
    deep = np.stack(np.split(row[:, :TS], count // 2, axis=1))
    padded, half = row.shape[0] // 2, width_cols // 2
    tile = lax.axis_index("tile").astype(jnp.int32).reshape(1)
    plane, quads = (padded, half), (2 * padded, width_cols)
    f32, bf16 = jnp.float32, jnp.bfloat16
    mine = tpl_count // 2
    pass_flops = 2 * quads[0] * quads[1] * STRIP

    strips = spread_out(micrograph, "tile")
    raw = on_device(
        pair_kernel,
        [tile],
        [templates, swapped(templates, "tile", 1)],
        [pltpu.VMEM((mine, 2 * depth, TS), bf16 if depth % 16 == 0 else f32)],
        jax.ShapeDtypeStruct((mine, 2 * depth, TS), bf16),
        None,
    )
    pieces = spread_out(raw, "tile")
    ctf = on_device(
        functools.partial(ctf_kernel, half, width_rows),
        [tile, group_of_tile, swapped(group_of_tile, "tile", 1), defocus],
        [],
        [],
        jax.ShapeDtypeStruct((2, 2, *plane), f32),
        20 * pass_flops,
    )
    early_in = [micrograph, swapped(micrograph, "tile", 1), raw, col, row, deep]
    early_out = [
        jax.ShapeDtypeStruct((mine, *quads), f32),
        jax.ShapeDtypeStruct((round_up(2 * mine, 8), TS), f32),
    ]
    columns_out = jax.ShapeDtypeStruct((2 * STRIP, width_cols), bf16)
    all_quads, power_out = jax.ShapeDtypeStruct((4, *quads), f32), jax.ShapeDtypeStruct((2, *plane), f32)
    weighted_out = jax.ShapeDtypeStruct((2, 4, *plane), f32)
    if count == 4:
        column, quads_0, power, shape, moment = on_device(
            early_kernel, [tile], early_in, [], (columns_out, all_quads, power_out, *early_out), None
        )
        strips, power, ctf = lax.optimization_barrier((strips, power, ctf))
        block = pltpu.VMEM((STRIP, width_cols), bf16)
        quads_1, power = on_device(
            functools.partial(stage_kernel, 1),
            [tile],
            [quads_0, power, strips[0], col, row],
            [block],
            (all_quads, power_out),
            30 * pass_flops,
        )
        weighted = on_device(
            last_kernel,
            [tile],
            [quads_0, quads_1, power, swapped(strips[0], "tile", 1), col, row, ctf],
            [pltpu.VMEM((4, *quads), f32), pltpu.VMEM((2, *plane), f32), block],
            weighted_out,
            12 * pass_flops,
        )
    else:
        column, partial, shape, moment = on_device(
            early_kernel,
            [tile],
            early_in,
            [],
            (columns_out, jax.ShapeDtypeStruct((2, *quads), f32), *early_out),
            None,
        )
        strips, column, ctf = lax.optimization_barrier((strips, column, ctf))
        part, power = on_device(
            functools.partial(other_kernel, count),
            [tile],
            [*with_partners(strips, "tile"), column, col, row],
            [pltpu.VMEM((2, *quads), f32)],
            (jax.ShapeDtypeStruct((count * STRIP, width_cols), bf16), power_out),
            None,
        )
        weighted = on_device(
            functools.partial(own_kernel, count),
            [tile],
            [part, partial, power, ctf, row],
            [pltpu.VMEM((2, *quads), f32), pltpu.VMEM((2, *plane), f32)],
            weighted_out,
            None,
        )
    scores = on_device(
        functools.partial(score_kernel, count),
        [tile],
        [*pieces, weighted, shape, moment, col, deep, back, out, row_sum, col_sum],
        [
            pltpu.VMEM(quads, f32),
            pltpu.VMEM((4 * padded, width_cols), bf16),
            pltpu.VMEM((out.shape[1], 2 * OUTC), bf16),
        ],
        jax.ShapeDtypeStruct((2 * orient_count, mine, STRIP // orient_count, OUTC), bf16),
        None,
    )
    chips = [[first + k for k in range(2 * orient_count)] for first in range(0, count * orient_count, 2 * orient_count)]
    received = lax.all_to_all(
        scores, ("tile", "orient"), split_axis=0, concat_axis=0, tiled=True, axis_index_groups=chips
    ).astype(f32)
    orient_total = tpl_count * orient_count
    best = jnp.max(received, axis=(0, 1))
    score_mean = jnp.sum(received, axis=(0, 1)) / orient_total
    score_var = jnp.sum(received * received, axis=(0, 1)) / orient_total - score_mean * score_mean
    return (best, (best - score_mean) / jnp.sqrt(score_var + 1e-05))


def solution(mesh):
    placed = (P("tile", None), P("orient", "tile", None), P(), P("tile"))
    return jax.shard_map(
        local,
        mesh=mesh,
        in_specs=placed,
        out_specs=(P(("tile", "orient"), None), P(("tile", "orient"), None)),
        check_vma=False,
    )
```

time: 32.9 us -> 32 us (0.973)
  starting transfers between devices: 4.68 us -> 3.96 us
    ppermute x8 -> x6, starting transfers between devices: 4.68 us -> 3.96 us  [swapped(): lax.ppermute(value, axis, [(source, source ^ step) for source in range(co...]
    pallas_call x7 -> x6, Pallas kernels: 9.74 us -> 9.54 us  [on_device(): pl.pallas_call(kernel, out_shape=result, in_specs=[smem] * len(scalars) +...]
    ppermute x8 -> x6, waiting for transfers between devices: 1.4 us -> 1.57 us  [swapped(): lax.ppermute(value, axis, [(source, source ^ step) for source in range(co...]
  transfers between devices with their start and end apart: 8 -> 6, of which waited for: 4 -> 3; matrix products, arithmetic and copies ran while one was open for 0% -> 0% of each run, Pallas kernels for 23% -> 24%
where the time goes in v3:
time: 32 us; the launch traced here: 31.7 us
  blocking collectives  13.9 us (43%)
  Pallas kernels  9.54 us (30%)
  starting transfers between devices  3.96 us (12%)
  waiting for transfers between devices  1.57 us (5%)
  between operations  1.43 us (4%)
  local copies, waits for them, and re-layouts  0.69 us (2%)
  other arithmetic  0.69 us (2%)
    all_to_all x1, blocking collectives, local(): lax.all_to_all(scores, ('tile', 'orient'), split_axis=0, concat_axis=0, t...  13.9 us
    pallas_call x6, Pallas kernels, on_device(): pl.pallas_call(kernel, out_shape=result, in_specs=[smem] * len(scalars) +...  9.54 us
    ppermute x6, starting transfers between devices, swapped(): lax.ppermute(value, axis, [(source, source ^ step) for source in range(co...  3.96 us
    ppermute x6, waiting for transfers between devices, swapped(): lax.ppermute(value, axis, [(source, source ^ step) for source in range(co...  1.57 us
    unnamed x20, local copies, waits for them, and re-layouts  0.69 us
  transfers between devices with their start and end apart: 6, of which 3 were waited for; matrix products, arithmetic and copies ran while one was open for 0% of the time, Pallas kernels for 24%

profile of v3, /device:TPU:0, one launch (start us, length us, event | category | flops | bytes accessed | tf_op | source)
XLA Modules:
  0.0 31.7 jit_solution(5450401797202310103)
XLA Ops:
  0.6 0.5 %collective-permute-start.2 = (bf16[256,512]{1,0:T(8,128)(2,1)}, bf16[256,512]{1,0:T(8,128)(2,1)S(1)}, u32[]{:S(2)}, u32[]{:S(2)}) collective-permute-start(bf16[256,512]{1,0:T(8,128)(2,1)} %strip_a.1), channel_id=1, source_target_pairs={{0,8},{8,0},{16,24},{24,16},{1,9},{9,1},{17,25},{25,17},{2,10},{10... | collective-permute-start | bytes 786440 | tf_op jit(solution)/shard_map/ppermute | solution.py:68
  1.1 2.6 %collective-permute-start.3 = (bf16[256,512]{1,0:T(8,128)(2,1)}, bf16[256,512]{1,0:T(8,128)(2,1)S(1)}, u32[]{:S(2)}, u32[]{:S(2)}) collective-permute-start(bf16[256,512]{1,0:T(8,128)(2,1)} %strip_a.1), channel_id=1, source_target_pairs={{0,16},{8,24},{16,0},{24,8},{1,17},{9,25},{17,1},{25,9},{2,18},{10... | collective-permute-start | bytes 786440 | tf_op jit(solution)/shard_map/ppermute | solution.py:68
  3.7 0.2 collective-permute-start.4
  3.9 0.3 %collective-permute-start = (bf16[2,96,384]{2,1,0:T(8,128)(2,1)}, bf16[2,96,384]{2,1,0:T(8,128)(2,1)S(1)}, u32[]{:S(2)}, u32[]{:S(2)}) collective-permute-start(bf16[2,96,384]{2,1,0:T(8,128)(2,1)} %tpl_a.1), channel_id=1, source_target_pairs={{0,8},{8,0},{16,24},{24,16},{1,9},{9,1},{17,25},{25,17},{2,10},{10... | collective-permute-start | bytes 442376 | tf_op jit(solution)/shard_map/ppermute | solution.py:68
  4.9 0.1 collective-permute-done.4.group_b
  5.0 0.7 %copy-done.9 = f32[4]{0:T(128)S(1)} copy-done((f32[4]{0:T(128)S(1)}, f32[4]{0:T(128)}, u32[]{:S(2)}) %copy-start.9) | copy-done | bytes 40
  5.6 0.0 copy-start.5
  5.6 1.9 %shard_map.124.ctf_ref = f32[2,2,336,256]{3,2,1,0:T(8,128)S(1)} custom-call(s32[1]{0:T(128)} %bitcast.tile_ref, s32[1]{0:T(128)S(6)} %copy.13.group_a, s32[1]{0:T(128)} %collective-permute-done.4.group_b, f32[4]{0:T(128)S(1)} %copy-done.9), custom_call_target="tpu_custom_call" | custom-call | flops 3523215360 | tf_op jit(solution)/shard_map/pallas_call | solution.py:387
  7.5 0.0 collective-permute-done.tpl_b
  7.5 0.0 copy-done.6
  7.6 0.4 %collective-permute-start.1 = (bf16[1,192,384]{2,1,0:T(8,128)(2,1)S(1)}, bf16[1,192,384]{2,1,0:T(8,128)(2,1)S(1)}, u32[]{:S(2)}, u32[]{:S(2)}) collective-permute-start(bf16[1,192,384]{2,1,0:T(8,128)(2,1)S(1)} %shard_map.122.raw_ref), channel_id=1, source_target_pairs={{0,16},{8,24},{16,0},{24,8},{1,17},{9,25},{17,1},{25,9},{2,18},{10... | collective-permute-start | bytes 442376 | tf_op jit(solution)/shard_map/ppermute | solution.py:68
  7.9 0.0 collective-permute-done.2.strip_b
  7.9 0.0 copy-done.2
  8.0 0.0 copy-done.5
  8.0 2.0 %shard_map.123 = (bf16[512,512]{1,0:T(8,128)(2,1)}, f32[4,672,512]{2,1,0:T(8,128)S(1)}, f32[2,336,256]{2,1,0:T(8,128)S(1)}, f32[1,672,512]{2,1,0:T(8,128)S(1)}, f32[8,384]{1,0:T(8,128)S(1)}) custom-call(s32[1]{0:T(128)} %bitcast.tile_ref, bf16[256,512]{1,0:T(8,128)(2,1)S(1)} %copy-done.5, bf16[256,512]{1,0:T(8,128)(2,1)S(1)} %collective-permute-done.2.strip_b, ...), custom_call_target="tpu_custom_call" | custom-call | tf_op jit(solution)/shard_map/pallas_call | solution.py:387
  9.9 1.1 %collective-permute-done.3.refs_2_ = bf16[256,512]{1,0:T(8,128)(2,1)S(1)} collective-permute-done((bf16[256,512]{1,0:T(8,128)(2,1)}, bf16[256,512]{1,0:T(8,128)(2,1)S(1)}, u32[]{:S(2)}, u32[]{:S(2)}) %collective-permute-start.3) | collective-permute-done | bytes 262176 | tf_op jit(solution)/shard_map/ppermute | solution.py:68
  11.1 0.0 collective-permute-start.5
  11.1 1.2 %shard_map.125 = (f32[4,672,512]{2,1,0:T(8,128)S(1)}, f32[2,336,256]{2,1,0:T(8,128)S(1)}) custom-call(s32[1]{0:T(128)} %bitcast.tile_ref, f32[4,672,512]{2,1,0:T(8,128)S(1)} %get-tuple-element.11.refs_0_.first_ref, f32[2,336,256]{2,1,0:T(8,128)S(1)} %get-tuple-element.13.refs_1_, bf16[256,512]{1,0:T(8,128)(2,1)S(1)} %collective-permute-done.3.refs_2_, ...), custom_call_target="tpu_custom_call" | custom-call | flops 5284823040 | tf_op jit(solution)/shard_map/pallas_call | solution.py:387
  12.3 0.3 %collective-permute-done.5.strip_ref = bf16[256,512]{1,0:T(8,128)(2,1)S(1)} collective-permute-done((bf16[256,512]{1,0:T(8,128)(2,1)S(1)}, bf16[256,512]{1,0:T(8,128)(2,1)S(1)}, u32[]{:S(2)}, u32[]{:S(2)}) %collective-permute-start.5) | collective-permute-done | bytes 262176 | tf_op jit(solution)/shard_map/ppermute | solution.py:68
  12.6 2.4 %shard_map.126.refs_1_ = f32[2,4,336,256]{3,2,1,0:T(8,128)S(1)} custom-call(s32[1]{0:T(128)} %bitcast.tile_ref, f32[4,672,512]{2,1,0:T(8,128)S(1)} %get-tuple-element.11.refs_0_.first_ref, f32[4,672,512]{2,1,0:T(8,128)S(1)} %get-tuple-element.15.second_ref, f32[2,336,256]{2,1,0:T(8,128)S(1)} %get-tuple-element.16.previous_ref, ...), custom_call_target="tpu_custom_call" | custom-call | flops 2113929216 | tf_op jit(solution)/shard_map/pallas_call | solution.py:387
  15.1 0.0 collective-permute-done.1.refs_0_
  15.1 2.1 %shard_map.127 = bf16[16,1,32,128]{3,2,1,0:T(8,128)(2,1)S(1)} custom-call(s32[1]{0:T(128)} %bitcast.tile_ref, bf16[1,192,384]{2,1,0:T(8,128)(2,1)S(1)} %collective-permute-done.1.refs_0_, f32[2,4,336,256]{3,2,1,0:T(8,128)S(1)} %shard_map.126.refs_1_, f32[1,672,512]{2,1,0:T(8,128)S(1)} %get-tuple-element.18.refs_2_, f32[8,384]{1,0:T(8,128)S(1)} %get-tuple-element.19.refs_3_, ...), custom_call_target="tpu_custom_call" | custom-call | tf_op jit(solution)/shard_map/pallas_call | solution.py:387
  17.2 13.9 %all_to_all.5 = bf16[16,1,32,128]{3,2,1,0:T(8,128)(2,1)S(1)} all-to-all(bf16[16,1,32,128]{3,2,1,0:T(8,128)(2,1)S(1)} %shard_map.127), channel_id=1, replica_groups={{0,1,2,3,4,5,6,7,8,9,10,11,12,13,14,15},{16,17,18,19,20,21,22,23,24,25,..., dimensions={0} | all-to-all | bytes 262144 | tf_op jit(solution)/shard_map/all_to_all | solution.py:500
  31.1 0.6 %rsqrt_multiply_fusion = (f32[32,128]{1,0:T(8,128)}, f32[32,128]{1,0:T(8,128)}) fusion(f32[32,128]{1,0:T(8,128)S(1)} %get-tuple-element.21, f32[32,128]{1,0:T(8,128)S(1)} %get-tuple-element.20, bf16[32,128]{1,0:T(8,128)(2,1)S(1)} %reduce_max.14), kind=kLoop, calls=%fused_computation.3 | loop fusion | flops 32768 | bytes 73728 | tf_op jit(solution)/shard_map/div | solution.py:507
  (18 shorter events, 0.1 us)
Async XLA Ops:
  0.6 7.3 %collective-permute-start.2 = (bf16[256,512]{1,0:T(8,128)(2,1)}, bf16[256,512]{1,0:T(8,128)(2,1)S(1)}, u32[]{:S(2)}, u32[]{:S(2)}) collective-permute-start(bf16[256,512]{1,0:T(8,128)(2,1)} %strip_a.1), channel_id=1, source_target_pairs={{0,8},{8,0},{16,24},{24,16},{1,9},{9,1},{17,25},{25,17},{2,10},{10... | collective-permute-start | bytes 786440 | tf_op jit(solution)/shard_map/ppermute | solution.py:68
  1.1 9.9 %collective-permute-start.3 = (bf16[256,512]{1,0:T(8,128)(2,1)}, bf16[256,512]{1,0:T(8,128)(2,1)S(1)}, u32[]{:S(2)}, u32[]{:S(2)}) collective-permute-start(bf16[256,512]{1,0:T(8,128)(2,1)} %strip_a.1), channel_id=1, source_target_pairs={{0,16},{8,24},{16,0},{24,8},{1,17},{9,25},{17,1},{25,9},{2,18},{10... | collective-permute-start | bytes 786440 | tf_op jit(solution)/shard_map/ppermute | solution.py:68
  3.7 1.2 %collective-permute-start.4 = (s32[1]{0:T(128)}, s32[1]{0:T(128)}, u32[]{:S(2)}, u32[]{:S(2)}) collective-permute-start(s32[1]{0:T(128)} %param.14), channel_id=1, source_target_pairs={{0,8},{8,0},{16,24},{24,16},{1,9},{9,1},{17,25},{25,17},{2,10},{10... | collective-permute-start | bytes 20 | tf_op jit(solution)/shard_map/ppermute | solution.py:68
  3.9 3.6 %collective-permute-start = (bf16[2,96,384]{2,1,0:T(8,128)(2,1)}, bf16[2,96,384]{2,1,0:T(8,128)(2,1)S(1)}, u32[]{:S(2)}, u32[]{:S(2)}) collective-permute-start(bf16[2,96,384]{2,1,0:T(8,128)(2,1)} %tpl_a.1), channel_id=1, source_target_pairs={{0,8},{8,0},{16,24},{24,16},{1,9},{9,1},{17,25},{25,17},{2,10},{10... | collective-permute-start | bytes 442376 | tf_op jit(solution)/shard_map/ppermute | solution.py:68
  4.9 0.7 %copy-start.9 = (f32[4]{0:T(128)S(1)}, f32[4]{0:T(128)}, u32[]{:S(2)}) copy-start(f32[4]{0:T(128)} %defocus_ref.1) | copy-start | bytes 52
  5.6 1.9 %copy-start.6 = (bf16[2,96,384]{2,1,0:T(8,128)(2,1)S(1)}, bf16[2,96,384]{2,1,0:T(8,128)(2,1)}, u32[]{:S(2)}) copy-start(bf16[2,96,384]{2,1,0:T(8,128)(2,1)} %tpl_a.1) | copy-start | bytes 442372
  5.6 2.3 %copy-start = (bf16[512,512]{1,0:T(8,128)(2,1)S(1)}, bf16[512,512]{1,0:T(8,128)(2,1)}, u32[]{:S(2)}) copy-start(bf16[512,512]{1,0:T(8,128)(2,1)} %constant.30.clone.col_ref.refs_3_.refs_4_) | copy-start | bytes 1572868
  5.6 2.3 %copy-start.1 = (bf16[672,640]{1,0:T(8,128)(2,1)S(1)}, bf16[672,640]{1,0:T(8,128)(2,1)}, u32[]{:S(2)}) copy-start(bf16[672,640]{1,0:T(8,128)(2,1)} %constant.31.clone.row_ref.refs_4_) | copy-start | bytes 2580484
  5.6 2.3 %copy-start.2 = (bf16[2,672,192]{2,1,0:T(8,128)(2,1)S(1)}, bf16[2,672,192]{2,1,0:T(8,128)(2,1)}, u32[]{:S(2)}) copy-start(bf16[2,672,192]{2,1,0:T(8,128)(2,1)} %constant.32.clone.deep_ref.refs_5_) | copy-start | bytes 1548292
  5.6 2.3 %copy-start.5 = (bf16[256,512]{1,0:T(8,128)(2,1)S(1)}, bf16[256,512]{1,0:T(8,128)(2,1)}, u32[]{:S(2)}) copy-start(bf16[256,512]{1,0:T(8,128)(2,1)} %strip_a.1) | copy-start | bytes 786436
  7.6 7.5 %collective-permute-start.1 = (bf16[1,192,384]{2,1,0:T(8,128)(2,1)S(1)}, bf16[1,192,384]{2,1,0:T(8,128)(2,1)S(1)}, u32[]{:S(2)}, u32[]{:S(2)}) collective-permute-start(bf16[1,192,384]{2,1,0:T(8,128)(2,1)S(1)} %shard_map.122.raw_ref), channel_id=1, source_target_pairs={{0,16},{8,24},{16,0},{24,8},{1,17},{9,25},{17,1},{25,9},{2,18},{10... | collective-permute-start | bytes 442376 | tf_op jit(solution)/shard_map/ppermute | solution.py:68
  11.1 1.5 %collective-permute-start.5 = (bf16[256,512]{1,0:T(8,128)(2,1)S(1)}, bf16[256,512]{1,0:T(8,128)(2,1)S(1)}, u32[]{:S(2)}, u32[]{:S(2)}) collective-permute-start(bf16[256,512]{1,0:T(8,128)(2,1)S(1)} %collective-permute-done.3.refs_2_), channel_id=1, source_target_pairs={{0,8},{8,0},{16,24},{24,16},{1,9},{9,1},{17,25},{25,17},{2,10},{10... | collective-permute-start | bytes 786440 | tf_op jit(solution)/shard_map/ppermute | solution.py:68
  12.6 2.5 %copy-start.3 = (bf16[256,768]{1,0:T(8,128)(2,1)S(1)}, bf16[256,768]{1,0:T(8,128)(2,1)}, u32[]{:S(2)}) copy-start(bf16[256,768]{1,0:T(8,128)(2,1)} %constant.34.clone.refs_7_) | copy-start | bytes 1179652
  12.6 2.5 %copy-start.4 = (f32[672,1]{1,0:T(8,128)S(1)}, f32[672,1]{1,0:T(8,128)}, u32[]{:S(2)}) copy-start(f32[672,1]{1,0:T(8,128)} %constant.35.clone.refs_8_) | copy-start | bytes 8068
  12.6 2.5 %copy-start.7 = (bf16[512,128]{1,0:T(8,128)(2,1)S(1)}, bf16[512,128]{1,0:T(8,128)(2,1)}, u32[]{:S(2)}) copy-start(bf16[512,128]{1,0:T(8,128)(2,1)} %constant.33.clone.refs_6_) | copy-start | bytes 393220
  12.6 2.5 %copy-start.8 = (f32[1,512]{1,0:T(1,128)S(1)}, f32[1,512]{1,0:T(1,128)}, u32[]{:S(2)}) copy-start(f32[1,512]{1,0:T(1,128)} %constant.36.clone.refs_9_) | copy-start | bytes 6148

commit v4 on v3

--- a/solution.py
+++ b/solution.py
@@ -14,6 +14,7 @@
 STRIP = 256
 OUTC = 128
 CHUNK = 16
+STEP = 8
 LANES = 256
 VMEM_BYTES = 24 * 1024 * 1024
 
@@ -84,8 +85,8 @@
     return jnp.dot(left, right, preferred_element_type=jnp.float32)
 
 
-def tiles(padded, half):
-    return [(slice(r, r + CHUNK), lane) for r in range(0, padded, CHUNK) for lane in (0,)]
+def tiles(padded, half, step):
+    return [(slice(r, r + step), lane) for r in range(0, padded, step) for lane in range(0, half, LANES)]
 
 
 def lanes(lane):
@@ -116,9 +117,9 @@
 def sum_power(source_ref, power_ref, loads):
     padded, half = power_ref.shape[1:]
     total = 0.0
-    for rows, lane in tiles(padded, half):
+    for rows, lane in tiles(padded, half, STEP):
         at = lanes(lane)
-        zero = jnp.zeros((CHUNK, LANES), jnp.float32)
+        zero = jnp.zeros((STEP, LANES), jnp.float32)
         plus, minus = (zero, zero) if source_ref is None else (source_ref[0, rows, at], source_ref[1, rows, at])
         for load in loads:
             more = squared(quadrants(load, rows, lane, padded, half))
@@ -138,7 +139,7 @@
 
 def whiten(power_ref, mean, count, ctf_ref, loads, weighted_ref):
     padded, half = power_ref.shape[1:]
-    for rows, lane in tiles(padded, half):
+    for rows, lane in tiles(padded, half, STEP):
         at = lanes(lane)
         gains = [lax.rsqrt(power_ref[side, rows, at] * (1.0 / count) + mean) for side in range(2)]
         for k, load in enumerate(loads):
@@ -182,25 +183,35 @@
     return jnp.sum(wide, axis=0, keepdims=True), jnp.sum(wide * wide, axis=0, keepdims=True)
 
 
-def early_kernel(
-    tile_ref, strip_a, strip_b, raw_ref, col_ref, row_ref, deep_ref, column_ref, *outs
-):
+def early_kernel(tile_ref, strip_a, strip_b, raw_ref, col_ref, row_ref, deep_ref, *outs):
     tile = tile_ref[0]
     bit = tile & 1
-    shape_ref, moment_ref = outs[-2:]
+    four = len(outs) == 5
+    column_ref = outs[4] if four else outs[0]
+    shape_ref, moment_ref = outs[2:4]
     for j, strip in enumerate((strip_a, strip_b)):
         start = pl.multiple_of((bit ^ j) * STRIP, STRIP)
         column_ref[pl.ds(start, STRIP), :] = dot(strip[...], col_ref[...]).astype(jnp.bfloat16)
-    if len(outs) == 3:
-        outs[0][0] = dot(row_ref[:, : 2 * STRIP], column_ref[...])
-        outs[0][1] = dot(row_ref[:, :STRIP], column_ref[STRIP:, :])
+    if four:
+        stage_kernel(0, tile_ref, column_ref, row_ref, *outs[:2])
     else:
-        stage_kernel(0, tile_ref, column_ref, row_ref, *outs[:2])
+        outs[1][0] = dot(row_ref[:, : 2 * STRIP], column_ref[...])
+        outs[1][1] = dot(row_ref[:, :STRIP], column_ref[STRIP:, :])
     for index in range(shape_ref.shape[0]):
         for k, moment in enumerate(moments(raw_ref[index])):
             moment_ref[2 * index + k : 2 * index + k + 1, :] = moment
         columns = dot(raw_ref[index], col_ref[:TS, :]).astype(jnp.bfloat16)
         shape_ref[index] = dot(deep_ref[tile >> 1], columns)
+
+
+def by_case(tile, body):
+    def choose(low, high):
+        if high - low == 1:
+            return body(low)
+        middle = (low + high) // 2
+        lax.cond(tile < middle, lambda: choose(low, middle), lambda: choose(middle, high))
+
+    choose(0, 4)
 
 
 def rows_of(pair, offset, length):
@@ -273,19 +284,17 @@
     return sets, strips, [[k for k in range(3) if s in strips[k]] for s in range(4)]
 
 
-def summed(refs, strip, which):
-    def load(rows, at):
-        parts = [refs[k][strip, rows, at] for k in which]
-        return functools.reduce(lambda left, right: left + right, parts)
-
-    return load
-
-
-def add_blocks(case, stage, block_ref, row_ref, quad_ref):
-    sets, strips, _ = sources(case)
+def view(ref, strip):
+    return lambda rows, at: ref[strip, rows, at]
+
+
+def add_blocks(case, stage, block_ref, row_ref, quads):
+    sets, strips, needs = sources(case)
     for s in strips[stage]:
         columns, rows = span(s, sets[stage])
-        quad_ref[s] = dot(row_ref[:, columns], block_ref[rows, :])
+        part = dot(row_ref[:, columns], block_ref[rows, :])
+        before = [k for k in needs[s] if k < stage]
+        quads[stage][s] = quads[before[-1]][s] + part if before else part
 
 
 def stage_kernel(stage, tile_ref, *refs):
@@ -296,14 +305,14 @@
     else:
         previous, (block_ref, row_ref, quad_ref, power_ref) = None, refs
     quads = [*earlier, quad_ref]
-    for case in range(4):
-
-        @pl.when(tile_ref[0] == case)
-        def _():
-            add_blocks(case, stage, block_ref, row_ref, quad_ref)
-            needs = sources(case)[2]
-            done = [s for s in range(4) if max(needs[s]) == stage]
-            sum_power(previous, power_ref, [summed(quads, s, needs[s]) for s in done])
+
+    def body(case):
+        add_blocks(case, stage, block_ref, row_ref, quads)
+        needs = sources(case)[2]
+        done = [s for s in range(4) if max(needs[s]) == stage]
+        sum_power(previous, power_ref, [view(quads[needs[s][-1]], s) for s in done])
+
+    by_case(tile_ref[0], body)
 
 
 def last_kernel(
@@ -312,16 +321,16 @@
 ):
     block_ref[...] = dot(strip_ref[...], col_ref[...]).astype(jnp.bfloat16)
     quads = [first_ref, second_ref, third_ref]
-    for case in range(4):
-
-        @pl.when(tile_ref[0] == case)
-        def _():
-            add_blocks(case, 2, block_ref, row_ref, third_ref)
-            needs = sources(case)[2]
-            loads = [summed(quads, s, needs[s]) for s in range(4)]
-            total = sum_power(previous_ref, power_ref, [loads[s] for s in range(4) if max(needs[s]) == 2])
-            mean = mean_power(total, power_ref, 4, STRIP + TS)
-            whiten(power_ref, mean, 4, ctf_ref, loads[case & 2 : (case & 2) + 2], weighted_ref)
+
+    def body(case):
+        add_blocks(case, 2, block_ref, row_ref, quads)
+        needs = sources(case)[2]
+        loads = [view(quads[needs[s][-1]], s) for s in range(4)]
+        total = sum_power(previous_ref, power_ref, [loads[s] for s in range(4) if max(needs[s]) == 2])
+        mean = mean_power(total, power_ref, 4, STRIP + TS)
+        whiten(power_ref, mean, 4, ctf_ref, loads[case & 2 : (case & 2) + 2], weighted_ref)
+
+    by_case(tile_ref[0], body)
 
 
 def score_kernel(count, tile_ref, *refs):
@@ -330,14 +339,14 @@
     (weighted_ref, shape_ref, moment_ref, col_ref, deep_ref, back_ref, out_ref, row_sum_ref, col_sum_ref) = refs[
         pairs - 1 : pairs + 8
     ]
-    score_ref, quad_ref, product_ref, y_ref = refs[pairs + 8 :]
+    score_ref, quad_ref, product_ref = refs[pairs + 8 :]
     padded, half = deep_ref.shape[1] // 2, col_ref.shape[1] // 2
     scale = 1.0 / ((STRIP + TS) * col_ref.shape[0])
     pieces, mine = score_ref.shape[:2]
     tile = tile_ref[0]
-    tall = y_ref.shape[0] // 2
+    tall = product_ref.shape[0] // 2
     for h in range(2):
-        y_ref[tall * h + padded : tall * (h + 1), :] = jnp.zeros((tall - padded, 2 * OUTC), jnp.bfloat16)
+        product_ref[tall * h + padded : tall * (h + 1), :] = jnp.zeros((tall - padded, 4 * half), jnp.bfloat16)
     for index in range(mine):
         sums, squares = (moment_ref[2 * index + k : 2 * index + k + 1, :] for k in range(2))
         for j in range(1, pairs):
@@ -354,15 +363,14 @@
             known = shape_ref[index, rows, at] + quad_ref[rows, at] if pairs > 1 else shape_ref[index, rows, at]
             return known - row_sum_ref[rows, :] * col_sum[:, at]
 
-        for rows, lane in tiles(padded, half):
+        for rows, lane in tiles(padded, half, CHUNK):
             a, b, c, d = quadrants(load, rows, lane, padded, half)
-            left, right = lanes(lane), lanes(half + lane)
             for k in range(2):
-                p, q, s, t = (weighted_ref[k, m, rows, left] for m in range(4))
+                p, q, s, t = (weighted_ref[k, m, rows, lanes(lane)] for m in range(4))
                 plus_re, plus_im = p * a + q * b, q * a - p * b
                 minus_re, minus_im = s * c + t * d, t * c - s * d
-                up = slice(2 * k * padded + rows.start, 2 * k * padded + rows.stop)
-                down = slice(up.start + padded, up.stop + padded)
+                up, down = rows, slice(rows.start + tall, rows.stop + tall)
+                left, right = lanes(2 * half * k + lane), lanes(2 * half * k + half + lane)
                 parts = (
                     (up, left, plus_re + where_first(lane, 0.0, minus_re)),
                     (up, right, where_first(lane, minus_re, -(plus_im + minus_im))),
@@ -371,14 +379,10 @@
                 )
                 for height, at, value in parts:
                     product_ref[height, at] = value.astype(jnp.bfloat16)
-        back = dot(product_ref[...], back_ref[...]).astype(jnp.bfloat16)
         for k in range(2):
-            for h in range(2):
-                part = back[(2 * k + h) * padded : (2 * k + h + 1) * padded]
-                y_ref[tall * h : tall * h + padded, k * OUTC : (k + 1) * OUTC] = part
-        score = dot(out_ref[...], y_ref[...]) * (scale / spread)
-        for k in range(2):
-            strip = score[:, k * OUTC : (k + 1) * OUTC].reshape(pieces // 2, 2 * STRIP // pieces, OUTC)
+            rows_first = dot(out_ref[...], product_ref[:, 2 * half * k : 2 * half * (k + 1)]).astype(jnp.bfloat16)
+            score = dot(rows_first, back_ref[...]) * (scale / spread)
+            strip = score.reshape(pieces // 2, 2 * STRIP // pieces, OUTC)
             score_ref[k * (pieces // 2) : (k + 1) * (pieces // 2), index] = strip.astype(jnp.bfloat16)
 
 
@@ -437,8 +441,13 @@
     all_quads, power_out = jax.ShapeDtypeStruct((4, *quads), f32), jax.ShapeDtypeStruct((2, *plane), f32)
     weighted_out = jax.ShapeDtypeStruct((2, 4, *plane), f32)
     if count == 4:
-        column, quads_0, power, shape, moment = on_device(
-            early_kernel, [tile], early_in, [], (columns_out, all_quads, power_out, *early_out), None
+        quads_0, power, shape, moment = on_device(
+            early_kernel,
+            [tile],
+            early_in,
+            [pltpu.VMEM(columns_out.shape, bf16)],
+            (all_quads, power_out, *early_out),
+            None,
         )
         strips, power, ctf = lax.optimization_barrier((strips, power, ctf))
         block = pltpu.VMEM((STRIP, width_cols), bf16)
@@ -490,8 +499,7 @@
         [*pieces, weighted, shape, moment, col, deep, back, out, row_sum, col_sum],
         [
             pltpu.VMEM(quads, f32),
-            pltpu.VMEM((4 * padded, width_cols), bf16),
-            pltpu.VMEM((out.shape[1], 2 * OUTC), bf16),
+            pltpu.VMEM((out.shape[1], 2 * width_cols), bf16),
         ],
         jax.ShapeDtypeStruct((2 * orient_count, mine, STRIP // orient_count, OUTC), bf16),
         None,

time: 32 us -> 31.3 us (0.978)
  Pallas kernels: 9.54 us -> 8.66 us
    pallas_call x6, Pallas kernels: 9.54 us -> 8.66 us  [on_device(): pl.pallas_call(kernel, out_shape=result, in_specs=[smem] * len(scalars) +...]
  transfers between devices with their start and end apart: 6 -> 6, of which waited for: 3 -> 3; matrix products, arithmetic and copies ran while one was open for 0% -> 0% of each run, Pallas kernels for 24% -> 22%
where the time goes in v4:
time: 31.3 us; the launch traced here: 31.1 us
  blocking collectives  13.9 us (44%)
  Pallas kernels  8.66 us (28%)
  starting transfers between devices  3.96 us (13%)
  waiting for transfers between devices  1.82 us (6%)
  between operations  1.43 us (5%)
  local copies, waits for them, and re-layouts  0.69 us (2%)
  other arithmetic  0.69 us (2%)
    all_to_all x1, blocking collectives, local(): lax.all_to_all(scores, ('tile', 'orient'), split_axis=0, concat_axis=0, t...  13.9 us
    pallas_call x6, Pallas kernels, on_device(): pl.pallas_call(kernel, out_shape=result, in_specs=[smem] * len(scalars) +...  8.66 us
    ppermute x6, starting transfers between devices, swapped(): lax.ppermute(value, axis, [(source, source ^ step) for source in range(co...  3.96 us
    ppermute x6, waiting for transfers between devices, swapped(): lax.ppermute(value, axis, [(source, source ^ step) for source in range(co...  1.82 us
    unnamed x20, local copies, waits for them, and re-layouts  0.69 us
  transfers between devices with their start and end apart: 6, of which 3 were waited for; matrix products, arithmetic and copies ran while one was open for 0% of the time, Pallas kernels for 22%

profile of v4, /device:TPU:0, one launch (start us, length us, event | category | flops | bytes accessed | tf_op | source)
XLA Modules:
  0.0 31.1 jit_solution(9556940934807985598)
XLA Ops:
  0.6 0.5 %collective-permute-start.2 = (bf16[256,512]{1,0:T(8,128)(2,1)}, bf16[256,512]{1,0:T(8,128)(2,1)S(1)}, u32[]{:S(2)}, u32[]{:S(2)}) collective-permute-start(bf16[256,512]{1,0:T(8,128)(2,1)} %strip_a.1), channel_id=1, source_target_pairs={{0,8},{8,0},{16,24},{24,16},{1,9},{9,1},{17,25},{25,17},{2,10},{10... | collective-permute-start | bytes 786440 | tf_op jit(solution)/shard_map/ppermute | solution.py:69
  1.1 2.6 %collective-permute-start.3 = (bf16[256,512]{1,0:T(8,128)(2,1)}, bf16[256,512]{1,0:T(8,128)(2,1)S(1)}, u32[]{:S(2)}, u32[]{:S(2)}) collective-permute-start(bf16[256,512]{1,0:T(8,128)(2,1)} %strip_a.1), channel_id=1, source_target_pairs={{0,16},{8,24},{16,0},{24,8},{1,17},{9,25},{17,1},{25,9},{2,18},{10... | collective-permute-start | bytes 786440 | tf_op jit(solution)/shard_map/ppermute | solution.py:69
  3.7 0.2 collective-permute-start.4
  3.9 0.3 %collective-permute-start = (bf16[2,96,384]{2,1,0:T(8,128)(2,1)}, bf16[2,96,384]{2,1,0:T(8,128)(2,1)S(1)}, u32[]{:S(2)}, u32[]{:S(2)}) collective-permute-start(bf16[2,96,384]{2,1,0:T(8,128)(2,1)} %tpl_a.1), channel_id=1, source_target_pairs={{0,8},{8,0},{16,24},{24,16},{1,9},{9,1},{17,25},{25,17},{2,10},{10... | collective-permute-start | bytes 442376 | tf_op jit(solution)/shard_map/ppermute | solution.py:69
  4.9 0.1 collective-permute-done.4.group_b
  5.0 0.7 %copy-done.9 = f32[4]{0:T(128)S(1)} copy-done((f32[4]{0:T(128)S(1)}, f32[4]{0:T(128)}, u32[]{:S(2)}) %copy-start.9) | copy-done | bytes 40
  5.6 0.0 copy-start.5
  5.6 1.9 %shard_map.124.ctf_ref = f32[2,2,336,256]{3,2,1,0:T(8,128)S(1)} custom-call(s32[1]{0:T(128)} %bitcast.tile_ref, s32[1]{0:T(128)S(6)} %copy.13.group_a, s32[1]{0:T(128)} %collective-permute-done.4.group_b, f32[4]{0:T(128)S(1)} %copy-done.9), custom_call_target="tpu_custom_call" | custom-call | flops 3523215360 | tf_op jit(solution)/shard_map/pallas_call | solution.py:391
  7.5 0.0 collective-permute-done.tpl_b
  7.5 0.0 copy-done.6
  7.6 0.4 %collective-permute-start.1 = (bf16[1,192,384]{2,1,0:T(8,128)(2,1)S(1)}, bf16[1,192,384]{2,1,0:T(8,128)(2,1)S(1)}, u32[]{:S(2)}, u32[]{:S(2)}) collective-permute-start(bf16[1,192,384]{2,1,0:T(8,128)(2,1)S(1)} %shard_map.122.raw_ref), channel_id=1, source_target_pairs={{0,16},{8,24},{16,0},{24,8},{1,17},{9,25},{17,1},{25,9},{2,18},{10... | collective-permute-start | bytes 442376 | tf_op jit(solution)/shard_map/ppermute | solution.py:69
  7.9 0.0 collective-permute-done.2.strip_b
  7.9 0.0 copy-done.2
  8.0 0.0 copy-done.5
  8.0 1.7 %shard_map.123 = (f32[4,672,512]{2,1,0:T(8,128)S(1)}, f32[2,336,256]{2,1,0:T(8,128)S(1)}, f32[1,672,512]{2,1,0:T(8,128)S(1)}, f32[8,384]{1,0:T(8,128)S(1)}) custom-call(s32[1]{0:T(128)} %bitcast.tile_ref, bf16[256,512]{1,0:T(8,128)(2,1)S(1)} %copy-done.5, bf16[256,512]{1,0:T(8,128)(2,1)S(1)} %collective-permute-done.2.strip_b, ...), custom_call_target="tpu_custom_call" | custom-call | tf_op jit(solution)/shard_map/pallas_call | solution.py:391
  9.7 1.4 %collective-permute-done.3.refs_2_ = bf16[256,512]{1,0:T(8,128)(2,1)S(1)} collective-permute-done((bf16[256,512]{1,0:T(8,128)(2,1)}, bf16[256,512]{1,0:T(8,128)(2,1)S(1)}, u32[]{:S(2)}, u32[]{:S(2)}) %collective-permute-start.3) | collective-permute-done | bytes 262176 | tf_op jit(solution)/shard_map/ppermute | solution.py:69
  11.1 0.0 collective-permute-start.5
  11.1 1.2 %shard_map.125 = (f32[4,672,512]{2,1,0:T(8,128)S(1)}, f32[2,336,256]{2,1,0:T(8,128)S(1)}) custom-call(s32[1]{0:T(128)} %bitcast.tile_ref, f32[4,672,512]{2,1,0:T(8,128)S(1)} %get-tuple-element.11.refs_0_.first_ref, f32[2,336,256]{2,1,0:T(8,128)S(1)} %get-tuple-element.13.refs_1_, bf16[256,512]{1,0:T(8,128)(2,1)S(1)} %collective-permute-done.3.refs_2_, ...), custom_call_target="tpu_custom_call" | custom-call | flops 5284823040 | tf_op jit(solution)/shard_map/pallas_call | solution.py:391
  12.3 0.3 %collective-permute-done.5.strip_ref = bf16[256,512]{1,0:T(8,128)(2,1)S(1)} collective-permute-done((bf16[256,512]{1,0:T(8,128)(2,1)S(1)}, bf16[256,512]{1,0:T(8,128)(2,1)S(1)}, u32[]{:S(2)}, u32[]{:S(2)}) %collective-permute-start.5) | collective-permute-done | bytes 262176 | tf_op jit(solution)/shard_map/ppermute | solution.py:69
  12.6 1.9 %shard_map.126.refs_1_ = f32[2,4,336,256]{3,2,1,0:T(8,128)S(1)} custom-call(s32[1]{0:T(128)} %bitcast.tile_ref, f32[4,672,512]{2,1,0:T(8,128)S(1)} %get-tuple-element.11.refs_0_.first_ref, f32[4,672,512]{2,1,0:T(8,128)S(1)} %get-tuple-element.15.second_ref, f32[2,336,256]{2,1,0:T(8,128)S(1)} %get-tuple-element.16.previous_ref, ...), custom_call_target="tpu_custom_call" | custom-call | flops 2113929216 | tf_op jit(solution)/shard_map/pallas_call | solution.py:391
  14.6 0.0 collective-permute-done.1.refs_0_
  14.6 1.9 %shard_map.127 = bf16[16,1,32,128]{3,2,1,0:T(8,128)(2,1)S(1)} custom-call(s32[1]{0:T(128)} %bitcast.tile_ref, bf16[1,192,384]{2,1,0:T(8,128)(2,1)S(1)} %collective-permute-done.1.refs_0_, f32[2,4,336,256]{3,2,1,0:T(8,128)S(1)} %shard_map.126.refs_1_, f32[1,672,512]{2,1,0:T(8,128)S(1)} %get-tuple-element.18.refs_2_, f32[8,384]{1,0:T(8,128)S(1)} %get-tuple-element.19.refs_3_, ...), custom_call_target="tpu_custom_call" | custom-call | tf_op jit(solution)/shard_map/pallas_call | solution.py:391
  16.5 13.9 %all_to_all.5 = bf16[16,1,32,128]{3,2,1,0:T(8,128)(2,1)S(1)} all-to-all(bf16[16,1,32,128]{3,2,1,0:T(8,128)(2,1)S(1)} %shard_map.127), channel_id=1, replica_groups={{0,1,2,3,4,5,6,7,8,9,10,11,12,13,14,15},{16,17,18,19,20,21,22,23,24,25,..., dimensions={0} | all-to-all | bytes 262144 | tf_op jit(solution)/shard_map/all_to_all | solution.py:508
  30.5 0.6 %rsqrt_multiply_fusion = (f32[32,128]{1,0:T(8,128)}, f32[32,128]{1,0:T(8,128)}) fusion(f32[32,128]{1,0:T(8,128)S(1)} %get-tuple-element.21, f32[32,128]{1,0:T(8,128)S(1)} %get-tuple-element.20, bf16[32,128]{1,0:T(8,128)(2,1)S(1)} %reduce_max.14), kind=kLoop, calls=%fused_computation.3 | loop fusion | flops 32768 | bytes 73728 | tf_op jit(solution)/shard_map/div | solution.py:515
  (18 shorter events, 0.1 us)
Async XLA Ops:
  0.6 7.3 %collective-permute-start.2 = (bf16[256,512]{1,0:T(8,128)(2,1)}, bf16[256,512]{1,0:T(8,128)(2,1)S(1)}, u32[]{:S(2)}, u32[]{:S(2)}) collective-permute-start(bf16[256,512]{1,0:T(8,128)(2,1)} %strip_a.1), channel_id=1, source_target_pairs={{0,8},{8,0},{16,24},{24,16},{1,9},{9,1},{17,25},{25,17},{2,10},{10... | collective-permute-start | bytes 786440 | tf_op jit(solution)/shard_map/ppermute | solution.py:69
  1.1 9.9 %collective-permute-start.3 = (bf16[256,512]{1,0:T(8,128)(2,1)}, bf16[256,512]{1,0:T(8,128)(2,1)S(1)}, u32[]{:S(2)}, u32[]{:S(2)}) collective-permute-start(bf16[256,512]{1,0:T(8,128)(2,1)} %strip_a.1), channel_id=1, source_target_pairs={{0,16},{8,24},{16,0},{24,8},{1,17},{9,25},{17,1},{25,9},{2,18},{10... | collective-permute-start | bytes 786440 | tf_op jit(solution)/shard_map/ppermute | solution.py:69
  3.7 1.2 %collective-permute-start.4 = (s32[1]{0:T(128)}, s32[1]{0:T(128)}, u32[]{:S(2)}, u32[]{:S(2)}) collective-permute-start(s32[1]{0:T(128)} %param.14), channel_id=1, source_target_pairs={{0,8},{8,0},{16,24},{24,16},{1,9},{9,1},{17,25},{25,17},{2,10},{10... | collective-permute-start | bytes 20 | tf_op jit(solution)/shard_map/ppermute | solution.py:69
  3.9 3.6 %collective-permute-start = (bf16[2,96,384]{2,1,0:T(8,128)(2,1)}, bf16[2,96,384]{2,1,0:T(8,128)(2,1)S(1)}, u32[]{:S(2)}, u32[]{:S(2)}) collective-permute-start(bf16[2,96,384]{2,1,0:T(8,128)(2,1)} %tpl_a.1), channel_id=1, source_target_pairs={{0,8},{8,0},{16,24},{24,16},{1,9},{9,1},{17,25},{25,17},{2,10},{10... | collective-permute-start | bytes 442376 | tf_op jit(solution)/shard_map/ppermute | solution.py:69
  4.9 0.7 %copy-start.9 = (f32[4]{0:T(128)S(1)}, f32[4]{0:T(128)}, u32[]{:S(2)}) copy-start(f32[4]{0:T(128)} %defocus_ref.1) | copy-start | bytes 52
  5.6 1.9 %copy-start.6 = (bf16[2,96,384]{2,1,0:T(8,128)(2,1)S(1)}, bf16[2,96,384]{2,1,0:T(8,128)(2,1)}, u32[]{:S(2)}) copy-start(bf16[2,96,384]{2,1,0:T(8,128)(2,1)} %tpl_a.1) | copy-start | bytes 442372
  5.6 2.3 %copy-start = (bf16[512,512]{1,0:T(8,128)(2,1)S(1)}, bf16[512,512]{1,0:T(8,128)(2,1)}, u32[]{:S(2)}) copy-start(bf16[512,512]{1,0:T(8,128)(2,1)} %constant.30.clone.col_ref.refs_3_.refs_4_) | copy-start | bytes 1572868
  5.6 2.3 %copy-start.1 = (bf16[672,640]{1,0:T(8,128)(2,1)S(1)}, bf16[672,640]{1,0:T(8,128)(2,1)}, u32[]{:S(2)}) copy-start(bf16[672,640]{1,0:T(8,128)(2,1)} %constant.31.clone.row_ref.refs_4_) | copy-start | bytes 2580484
  5.6 2.3 %copy-start.2 = (bf16[2,672,192]{2,1,0:T(8,128)(2,1)S(1)}, bf16[2,672,192]{2,1,0:T(8,128)(2,1)}, u32[]{:S(2)}) copy-start(bf16[2,672,192]{2,1,0:T(8,128)(2,1)} %constant.32.clone.deep_ref.refs_5_) | copy-start | bytes 1548292
  5.6 2.3 %copy-start.5 = (bf16[256,512]{1,0:T(8,128)(2,1)S(1)}, bf16[256,512]{1,0:T(8,128)(2,1)}, u32[]{:S(2)}) copy-start(bf16[256,512]{1,0:T(8,128)(2,1)} %strip_a.1) | copy-start | bytes 786436
  7.6 7.0 %collective-permute-start.1 = (bf16[1,192,384]{2,1,0:T(8,128)(2,1)S(1)}, bf16[1,192,384]{2,1,0:T(8,128)(2,1)S(1)}, u32[]{:S(2)}, u32[]{:S(2)}) collective-permute-start(bf16[1,192,384]{2,1,0:T(8,128)(2,1)S(1)} %shard_map.122.raw_ref), channel_id=1, source_target_pairs={{0,16},{8,24},{16,0},{24,8},{1,17},{9,25},{17,1},{25,9},{2,18},{10... | collective-permute-start | bytes 442376 | tf_op jit(solution)/shard_map/ppermute | solution.py:69
  11.1 1.5 %collective-permute-start.5 = (bf16[256,512]{1,0:T(8,128)(2,1)S(1)}, bf16[256,512]{1,0:T(8,128)(2,1)S(1)}, u32[]{:S(2)}, u32[]{:S(2)}) collective-permute-start(bf16[256,512]{1,0:T(8,128)(2,1)S(1)} %collective-permute-done.3.refs_2_), channel_id=1, source_target_pairs={{0,8},{8,0},{16,24},{24,16},{1,9},{9,1},{17,25},{25,17},{2,10},{10... | collective-permute-start | bytes 786440 | tf_op jit(solution)/shard_map/ppermute | solution.py:69
  12.6 2.0 %copy-start.3 = (bf16[256,768]{1,0:T(8,128)(2,1)S(1)}, bf16[256,768]{1,0:T(8,128)(2,1)}, u32[]{:S(2)}) copy-start(bf16[256,768]{1,0:T(8,128)(2,1)} %constant.34.clone.refs_7_) | copy-start | bytes 1179652
  12.6 2.0 %copy-start.4 = (f32[672,1]{1,0:T(8,128)S(1)}, f32[672,1]{1,0:T(8,128)}, u32[]{:S(2)}) copy-start(f32[672,1]{1,0:T(8,128)} %constant.35.clone.refs_8_) | copy-start | bytes 8068
  12.6 2.0 %copy-start.7 = (bf16[512,128]{1,0:T(8,128)(2,1)S(1)}, bf16[512,128]{1,0:T(8,128)(2,1)}, u32[]{:S(2)}) copy-start(bf16[512,128]{1,0:T(8,128)(2,1)} %constant.33.clone.refs_6_) | copy-start | bytes 393220
  12.6 2.0 %copy-start.8 = (f32[1,512]{1,0:T(1,128)S(1)}, f32[1,512]{1,0:T(1,128)}, u32[]{:S(2)}) copy-start(f32[1,512]{1,0:T(1,128)} %constant.36.clone.refs_9_) | copy-start | bytes 6148

commit v5 on v4

--- a/solution.py
+++ b/solution.py
@@ -152,21 +152,28 @@
 
 def ctf_kernel(half, width_rows, tile_ref, group_a, group_b, defocus_ref, ctf_ref):
     padded = ctf_ref.shape[2]
-    u = lax.broadcasted_iota(jnp.int32, (8, round_up(padded, 128)), 1).astype(jnp.float32) / width_rows
-    column = lax.broadcasted_iota(jnp.int32, (8, half), 1)
-    wrapped = (lax.broadcasted_iota(jnp.int32, (8, half), 0) == 1) & (column == 0)
-    v = jnp.where(wrapped, half, column).astype(jnp.float32) / (2 * half)
+    shape_u, shape_v = (8, round_up(padded, 128)), (8, half)
+    turns = []
     for k in range(2):
         group = jnp.where((tile_ref[0] & 1) == k, group_a[0], group_b[0])
-        turn = jnp.float32(math.pi) * defocus_ref[group]
-        phase_u, phase_v = turn * (u * u) + 0.07, turn * (v * v)
-        sin_u, cos_u = jnp.sin(phase_u).T[:padded, :1], jnp.cos(phase_u).T[:padded, :1]
-        sin_v, cos_v = jnp.sin(phase_v), jnp.cos(phase_v)
+        turns.append(jnp.float32(math.pi) * defocus_ref[group])
+
+    def turn(shape):
+        return jnp.where(lax.broadcasted_iota(jnp.int32, shape, 0) < 2, turns[0], turns[1])
+
+    u = lax.broadcasted_iota(jnp.int32, shape_u, 1).astype(jnp.float32) / width_rows
+    column = lax.broadcasted_iota(jnp.int32, shape_v, 1)
+    wrapped = ((lax.broadcasted_iota(jnp.int32, shape_v, 0) & 1) == 1) & (column == 0)
+    v = jnp.where(wrapped, half, column).astype(jnp.float32) / (2 * half)
+    phase_u, phase_v = turn(shape_u) * (u * u) + 0.07, turn(shape_v) * (v * v)
+    sin_u, cos_u = jnp.sin(phase_u).T, jnp.cos(phase_u).T
+    sin_v, cos_v = jnp.sin(phase_v), jnp.cos(phase_v)
+    for k in range(2):
         for r in range(0, padded, CHUNK):
-            up = slice(r, r + CHUNK)
+            up, at = slice(r, r + CHUNK), slice(2 * k, 2 * k + 1)
             for side in range(2):
-                row = slice(side, side + 1)
-                ctf_ref[k, side, up] = -(sin_u[up] * cos_v[row] + cos_u[up] * sin_v[row])
+                row = slice(2 * k + side, 2 * k + side + 1)
+                ctf_ref[k, side, up] = -(sin_u[up, at] * cos_v[row] + cos_u[up, at] * sin_v[row])
 
 
 def pair_kernel(tile_ref, tpl_a, tpl_b, raw_ref, order_ref):
@@ -183,12 +190,10 @@
     return jnp.sum(wide, axis=0, keepdims=True), jnp.sum(wide * wide, axis=0, keepdims=True)
 
 
-def early_kernel(tile_ref, strip_a, strip_b, raw_ref, col_ref, row_ref, deep_ref, *outs):
-    tile = tile_ref[0]
-    bit = tile & 1
-    four = len(outs) == 5
-    column_ref = outs[4] if four else outs[0]
-    shape_ref, moment_ref = outs[2:4]
+def early_kernel(tile_ref, strip_a, strip_b, col_ref, row_ref, *outs):
+    bit = tile_ref[0] & 1
+    four = len(outs) == 3
+    column_ref = outs[2] if four else outs[0]
     for j, strip in enumerate((strip_a, strip_b)):
         start = pl.multiple_of((bit ^ j) * STRIP, STRIP)
         column_ref[pl.ds(start, STRIP), :] = dot(strip[...], col_ref[...]).astype(jnp.bfloat16)
@@ -197,11 +202,14 @@
     else:
         outs[1][0] = dot(row_ref[:, : 2 * STRIP], column_ref[...])
         outs[1][1] = dot(row_ref[:, :STRIP], column_ref[STRIP:, :])
+
+
+def shape_kernel(tile_ref, raw_ref, col_ref, deep_ref, shape_ref, moment_ref):
     for index in range(shape_ref.shape[0]):
         for k, moment in enumerate(moments(raw_ref[index])):
             moment_ref[2 * index + k : 2 * index + k + 1, :] = moment
         columns = dot(raw_ref[index], col_ref[:TS, :]).astype(jnp.bfloat16)
-        shape_ref[index] = dot(deep_ref[tile >> 1], columns)
+        shape_ref[index] = dot(deep_ref[tile_ref[0] >> 1], columns)
 
 
 def by_case(tile, body):
@@ -423,7 +431,6 @@
         jax.ShapeDtypeStruct((mine, 2 * depth, TS), bf16),
         None,
     )
-    pieces = spread_out(raw, "tile")
     ctf = on_device(
         functools.partial(ctf_kernel, half, width_rows),
         [tile, group_of_tile, swapped(group_of_tile, "tile", 1), defocus],
@@ -432,24 +439,27 @@
         jax.ShapeDtypeStruct((2, 2, *plane), f32),
         20 * pass_flops,
     )
-    early_in = [micrograph, swapped(micrograph, "tile", 1), raw, col, row, deep]
-    early_out = [
+    early_in = [micrograph, swapped(micrograph, "tile", 1), col, row]
+    shape_out = (
         jax.ShapeDtypeStruct((mine, *quads), f32),
         jax.ShapeDtypeStruct((round_up(2 * mine, 8), TS), f32),
-    ]
+    )
     columns_out = jax.ShapeDtypeStruct((2 * STRIP, width_cols), bf16)
     all_quads, power_out = jax.ShapeDtypeStruct((4, *quads), f32), jax.ShapeDtypeStruct((2, *plane), f32)
     weighted_out = jax.ShapeDtypeStruct((2, 4, *plane), f32)
     if count == 4:
-        quads_0, power, shape, moment = on_device(
+        shape, moment = on_device(shape_kernel, [tile], [raw, col, deep], [], shape_out, None)
+        early_in[0], shape = lax.optimization_barrier((early_in[0], shape))
+        pieces = spread_out(raw, "tile")
+        quads_0, power = on_device(
             early_kernel,
             [tile],
             early_in,
             [pltpu.VMEM(columns_out.shape, bf16)],
-            (all_quads, power_out, *early_out),
+            (all_quads, power_out),
             None,
         )
-        strips, power, ctf = lax.optimization_barrier((strips, power, ctf))
+        strips, power, ctf, shape = lax.optimization_barrier((strips, power, ctf, shape))
         block = pltpu.VMEM((STRIP, width_cols), bf16)
         quads_1, power = on_device(
             functools.partial(stage_kernel, 1),
@@ -468,14 +478,16 @@
             12 * pass_flops,
         )
     else:
-        column, partial, shape, moment = on_device(
+        column, partial = on_device(
             early_kernel,
             [tile],
             early_in,
             [],
-            (columns_out, jax.ShapeDtypeStruct((2, *quads), f32), *early_out),
+            (columns_out, jax.ShapeDtypeStruct((2, *quads), f32)),
             None,
         )
+        pieces = spread_out(raw, "tile")
+        shape, moment = on_device(shape_kernel, [tile], [raw, col, deep], [], shape_out, None)
         strips, column, ctf = lax.optimization_barrier((strips, column, ctf))
         part, power = on_device(
             functools.partial(other_kernel, count),

time: 31.3 us -> 30.2 us (0.965)
  waiting for transfers between devices: 1.82 us -> 1.34 us
  blocking collectives: 13.9 us -> 13.5 us
    ppermute x6, waiting for transfers between devices: 1.82 us -> 1.34 us  [swapped(): lax.ppermute(value, axis, [(source, source ^ step) for source in range(co...]
    all_to_all x1, blocking collectives: 13.9 us -> 13.5 us  [local(): lax.all_to_all(scores, ('tile', 'orient'), split_axis=0, concat_axis=0, t...]
    pallas_call x6 -> x7, Pallas kernels: 8.66 us -> 8.56 us  [on_device(): pl.pallas_call(kernel, out_shape=result, in_specs=[smem] * len(scalars) +...]
  transfers between devices with their start and end apart: 6 -> 6, of which waited for: 3 -> 4; matrix products, arithmetic and copies ran while one was open for 0% -> 0% of each run, Pallas kernels for 22% -> 22%
where the time goes in v5:
time: 30.2 us; the launch traced here: 30 us
  blocking collectives  13.5 us (45%)
  Pallas kernels  8.56 us (28%)
  starting transfers between devices  3.83 us (13%)
  between operations  1.41 us (5%)
  waiting for transfers between devices  1.34 us (4%)
  local copies, waits for them, and re-layouts  0.69 us (2%)
  other arithmetic  0.69 us (2%)
    all_to_all x1, blocking collectives, local(): lax.all_to_all(scores, ('tile', 'orient'), split_axis=0, concat_axis=0, t...  13.5 us
    pallas_call x7, Pallas kernels, on_device(): pl.pallas_call(kernel, out_shape=result, in_specs=[smem] * len(scalars) +...  8.56 us
    ppermute x6, starting transfers between devices, swapped(): lax.ppermute(value, axis, [(source, source ^ step) for source in range(co...  3.83 us
    ppermute x6, waiting for transfers between devices, swapped(): lax.ppermute(value, axis, [(source, source ^ step) for source in range(co...  1.34 us
    unnamed x20, local copies, waits for them, and re-layouts  0.69 us
    div x1, other arithmetic, local(): return (best, (best - score_mean) / jnp.sqrt(score_var + 1e-05))  0.62 us
  transfers between devices with their start and end apart: 6, of which 4 were waited for; matrix products, arithmetic and copies ran while one was open for 0% of the time, Pallas kernels for 22%

profile of v5, /device:TPU:0, one launch (start us, length us, event | category | flops | bytes accessed | tf_op | source)
XLA Modules:
  0.0 30.0 jit_solution(12363110879780479774)
XLA Ops:
  0.6 3.0 %collective-permute-start.3 = (bf16[256,512]{1,0:T(8,128)(2,1)}, bf16[256,512]{1,0:T(8,128)(2,1)S(1)}, u32[]{:S(2)}, u32[]{:S(2)}) collective-permute-start(bf16[256,512]{1,0:T(8,128)(2,1)} %strip_a), channel_id=1, source_target_pairs={{0,16},{8,24},{16,0},{24,8},{1,17},{9,25},{17,1},{25,9},{2,18},{10... | collective-permute-start | bytes 786440 | tf_op jit(solution)/shard_map/ppermute | solution.py:69
  3.6 0.0 collective-permute-start.2
  3.6 0.5 %collective-permute-start.4 = (s32[1]{0:T(128)}, s32[1]{0:T(128)}, u32[]{:S(2)}, u32[]{:S(2)}) collective-permute-start(s32[1]{0:T(128)} %param.14), channel_id=1, source_target_pairs={{0,8},{8,0},{16,24},{24,16},{1,9},{9,1},{17,25},{25,17},{2,10},{10... | collective-permute-start | bytes 20 | tf_op jit(solution)/shard_map/ppermute | solution.py:69
  4.1 0.0 collective-permute-start
  4.8 0.4 %collective-permute-done.4.group_b = s32[1]{0:T(128)} collective-permute-done((s32[1]{0:T(128)}, s32[1]{0:T(128)}, u32[]{:S(2)}, u32[]{:S(2)}) %collective-permute-start.4) | collective-permute-done | bytes 36 | tf_op jit(solution)/shard_map/ppermute | solution.py:69
  5.2 0.7 %copy-done.9 = f32[4]{0:T(128)S(1)} copy-done((f32[4]{0:T(128)S(1)}, f32[4]{0:T(128)}, u32[]{:S(2)}) %copy-start.9) | copy-done | bytes 40
  5.9 0.0 copy-start.5
  5.9 1.8 %shard_map.125.ctf_ref = f32[2,2,336,256]{3,2,1,0:T(8,128)S(1)} custom-call(s32[1]{0:T(128)} %bitcast.tile_ref, s32[1]{0:T(128)S(6)} %copy.13.group_a, s32[1]{0:T(128)} %collective-permute-done.4.group_b, f32[4]{0:T(128)S(1)} %copy-done.9), custom_call_target="tpu_custom_call" | custom-call | flops 3523215360 | tf_op jit(solution)/shard_map/pallas_call | solution.py:399
  7.7 0.0 collective-permute-done.tpl_b
  7.8 0.3 %collective-permute-start.1 = (bf16[1,192,384]{2,1,0:T(8,128)(2,1)S(1)}, bf16[1,192,384]{2,1,0:T(8,128)(2,1)S(1)}, u32[]{:S(2)}, u32[]{:S(2)}) collective-permute-start(bf16[1,192,384]{2,1,0:T(8,128)(2,1)S(1)} %shard_map.122.raw_ref), channel_id=1, source_target_pairs={{0,16},{8,24},{16,0},{24,8},{1,17},{9,25},{17,1},{25,9},{2,18},{10... | collective-permute-start | bytes 442376 | tf_op jit(solution)/shard_map/ppermute | solution.py:69
  8.1 0.0 copy-done.2
  8.1 0.6 %shard_map.123 = (f32[1,672,512]{2,1,0:T(8,128)S(1)}, f32[8,384]{1,0:T(8,128)S(1)}) custom-call(s32[1]{0:T(128)} %bitcast.tile_ref, bf16[1,192,384]{2,1,0:T(8,128)(2,1)S(1)} %shard_map.122.raw_ref, bf16[512,512]{1,0:T(8,128)(2,1)S(1)} %copy-done, bf16[2,672,192]{2,1,0:T(8,128)(2,1)S(1)} %copy-done.2), custom_call_target="tpu_custom_call" | custom-call | tf_op jit(solution)/shard_map/pallas_call | solution.py:399
  8.7 0.0 collective-permute-done.2.strip_b
  8.7 1.1 %shard_map.124 = (f32[4,672,512]{2,1,0:T(8,128)S(1)}, f32[2,336,256]{2,1,0:T(8,128)S(1)}) custom-call(s32[1]{0:T(128)} %bitcast.tile_ref, bf16[256,512]{1,0:T(8,128)(2,1)S(1)} %copy-done.5, bf16[256,512]{1,0:T(8,128)(2,1)S(1)} %collective-permute-done.2.strip_b, bf16[512,512]{1,0:T(8,128)(2,1)S(1)} %copy-done, bf16[672,640]{1,0:T(8,128)(2,1)S(1)} %copy-done.1), custom_call_target="tpu_custom_call" | custom-call | tf_op jit(solution)/shard_map/pallas_call | solution.py:399
  9.8 0.5 %collective-permute-done.3.refs_2_ = bf16[256,512]{1,0:T(8,128)(2,1)S(1)} collective-permute-done((bf16[256,512]{1,0:T(8,128)(2,1)}, bf16[256,512]{1,0:T(8,128)(2,1)S(1)}, u32[]{:S(2)}, u32[]{:S(2)}) %collective-permute-start.3) | collective-permute-done | bytes 262176 | tf_op jit(solution)/shard_map/ppermute | solution.py:69
  10.3 0.0 collective-permute-start.5
  10.3 1.2 %shard_map.126 = (f32[4,672,512]{2,1,0:T(8,128)S(1)}, f32[2,336,256]{2,1,0:T(8,128)S(1)}) custom-call(s32[1]{0:T(128)} %bitcast.tile_ref, f32[4,672,512]{2,1,0:T(8,128)S(1)} %get-tuple-element.16.refs_0_.first_ref, f32[2,336,256]{2,1,0:T(8,128)S(1)} %get-tuple-element.19.refs_1_, bf16[256,512]{1,0:T(8,128)(2,1)S(1)} %collective-permute-done.3.refs_2_, ...), custom_call_target="tpu_custom_call" | custom-call | flops 5284823040 | tf_op jit(solution)/shard_map/pallas_call | solution.py:399
  11.5 0.4 %collective-permute-done.5.strip_ref = bf16[256,512]{1,0:T(8,128)(2,1)S(1)} collective-permute-done((bf16[256,512]{1,0:T(8,128)(2,1)S(1)}, bf16[256,512]{1,0:T(8,128)(2,1)S(1)}, u32[]{:S(2)}, u32[]{:S(2)}) %collective-permute-start.5) | collective-permute-done | bytes 262176 | tf_op jit(solution)/shard_map/ppermute | solution.py:69
  11.9 1.9 %shard_map.127.refs_1_ = f32[2,4,336,256]{3,2,1,0:T(8,128)S(1)} custom-call(s32[1]{0:T(128)} %bitcast.tile_ref, f32[4,672,512]{2,1,0:T(8,128)S(1)} %get-tuple-element.16.refs_0_.first_ref, f32[4,672,512]{2,1,0:T(8,128)S(1)} %get-tuple-element.21.second_ref, f32[2,336,256]{2,1,0:T(8,128)S(1)} %get-tuple-element.22.previous_ref, ...), custom_call_target="tpu_custom_call" | custom-call | flops 2113929216 | tf_op jit(solution)/shard_map/pallas_call | solution.py:399
  13.8 0.1 collective-permute-done.1.refs_0_
  13.9 0.0 copy-done.3
  13.9 1.9 %shard_map.128 = bf16[16,1,32,128]{3,2,1,0:T(8,128)(2,1)S(1)} custom-call(s32[1]{0:T(128)} %bitcast.tile_ref, bf16[1,192,384]{2,1,0:T(8,128)(2,1)S(1)} %collective-permute-done.1.refs_0_, f32[2,4,336,256]{3,2,1,0:T(8,128)S(1)} %shard_map.127.refs_1_, f32[1,672,512]{2,1,0:T(8,128)S(1)} %get-tuple-element.24.refs_2_, f32[8,384]{1,0:T(8,128)S(1)} %get-tuple-element.25.refs_3_, ...), custom_call_target="tpu_custom_call" | custom-call | tf_op jit(solution)/shard_map/pallas_call | solution.py:399
  15.8 13.5 %all_to_all.5 = bf16[16,1,32,128]{3,2,1,0:T(8,128)(2,1)S(1)} all-to-all(bf16[16,1,32,128]{3,2,1,0:T(8,128)(2,1)S(1)} %shard_map.128), channel_id=1, replica_groups={{0,1,2,3,4,5,6,7,8,9,10,11,12,13,14,15},{16,17,18,19,20,21,22,23,24,25,..., dimensions={0} | all-to-all | bytes 262144 | tf_op jit(solution)/shard_map/all_to_all | solution.py:520
  29.4 0.6 %rsqrt_multiply_fusion = (f32[32,128]{1,0:T(8,128)}, f32[32,128]{1,0:T(8,128)}) fusion(f32[32,128]{1,0:T(8,128)S(1)} %get-tuple-element.27, f32[32,128]{1,0:T(8,128)S(1)} %get-tuple-element.26, bf16[32,128]{1,0:T(8,128)(2,1)S(1)} %reduce_max.14), kind=kLoop, calls=%fused_computation.3 | loop fusion | flops 32768 | bytes 73728 | tf_op jit(solution)/shard_map/div | solution.py:527
  (19 shorter events, 0.1 us)
Async XLA Ops:
  0.6 9.7 %collective-permute-start.3 = (bf16[256,512]{1,0:T(8,128)(2,1)}, bf16[256,512]{1,0:T(8,128)(2,1)S(1)}, u32[]{:S(2)}, u32[]{:S(2)}) collective-permute-start(bf16[256,512]{1,0:T(8,128)(2,1)} %strip_a), channel_id=1, source_target_pairs={{0,16},{8,24},{16,0},{24,8},{1,17},{9,25},{17,1},{25,9},{2,18},{10... | collective-permute-start | bytes 786440 | tf_op jit(solution)/shard_map/ppermute | solution.py:69
  3.6 5.0 %collective-permute-start.2 = (bf16[256,512]{1,0:T(8,128)(2,1)}, bf16[256,512]{1,0:T(8,128)(2,1)S(1)}, u32[]{:S(2)}, u32[]{:S(2)}) collective-permute-start(bf16[256,512]{1,0:T(8,128)(2,1)} %strip_a), channel_id=1, source_target_pairs={{0,8},{8,0},{16,24},{24,16},{1,9},{9,1},{17,25},{25,17},{2,10},{10... | collective-permute-start | bytes 786440 | tf_op jit(solution)/shard_map/ppermute | solution.py:69
  3.6 1.6 %collective-permute-start.4 = (s32[1]{0:T(128)}, s32[1]{0:T(128)}, u32[]{:S(2)}, u32[]{:S(2)}) collective-permute-start(s32[1]{0:T(128)} %param.14), channel_id=1, source_target_pairs={{0,8},{8,0},{16,24},{24,16},{1,9},{9,1},{17,25},{25,17},{2,10},{10... | collective-permute-start | bytes 20 | tf_op jit(solution)/shard_map/ppermute | solution.py:69
  4.1 3.6 %collective-permute-start = (bf16[2,96,384]{2,1,0:T(8,128)(2,1)}, bf16[2,96,384]{2,1,0:T(8,128)(2,1)S(1)}, u32[]{:S(2)}, u32[]{:S(2)}) collective-permute-start(bf16[2,96,384]{2,1,0:T(8,128)(2,1)} %tpl_a.1), channel_id=1, source_target_pairs={{0,8},{8,0},{16,24},{24,16},{1,9},{9,1},{17,25},{25,17},{2,10},{10... | collective-permute-start | bytes 442376 | tf_op jit(solution)/shard_map/ppermute | solution.py:69
  5.2 0.7 %copy-start.9 = (f32[4]{0:T(128)S(1)}, f32[4]{0:T(128)}, u32[]{:S(2)}) copy-start(f32[4]{0:T(128)} %defocus_ref.1) | copy-start | bytes 52
  5.9 1.8 %copy-start.6 = (bf16[2,96,384]{2,1,0:T(8,128)(2,1)S(1)}, bf16[2,96,384]{2,1,0:T(8,128)(2,1)}, u32[]{:S(2)}) copy-start(bf16[2,96,384]{2,1,0:T(8,128)(2,1)} %tpl_a.1) | copy-start | bytes 442372
  5.9 2.2 %copy-start = (bf16[512,512]{1,0:T(8,128)(2,1)S(1)}, bf16[512,512]{1,0:T(8,128)(2,1)}, u32[]{:S(2)}) copy-start(bf16[512,512]{1,0:T(8,128)(2,1)} %constant.30.clone.col_ref.refs_3_.refs_4_) | copy-start | bytes 1572868
  5.9 2.2 %copy-start.2 = (bf16[2,672,192]{2,1,0:T(8,128)(2,1)S(1)}, bf16[2,672,192]{2,1,0:T(8,128)(2,1)}, u32[]{:S(2)}) copy-start(bf16[2,672,192]{2,1,0:T(8,128)(2,1)} %constant.31.clone.deep_ref.refs_5_) | copy-start | bytes 1548292
  5.9 2.8 %copy-start.1 = (bf16[672,640]{1,0:T(8,128)(2,1)S(1)}, bf16[672,640]{1,0:T(8,128)(2,1)}, u32[]{:S(2)}) copy-start(bf16[672,640]{1,0:T(8,128)(2,1)} %constant.32.clone.row_ref.refs_4_) | copy-start | bytes 2580484
  5.9 2.8 %copy-start.5 = (bf16[256,512]{1,0:T(8,128)(2,1)S(1)}, bf16[256,512]{1,0:T(8,128)(2,1)}, u32[]{:S(2)}) copy-start(bf16[256,512]{1,0:T(8,128)(2,1)} %strip_a) | copy-start | bytes 786436
  7.8 6.1 %collective-permute-start.1 = (bf16[1,192,384]{2,1,0:T(8,128)(2,1)S(1)}, bf16[1,192,384]{2,1,0:T(8,128)(2,1)S(1)}, u32[]{:S(2)}, u32[]{:S(2)}) collective-permute-start(bf16[1,192,384]{2,1,0:T(8,128)(2,1)S(1)} %shard_map.122.raw_ref), channel_id=1, source_target_pairs={{0,16},{8,24},{16,0},{24,8},{1,17},{9,25},{17,1},{25,9},{2,18},{10... | collective-permute-start | bytes 442376 | tf_op jit(solution)/shard_map/ppermute | solution.py:69
  10.3 1.5 %collective-permute-start.5 = (bf16[256,512]{1,0:T(8,128)(2,1)S(1)}, bf16[256,512]{1,0:T(8,128)(2,1)S(1)}, u32[]{:S(2)}, u32[]{:S(2)}) collective-permute-start(bf16[256,512]{1,0:T(8,128)(2,1)S(1)} %collective-permute-done.3.refs_2_), channel_id=1, source_target_pairs={{0,8},{8,0},{16,24},{24,16},{1,9},{9,1},{17,25},{25,17},{2,10},{10... | collective-permute-start | bytes 786440 | tf_op jit(solution)/shard_map/ppermute | solution.py:69
  11.8 2.1 %copy-start.3 = (bf16[256,768]{1,0:T(8,128)(2,1)S(1)}, bf16[256,768]{1,0:T(8,128)(2,1)}, u32[]{:S(2)}) copy-start(bf16[256,768]{1,0:T(8,128)(2,1)} %constant.34.clone.refs_7_) | copy-start | bytes 1179652
  11.8 2.1 %copy-start.4 = (f32[672,1]{1,0:T(8,128)S(1)}, f32[672,1]{1,0:T(8,128)}, u32[]{:S(2)}) copy-start(f32[672,1]{1,0:T(8,128)} %constant.35.clone.refs_8_) | copy-start | bytes 8068
  11.9 2.1 %copy-start.7 = (bf16[512,128]{1,0:T(8,128)(2,1)S(1)}, bf16[512,128]{1,0:T(8,128)(2,1)}, u32[]{:S(2)}) copy-start(bf16[512,128]{1,0:T(8,128)(2,1)} %constant.33.clone.refs_6_) | copy-start | bytes 393220
  11.9 2.1 %copy-start.8 = (f32[1,512]{1,0:T(1,128)S(1)}, f32[1,512]{1,0:T(1,128)}, u32[]{:S(2)}) copy-start(f32[1,512]{1,0:T(1,128)} %constant.36.clone.refs_9_) | copy-start | bytes 6148

commit v6 on v5

--- a/solution.py
+++ b/solution.py
@@ -350,7 +350,7 @@
     score_ref, quad_ref, product_ref = refs[pairs + 8 :]
     padded, half = deep_ref.shape[1] // 2, col_ref.shape[1] // 2
     scale = 1.0 / ((STRIP + TS) * col_ref.shape[0])
-    pieces, mine = score_ref.shape[:2]
+    pieces, mine = 2 * score_ref.shape[0], score_ref.shape[2]
     tile = tile_ref[0]
     tall = product_ref.shape[0] // 2
     for h in range(2):
@@ -391,7 +391,7 @@
             rows_first = dot(out_ref[...], product_ref[:, 2 * half * k : 2 * half * (k + 1)]).astype(jnp.bfloat16)
             score = dot(rows_first, back_ref[...]) * (scale / spread)
             strip = score.reshape(pieces // 2, 2 * STRIP // pieces, OUTC)
-            score_ref[k * (pieces // 2) : (k + 1) * (pieces // 2), index] = strip.astype(jnp.bfloat16)
+            score_ref[:, k, index] = strip.astype(jnp.bfloat16)
 
 
 def on_device(kernel, scalars, operands, scratch, result, cost):
@@ -513,10 +513,14 @@
             pltpu.VMEM(quads, f32),
             pltpu.VMEM((out.shape[1], 2 * width_cols), bf16),
         ],
-        jax.ShapeDtypeStruct((2 * orient_count, mine, STRIP // orient_count, OUTC), bf16),
+        jax.ShapeDtypeStruct((orient_count, 2, mine, STRIP // orient_count, OUTC), bf16),
         None,
     )
-    chips = [[first + k for k in range(2 * orient_count)] for first in range(0, count * orient_count, 2 * orient_count)]
+    scores = scores.reshape(2 * orient_count, *scores.shape[2:])
+    chips = [
+        [(2 * chip + core) * orient_count + orient for orient in range(orient_count) for core in range(2)]
+        for chip in range(count // 2)
+    ]
     received = lax.all_to_all(
         scores, ("tile", "orient"), split_axis=0, concat_axis=0, tiled=True, axis_index_groups=chips
     ).astype(f32)

time: 30.2 us -> 30.4 us (level)
  no operation moved by 1% of the time
where the time goes in v6:
time: 30.4 us; the launch traced here: 30.2 us
  blocking collectives  13.7 us (45%)
  Pallas kernels  8.56 us (28%)
  starting transfers between devices  3.83 us (13%)
  between operations  1.41 us (5%)
  waiting for transfers between devices  1.34 us (4%)
  local copies, waits for them, and re-layouts  0.69 us (2%)
  other arithmetic  0.69 us (2%)
    all_to_all x1, blocking collectives, local(): lax.all_to_all(scores, ('tile', 'orient'), split_axis=0, concat_axis=0, t...  13.7 us
    pallas_call x7, Pallas kernels, on_device(): pl.pallas_call(kernel, out_shape=result, in_specs=[smem] * len(scalars) +...  8.56 us
    ppermute x6, starting transfers between devices, swapped(): lax.ppermute(value, axis, [(source, source ^ step) for source in range(co...  3.83 us
    ppermute x6, waiting for transfers between devices, swapped(): lax.ppermute(value, axis, [(source, source ^ step) for source in range(co...  1.34 us
    unnamed x20, local copies, waits for them, and re-layouts  0.69 us
    div x1, other arithmetic, local(): return (best, (best - score_mean) / jnp.sqrt(score_var + 1e-05))  0.62 us
  transfers between devices with their start and end apart: 6, of which 4 were waited for; matrix products, arithmetic and copies ran while one was open for 0% of the time, Pallas kernels for 22%

profile of v6, /device:TPU:0, one launch (start us, length us, event | category | flops | bytes accessed | tf_op | source)
XLA Modules:
  0.0 30.2 jit_solution(5977894829655315408)
XLA Ops:
  0.6 3.0 %collective-permute-start.3 = (bf16[256,512]{1,0:T(8,128)(2,1)}, bf16[256,512]{1,0:T(8,128)(2,1)S(1)}, u32[]{:S(2)}, u32[]{:S(2)}) collective-permute-start(bf16[256,512]{1,0:T(8,128)(2,1)} %strip_a), channel_id=1, source_target_pairs={{0,16},{8,24},{16,0},{24,8},{1,17},{9,25},{17,1},{25,9},{2,18},{10... | collective-permute-start | bytes 786440 | tf_op jit(solution)/shard_map/ppermute | solution.py:69
  3.6 0.0 collective-permute-start.2
  3.6 0.5 %collective-permute-start.4 = (s32[1]{0:T(128)}, s32[1]{0:T(128)}, u32[]{:S(2)}, u32[]{:S(2)}) collective-permute-start(s32[1]{0:T(128)} %param.14), channel_id=1, source_target_pairs={{0,8},{8,0},{16,24},{24,16},{1,9},{9,1},{17,25},{25,17},{2,10},{10... | collective-permute-start | bytes 20 | tf_op jit(solution)/shard_map/ppermute | solution.py:69
  4.1 0.0 collective-permute-start
  4.8 0.4 %collective-permute-done.4.group_b = s32[1]{0:T(128)} collective-permute-done((s32[1]{0:T(128)}, s32[1]{0:T(128)}, u32[]{:S(2)}, u32[]{:S(2)}) %collective-permute-start.4) | collective-permute-done | bytes 36 | tf_op jit(solution)/shard_map/ppermute | solution.py:69
  5.2 0.7 %copy-done.9 = f32[4]{0:T(128)S(1)} copy-done((f32[4]{0:T(128)S(1)}, f32[4]{0:T(128)}, u32[]{:S(2)}) %copy-start.9) | copy-done | bytes 40
  5.9 0.0 copy-start.5
  5.9 1.8 %shard_map.125.ctf_ref = f32[2,2,336,256]{3,2,1,0:T(8,128)S(1)} custom-call(s32[1]{0:T(128)} %bitcast.tile_ref, s32[1]{0:T(128)S(6)} %copy.14.group_a, s32[1]{0:T(128)} %collective-permute-done.4.group_b, f32[4]{0:T(128)S(1)} %copy-done.9), custom_call_target="tpu_custom_call" | custom-call | flops 3523215360 | tf_op jit(solution)/shard_map/pallas_call | solution.py:399
  7.7 0.0 collective-permute-done.tpl_b
  7.8 0.3 %collective-permute-start.1 = (bf16[1,192,384]{2,1,0:T(8,128)(2,1)S(1)}, bf16[1,192,384]{2,1,0:T(8,128)(2,1)S(1)}, u32[]{:S(2)}, u32[]{:S(2)}) collective-permute-start(bf16[1,192,384]{2,1,0:T(8,128)(2,1)S(1)} %shard_map.122.raw_ref), channel_id=1, source_target_pairs={{0,16},{8,24},{16,0},{24,8},{1,17},{9,25},{17,1},{25,9},{2,18},{10... | collective-permute-start | bytes 442376 | tf_op jit(solution)/shard_map/ppermute | solution.py:69
  8.1 0.0 copy-done.2
  8.1 0.6 %shard_map.123 = (f32[1,672,512]{2,1,0:T(8,128)S(1)}, f32[8,384]{1,0:T(8,128)S(1)}) custom-call(s32[1]{0:T(128)} %bitcast.tile_ref, bf16[1,192,384]{2,1,0:T(8,128)(2,1)S(1)} %shard_map.122.raw_ref, bf16[512,512]{1,0:T(8,128)(2,1)S(1)} %copy-done, bf16[2,672,192]{2,1,0:T(8,128)(2,1)S(1)} %copy-done.2), custom_call_target="tpu_custom_call" | custom-call | tf_op jit(solution)/shard_map/pallas_call | solution.py:399
  8.7 0.0 collective-permute-done.2.strip_b
  8.7 1.1 %shard_map.124 = (f32[4,672,512]{2,1,0:T(8,128)S(1)}, f32[2,336,256]{2,1,0:T(8,128)S(1)}) custom-call(s32[1]{0:T(128)} %bitcast.tile_ref, bf16[256,512]{1,0:T(8,128)(2,1)S(1)} %copy-done.5, bf16[256,512]{1,0:T(8,128)(2,1)S(1)} %collective-permute-done.2.strip_b, bf16[512,512]{1,0:T(8,128)(2,1)S(1)} %copy-done, bf16[672,640]{1,0:T(8,128)(2,1)S(1)} %copy-done.1), custom_call_target="tpu_custom_call" | custom-call | tf_op jit(solution)/shard_map/pallas_call | solution.py:399
  9.8 0.5 %collective-permute-done.3.refs_2_ = bf16[256,512]{1,0:T(8,128)(2,1)S(1)} collective-permute-done((bf16[256,512]{1,0:T(8,128)(2,1)}, bf16[256,512]{1,0:T(8,128)(2,1)S(1)}, u32[]{:S(2)}, u32[]{:S(2)}) %collective-permute-start.3) | collective-permute-done | bytes 262176 | tf_op jit(solution)/shard_map/ppermute | solution.py:69
  10.3 0.0 collective-permute-start.5
  10.3 1.2 %shard_map.126 = (f32[4,672,512]{2,1,0:T(8,128)S(1)}, f32[2,336,256]{2,1,0:T(8,128)S(1)}) custom-call(s32[1]{0:T(128)} %bitcast.tile_ref, f32[4,672,512]{2,1,0:T(8,128)S(1)} %get-tuple-element.16.refs_0_.first_ref, f32[2,336,256]{2,1,0:T(8,128)S(1)} %get-tuple-element.19.refs_1_, bf16[256,512]{1,0:T(8,128)(2,1)S(1)} %collective-permute-done.3.refs_2_, ...), custom_call_target="tpu_custom_call" | custom-call | flops 5284823040 | tf_op jit(solution)/shard_map/pallas_call | solution.py:399
  11.5 0.4 %collective-permute-done.5.strip_ref = bf16[256,512]{1,0:T(8,128)(2,1)S(1)} collective-permute-done((bf16[256,512]{1,0:T(8,128)(2,1)S(1)}, bf16[256,512]{1,0:T(8,128)(2,1)S(1)}, u32[]{:S(2)}, u32[]{:S(2)}) %collective-permute-start.5) | collective-permute-done | bytes 262176 | tf_op jit(solution)/shard_map/ppermute | solution.py:69
  11.9 1.9 %shard_map.127.refs_1_ = f32[2,4,336,256]{3,2,1,0:T(8,128)S(1)} custom-call(s32[1]{0:T(128)} %bitcast.tile_ref, f32[4,672,512]{2,1,0:T(8,128)S(1)} %get-tuple-element.16.refs_0_.first_ref, f32[4,672,512]{2,1,0:T(8,128)S(1)} %get-tuple-element.21.second_ref, f32[2,336,256]{2,1,0:T(8,128)S(1)} %get-tuple-element.22.previous_ref, ...), custom_call_target="tpu_custom_call" | custom-call | flops 2113929216 | tf_op jit(solution)/shard_map/pallas_call | solution.py:399
  13.8 0.1 collective-permute-done.1.refs_0_
  13.9 0.0 copy-done.3
  13.9 1.9 %shard_map.128 = bf16[8,2,1,32,128]{4,3,2,1,0:T(8,128)(2,1)S(1)} custom-call(s32[1]{0:T(128)} %bitcast.tile_ref, bf16[1,192,384]{2,1,0:T(8,128)(2,1)S(1)} %collective-permute-done.1.refs_0_, f32[2,4,336,256]{3,2,1,0:T(8,128)S(1)} %shard_map.127.refs_1_, f32[1,672,512]{2,1,0:T(8,128)S(1)} %get-tuple-element.24.refs_2_, ...), custom_call_target="tpu_custom_call" | custom-call | tf_op jit(solution)/shard_map/pallas_call | solution.py:399
  15.8 13.7 %all_to_all.5 = bf16[16,1,32,128]{3,2,1,0:T(8,128)(2,1)S(1)} all-to-all(bf16[16,1,32,128]{3,2,1,0:T(8,128)(2,1)S(1)} %bitcast.4), channel_id=1, replica_groups={{0,8,1,9,2,10,3,11,4,12,5,13,6,14,7,15},{16,24,17,25,18,26,19,27,20,28,..., dimensions={0} | all-to-all | bytes 262144 | tf_op jit(solution)/shard_map/all_to_all | solution.py:524
  29.6 0.6 %rsqrt_multiply_fusion = (f32[32,128]{1,0:T(8,128)}, f32[32,128]{1,0:T(8,128)}) fusion(f32[32,128]{1,0:T(8,128)S(1)} %get-tuple-element.27, f32[32,128]{1,0:T(8,128)S(1)} %get-tuple-element.26, bf16[32,128]{1,0:T(8,128)(2,1)S(1)} %reduce_max.14), kind=kLoop, calls=%fused_computation.3 | loop fusion | flops 32768 | bytes 73728 | tf_op jit(solution)/shard_map/div | solution.py:531
  (19 shorter events, 0.1 us)
Async XLA Ops:
  0.6 9.7 %collective-permute-start.3 = (bf16[256,512]{1,0:T(8,128)(2,1)}, bf16[256,512]{1,0:T(8,128)(2,1)S(1)}, u32[]{:S(2)}, u32[]{:S(2)}) collective-permute-start(bf16[256,512]{1,0:T(8,128)(2,1)} %strip_a), channel_id=1, source_target_pairs={{0,16},{8,24},{16,0},{24,8},{1,17},{9,25},{17,1},{25,9},{2,18},{10... | collective-permute-start | bytes 786440 | tf_op jit(solution)/shard_map/ppermute | solution.py:69
  3.6 5.0 %collective-permute-start.2 = (bf16[256,512]{1,0:T(8,128)(2,1)}, bf16[256,512]{1,0:T(8,128)(2,1)S(1)}, u32[]{:S(2)}, u32[]{:S(2)}) collective-permute-start(bf16[256,512]{1,0:T(8,128)(2,1)} %strip_a), channel_id=1, source_target_pairs={{0,8},{8,0},{16,24},{24,16},{1,9},{9,1},{17,25},{25,17},{2,10},{10... | collective-permute-start | bytes 786440 | tf_op jit(solution)/shard_map/ppermute | solution.py:69
  3.6 1.6 %collective-permute-start.4 = (s32[1]{0:T(128)}, s32[1]{0:T(128)}, u32[]{:S(2)}, u32[]{:S(2)}) collective-permute-start(s32[1]{0:T(128)} %param.14), channel_id=1, source_target_pairs={{0,8},{8,0},{16,24},{24,16},{1,9},{9,1},{17,25},{25,17},{2,10},{10... | collective-permute-start | bytes 20 | tf_op jit(solution)/shard_map/ppermute | solution.py:69
  4.1 3.6 %collective-permute-start = (bf16[2,96,384]{2,1,0:T(8,128)(2,1)}, bf16[2,96,384]{2,1,0:T(8,128)(2,1)S(1)}, u32[]{:S(2)}, u32[]{:S(2)}) collective-permute-start(bf16[2,96,384]{2,1,0:T(8,128)(2,1)} %tpl_a.1), channel_id=1, source_target_pairs={{0,8},{8,0},{16,24},{24,16},{1,9},{9,1},{17,25},{25,17},{2,10},{10... | collective-permute-start | bytes 442376 | tf_op jit(solution)/shard_map/ppermute | solution.py:69
  5.2 0.7 %copy-start.9 = (f32[4]{0:T(128)S(1)}, f32[4]{0:T(128)}, u32[]{:S(2)}) copy-start(f32[4]{0:T(128)} %defocus_ref.1) | copy-start | bytes 52
  5.9 1.8 %copy-start.6 = (bf16[2,96,384]{2,1,0:T(8,128)(2,1)S(1)}, bf16[2,96,384]{2,1,0:T(8,128)(2,1)}, u32[]{:S(2)}) copy-start(bf16[2,96,384]{2,1,0:T(8,128)(2,1)} %tpl_a.1) | copy-start | bytes 442372
  5.9 2.2 %copy-start = (bf16[512,512]{1,0:T(8,128)(2,1)S(1)}, bf16[512,512]{1,0:T(8,128)(2,1)}, u32[]{:S(2)}) copy-start(bf16[512,512]{1,0:T(8,128)(2,1)} %constant.30.clone.col_ref.refs_3_.refs_4_) | copy-start | bytes 1572868
  5.9 2.2 %copy-start.2 = (bf16[2,672,192]{2,1,0:T(8,128)(2,1)S(1)}, bf16[2,672,192]{2,1,0:T(8,128)(2,1)}, u32[]{:S(2)}) copy-start(bf16[2,672,192]{2,1,0:T(8,128)(2,1)} %constant.31.clone.deep_ref.refs_5_) | copy-start | bytes 1548292
  5.9 2.8 %copy-start.1 = (bf16[672,640]{1,0:T(8,128)(2,1)S(1)}, bf16[672,640]{1,0:T(8,128)(2,1)}, u32[]{:S(2)}) copy-start(bf16[672,640]{1,0:T(8,128)(2,1)} %constant.32.clone.row_ref.refs_4_) | copy-start | bytes 2580484
  5.9 2.8 %copy-start.5 = (bf16[256,512]{1,0:T(8,128)(2,1)S(1)}, bf16[256,512]{1,0:T(8,128)(2,1)}, u32[]{:S(2)}) copy-start(bf16[256,512]{1,0:T(8,128)(2,1)} %strip_a) | copy-start | bytes 786436
  7.8 6.1 %collective-permute-start.1 = (bf16[1,192,384]{2,1,0:T(8,128)(2,1)S(1)}, bf16[1,192,384]{2,1,0:T(8,128)(2,1)S(1)}, u32[]{:S(2)}, u32[]{:S(2)}) collective-permute-start(bf16[1,192,384]{2,1,0:T(8,128)(2,1)S(1)} %shard_map.122.raw_ref), channel_id=1, source_target_pairs={{0,16},{8,24},{16,0},{24,8},{1,17},{9,25},{17,1},{25,9},{2,18},{10... | collective-permute-start | bytes 442376 | tf_op jit(solution)/shard_map/ppermute | solution.py:69
  10.3 1.5 %collective-permute-start.5 = (bf16[256,512]{1,0:T(8,128)(2,1)S(1)}, bf16[256,512]{1,0:T(8,128)(2,1)S(1)}, u32[]{:S(2)}, u32[]{:S(2)}) collective-permute-start(bf16[256,512]{1,0:T(8,128)(2,1)S(1)} %collective-permute-done.3.refs_2_), channel_id=1, source_target_pairs={{0,8},{8,0},{16,24},{24,16},{1,9},{9,1},{17,25},{25,17},{2,10},{10... | collective-permute-start | bytes 786440 | tf_op jit(solution)/shard_map/ppermute | solution.py:69
  11.8 2.1 %copy-start.3 = (bf16[256,768]{1,0:T(8,128)(2,1)S(1)}, bf16[256,768]{1,0:T(8,128)(2,1)}, u32[]{:S(2)}) copy-start(bf16[256,768]{1,0:T(8,128)(2,1)} %constant.34.clone.refs_7_) | copy-start | bytes 1179652
  11.8 2.1 %copy-start.4 = (f32[672,1]{1,0:T(8,128)S(1)}, f32[672,1]{1,0:T(8,128)}, u32[]{:S(2)}) copy-start(f32[672,1]{1,0:T(8,128)} %constant.35.clone.refs_8_) | copy-start | bytes 8068
  11.9 2.1 %copy-start.7 = (bf16[512,128]{1,0:T(8,128)(2,1)S(1)}, bf16[512,128]{1,0:T(8,128)(2,1)}, u32[]{:S(2)}) copy-start(bf16[512,128]{1,0:T(8,128)(2,1)} %constant.33.clone.refs_6_) | copy-start | bytes 393220
  11.9 2.1 %copy-start.8 = (f32[1,512]{1,0:T(1,128)S(1)}, f32[1,512]{1,0:T(1,128)}, u32[]{:S(2)}) copy-start(f32[1,512]{1,0:T(1,128)} %constant.36.clone.refs_9_) | copy-start | bytes 6148

commit v7 on v5

--- a/solution.py
+++ b/solution.py
@@ -13,7 +13,7 @@
 TS = 384
 STRIP = 256
 OUTC = 128
-CHUNK = 16
+CHUNK = 48
 STEP = 8
 LANES = 256
 VMEM_BYTES = 24 * 1024 * 1024

time: 30.2 us -> 30.2 us (level)
  no operation moved by 1% of the time
where the time goes in v7:
time: 30.2 us; the launch traced here: 30 us
  blocking collectives  13.4 us (44%)
  Pallas kernels  8.57 us (28%)
  starting transfers between devices  3.83 us (13%)
  between operations  1.41 us (5%)
  waiting for transfers between devices  1.34 us (4%)
  local copies, waits for them, and re-layouts  0.69 us (2%)
  other arithmetic  0.69 us (2%)
    all_to_all x1, blocking collectives, local(): lax.all_to_all(scores, ('tile', 'orient'), split_axis=0, concat_axis=0, t...  13.4 us
    pallas_call x7, Pallas kernels, on_device(): pl.pallas_call(kernel, out_shape=result, in_specs=[smem] * len(scalars) +...  8.57 us
    ppermute x6, starting transfers between devices, swapped(): lax.ppermute(value, axis, [(source, source ^ step) for source in range(co...  3.83 us
    ppermute x6, waiting for transfers between devices, swapped(): lax.ppermute(value, axis, [(source, source ^ step) for source in range(co...  1.34 us
    unnamed x20, local copies, waits for them, and re-layouts  0.69 us
    div x1, other arithmetic, local(): return (best, (best - score_mean) / jnp.sqrt(score_var + 1e-05))  0.62 us
  transfers between devices with their start and end apart: 6, of which 4 were waited for; matrix products, arithmetic and copies ran while one was open for 0% of the time, Pallas kernels for 22%

profile of v7, /device:TPU:0, one launch (start us, length us, event | category | flops | bytes accessed | tf_op | source)
XLA Modules:
  0.0 30.0 jit_solution(6893836715353329395)
XLA Ops:
  0.6 3.0 %collective-permute-start.3 = (bf16[256,512]{1,0:T(8,128)(2,1)}, bf16[256,512]{1,0:T(8,128)(2,1)S(1)}, u32[]{:S(2)}, u32[]{:S(2)}) collective-permute-start(bf16[256,512]{1,0:T(8,128)(2,1)} %strip_a), channel_id=1, source_target_pairs={{0,16},{8,24},{16,0},{24,8},{1,17},{9,25},{17,1},{25,9},{2,18},{10... | collective-permute-start | bytes 786440 | tf_op jit(solution)/shard_map/ppermute | solution.py:69
  3.6 0.0 collective-permute-start.2
  3.6 0.5 %collective-permute-start.4 = (s32[1]{0:T(128)}, s32[1]{0:T(128)}, u32[]{:S(2)}, u32[]{:S(2)}) collective-permute-start(s32[1]{0:T(128)} %param.14), channel_id=1, source_target_pairs={{0,8},{8,0},{16,24},{24,16},{1,9},{9,1},{17,25},{25,17},{2,10},{10... | collective-permute-start | bytes 20 | tf_op jit(solution)/shard_map/ppermute | solution.py:69
  4.1 0.0 collective-permute-start
  4.8 0.4 %collective-permute-done.4.group_b = s32[1]{0:T(128)} collective-permute-done((s32[1]{0:T(128)}, s32[1]{0:T(128)}, u32[]{:S(2)}, u32[]{:S(2)}) %collective-permute-start.4) | collective-permute-done | bytes 36 | tf_op jit(solution)/shard_map/ppermute | solution.py:69
  5.2 0.7 %copy-done.9 = f32[4]{0:T(128)S(1)} copy-done((f32[4]{0:T(128)S(1)}, f32[4]{0:T(128)}, u32[]{:S(2)}) %copy-start.9) | copy-done | bytes 40
  5.9 0.0 copy-start.5
  5.9 1.8 %shard_map.125.ctf_ref = f32[2,2,336,256]{3,2,1,0:T(8,128)S(1)} custom-call(s32[1]{0:T(128)} %bitcast.tile_ref, s32[1]{0:T(128)S(6)} %copy.13.group_a, s32[1]{0:T(128)} %collective-permute-done.4.group_b, f32[4]{0:T(128)S(1)} %copy-done.9), custom_call_target="tpu_custom_call" | custom-call | flops 3523215360 | tf_op jit(solution)/shard_map/pallas_call | solution.py:399
  7.7 0.0 collective-permute-done.tpl_b
  7.7 0.0 copy-done.6
  7.8 0.3 %collective-permute-start.1 = (bf16[1,192,384]{2,1,0:T(8,128)(2,1)S(1)}, bf16[1,192,384]{2,1,0:T(8,128)(2,1)S(1)}, u32[]{:S(2)}, u32[]{:S(2)}) collective-permute-start(bf16[1,192,384]{2,1,0:T(8,128)(2,1)S(1)} %shard_map.122.raw_ref), channel_id=1, source_target_pairs={{0,16},{8,24},{16,0},{24,8},{1,17},{9,25},{17,1},{25,9},{2,18},{10... | collective-permute-start | bytes 442376 | tf_op jit(solution)/shard_map/ppermute | solution.py:69
  8.1 0.6 %shard_map.123 = (f32[1,672,512]{2,1,0:T(8,128)S(1)}, f32[8,384]{1,0:T(8,128)S(1)}) custom-call(s32[1]{0:T(128)} %bitcast.tile_ref, bf16[1,192,384]{2,1,0:T(8,128)(2,1)S(1)} %shard_map.122.raw_ref, bf16[512,512]{1,0:T(8,128)(2,1)S(1)} %copy-done, bf16[2,672,192]{2,1,0:T(8,128)(2,1)S(1)} %copy-done.2), custom_call_target="tpu_custom_call" | custom-call | tf_op jit(solution)/shard_map/pallas_call | solution.py:399
  8.7 0.0 collective-permute-done.2.strip_b
  8.7 1.1 %shard_map.124 = (f32[4,672,512]{2,1,0:T(8,128)S(1)}, f32[2,336,256]{2,1,0:T(8,128)S(1)}) custom-call(s32[1]{0:T(128)} %bitcast.tile_ref, bf16[256,512]{1,0:T(8,128)(2,1)S(1)} %copy-done.5, bf16[256,512]{1,0:T(8,128)(2,1)S(1)} %collective-permute-done.2.strip_b, bf16[512,512]{1,0:T(8,128)(2,1)S(1)} %copy-done, bf16[672,640]{1,0:T(8,128)(2,1)S(1)} %copy-done.1), custom_call_target="tpu_custom_call" | custom-call | tf_op jit(solution)/shard_map/pallas_call | solution.py:399
  9.8 0.5 %collective-permute-done.3.refs_2_ = bf16[256,512]{1,0:T(8,128)(2,1)S(1)} collective-permute-done((bf16[256,512]{1,0:T(8,128)(2,1)}, bf16[256,512]{1,0:T(8,128)(2,1)S(1)}, u32[]{:S(2)}, u32[]{:S(2)}) %collective-permute-start.3) | collective-permute-done | bytes 262176 | tf_op jit(solution)/shard_map/ppermute | solution.py:69
  10.3 0.0 collective-permute-start.5
  10.3 1.2 %shard_map.126 = (f32[4,672,512]{2,1,0:T(8,128)S(1)}, f32[2,336,256]{2,1,0:T(8,128)S(1)}) custom-call(s32[1]{0:T(128)} %bitcast.tile_ref, f32[4,672,512]{2,1,0:T(8,128)S(1)} %get-tuple-element.16.refs_0_.first_ref, f32[2,336,256]{2,1,0:T(8,128)S(1)} %get-tuple-element.19.refs_1_, bf16[256,512]{1,0:T(8,128)(2,1)S(1)} %collective-permute-done.3.refs_2_, ...), custom_call_target="tpu_custom_call" | custom-call | flops 5284823040 | tf_op jit(solution)/shard_map/pallas_call | solution.py:399
  11.5 0.4 %collective-permute-done.5.strip_ref = bf16[256,512]{1,0:T(8,128)(2,1)S(1)} collective-permute-done((bf16[256,512]{1,0:T(8,128)(2,1)S(1)}, bf16[256,512]{1,0:T(8,128)(2,1)S(1)}, u32[]{:S(2)}, u32[]{:S(2)}) %collective-permute-start.5) | collective-permute-done | bytes 262176 | tf_op jit(solution)/shard_map/ppermute | solution.py:69
  11.9 1.9 %shard_map.127.refs_1_ = f32[2,4,336,256]{3,2,1,0:T(8,128)S(1)} custom-call(s32[1]{0:T(128)} %bitcast.tile_ref, f32[4,672,512]{2,1,0:T(8,128)S(1)} %get-tuple-element.16.refs_0_.first_ref, f32[4,672,512]{2,1,0:T(8,128)S(1)} %get-tuple-element.21.second_ref, f32[2,336,256]{2,1,0:T(8,128)S(1)} %get-tuple-element.22.previous_ref, ...), custom_call_target="tpu_custom_call" | custom-call | flops 2113929216 | tf_op jit(solution)/shard_map/pallas_call | solution.py:399
  13.8 0.1 collective-permute-done.1.refs_0_
  13.9 0.0 copy-done.4
  13.9 1.9 %shard_map.128 = bf16[16,1,32,128]{3,2,1,0:T(8,128)(2,1)S(1)} custom-call(s32[1]{0:T(128)} %bitcast.tile_ref, bf16[1,192,384]{2,1,0:T(8,128)(2,1)S(1)} %collective-permute-done.1.refs_0_, f32[2,4,336,256]{3,2,1,0:T(8,128)S(1)} %shard_map.127.refs_1_, f32[1,672,512]{2,1,0:T(8,128)S(1)} %get-tuple-element.24.refs_2_, f32[8,384]{1,0:T(8,128)S(1)} %get-tuple-element.25.refs_3_, ...), custom_call_target="tpu_custom_call" | custom-call | tf_op jit(solution)/shard_map/pallas_call | solution.py:399
  15.8 13.4 %all_to_all.5 = bf16[16,1,32,128]{3,2,1,0:T(8,128)(2,1)S(1)} all-to-all(bf16[16,1,32,128]{3,2,1,0:T(8,128)(2,1)S(1)} %shard_map.128), channel_id=1, replica_groups={{0,1,2,3,4,5,6,7,8,9,10,11,12,13,14,15},{16,17,18,19,20,21,22,23,24,25,..., dimensions={0} | all-to-all | bytes 262144 | tf_op jit(solution)/shard_map/all_to_all | solution.py:520
  29.4 0.6 %rsqrt_multiply_fusion = (f32[32,128]{1,0:T(8,128)}, f32[32,128]{1,0:T(8,128)}) fusion(f32[32,128]{1,0:T(8,128)S(1)} %get-tuple-element.27, f32[32,128]{1,0:T(8,128)S(1)} %get-tuple-element.26, bf16[32,128]{1,0:T(8,128)(2,1)S(1)} %reduce_max.14), kind=kLoop, calls=%fused_computation.3 | loop fusion | flops 32768 | bytes 73728 | tf_op jit(solution)/shard_map/div | solution.py:527
  (19 shorter events, 0.1 us)
Async XLA Ops:
  0.6 9.7 %collective-permute-start.3 = (bf16[256,512]{1,0:T(8,128)(2,1)}, bf16[256,512]{1,0:T(8,128)(2,1)S(1)}, u32[]{:S(2)}, u32[]{:S(2)}) collective-permute-start(bf16[256,512]{1,0:T(8,128)(2,1)} %strip_a), channel_id=1, source_target_pairs={{0,16},{8,24},{16,0},{24,8},{1,17},{9,25},{17,1},{25,9},{2,18},{10... | collective-permute-start | bytes 786440 | tf_op jit(solution)/shard_map/ppermute | solution.py:69
  3.6 5.0 %collective-permute-start.2 = (bf16[256,512]{1,0:T(8,128)(2,1)}, bf16[256,512]{1,0:T(8,128)(2,1)S(1)}, u32[]{:S(2)}, u32[]{:S(2)}) collective-permute-start(bf16[256,512]{1,0:T(8,128)(2,1)} %strip_a), channel_id=1, source_target_pairs={{0,8},{8,0},{16,24},{24,16},{1,9},{9,1},{17,25},{25,17},{2,10},{10... | collective-permute-start | bytes 786440 | tf_op jit(solution)/shard_map/ppermute | solution.py:69
  3.6 1.6 %collective-permute-start.4 = (s32[1]{0:T(128)}, s32[1]{0:T(128)}, u32[]{:S(2)}, u32[]{:S(2)}) collective-permute-start(s32[1]{0:T(128)} %param.14), channel_id=1, source_target_pairs={{0,8},{8,0},{16,24},{24,16},{1,9},{9,1},{17,25},{25,17},{2,10},{10... | collective-permute-start | bytes 20 | tf_op jit(solution)/shard_map/ppermute | solution.py:69
  4.1 3.6 %collective-permute-start = (bf16[2,96,384]{2,1,0:T(8,128)(2,1)}, bf16[2,96,384]{2,1,0:T(8,128)(2,1)S(1)}, u32[]{:S(2)}, u32[]{:S(2)}) collective-permute-start(bf16[2,96,384]{2,1,0:T(8,128)(2,1)} %tpl_a.1), channel_id=1, source_target_pairs={{0,8},{8,0},{16,24},{24,16},{1,9},{9,1},{17,25},{25,17},{2,10},{10... | collective-permute-start | bytes 442376 | tf_op jit(solution)/shard_map/ppermute | solution.py:69
  5.2 0.7 %copy-start.9 = (f32[4]{0:T(128)S(1)}, f32[4]{0:T(128)}, u32[]{:S(2)}) copy-start(f32[4]{0:T(128)} %defocus_ref.1) | copy-start | bytes 52
  5.9 1.8 %copy-start.6 = (bf16[2,96,384]{2,1,0:T(8,128)(2,1)S(1)}, bf16[2,96,384]{2,1,0:T(8,128)(2,1)}, u32[]{:S(2)}) copy-start(bf16[2,96,384]{2,1,0:T(8,128)(2,1)} %tpl_a.1) | copy-start | bytes 442372
  5.9 2.2 %copy-start = (bf16[512,512]{1,0:T(8,128)(2,1)S(1)}, bf16[512,512]{1,0:T(8,128)(2,1)}, u32[]{:S(2)}) copy-start(bf16[512,512]{1,0:T(8,128)(2,1)} %constant.30.clone.col_ref.refs_3_.refs_4_) | copy-start | bytes 1572868
  5.9 2.2 %copy-start.2 = (bf16[2,672,192]{2,1,0:T(8,128)(2,1)S(1)}, bf16[2,672,192]{2,1,0:T(8,128)(2,1)}, u32[]{:S(2)}) copy-start(bf16[2,672,192]{2,1,0:T(8,128)(2,1)} %constant.31.clone.deep_ref.refs_5_) | copy-start | bytes 1548292
  5.9 2.8 %copy-start.1 = (bf16[672,640]{1,0:T(8,128)(2,1)S(1)}, bf16[672,640]{1,0:T(8,128)(2,1)}, u32[]{:S(2)}) copy-start(bf16[672,640]{1,0:T(8,128)(2,1)} %constant.32.clone.row_ref.refs_4_) | copy-start | bytes 2580484
  5.9 2.8 %copy-start.5 = (bf16[256,512]{1,0:T(8,128)(2,1)S(1)}, bf16[256,512]{1,0:T(8,128)(2,1)}, u32[]{:S(2)}) copy-start(bf16[256,512]{1,0:T(8,128)(2,1)} %strip_a) | copy-start | bytes 786436
  7.8 6.1 %collective-permute-start.1 = (bf16[1,192,384]{2,1,0:T(8,128)(2,1)S(1)}, bf16[1,192,384]{2,1,0:T(8,128)(2,1)S(1)}, u32[]{:S(2)}, u32[]{:S(2)}) collective-permute-start(bf16[1,192,384]{2,1,0:T(8,128)(2,1)S(1)} %shard_map.122.raw_ref), channel_id=1, source_target_pairs={{0,16},{8,24},{16,0},{24,8},{1,17},{9,25},{17,1},{25,9},{2,18},{10... | collective-permute-start | bytes 442376 | tf_op jit(solution)/shard_map/ppermute | solution.py:69
  10.3 1.5 %collective-permute-start.5 = (bf16[256,512]{1,0:T(8,128)(2,1)S(1)}, bf16[256,512]{1,0:T(8,128)(2,1)S(1)}, u32[]{:S(2)}, u32[]{:S(2)}) collective-permute-start(bf16[256,512]{1,0:T(8,128)(2,1)S(1)} %collective-permute-done.3.refs_2_), channel_id=1, source_target_pairs={{0,8},{8,0},{16,24},{24,16},{1,9},{9,1},{17,25},{25,17},{2,10},{10... | collective-permute-start | bytes 786440 | tf_op jit(solution)/shard_map/ppermute | solution.py:69
  11.8 2.1 %copy-start.3 = (bf16[256,768]{1,0:T(8,128)(2,1)S(1)}, bf16[256,768]{1,0:T(8,128)(2,1)}, u32[]{:S(2)}) copy-start(bf16[256,768]{1,0:T(8,128)(2,1)} %constant.34.clone.refs_7_) | copy-start | bytes 1179652
  11.8 2.1 %copy-start.4 = (f32[672,1]{1,0:T(8,128)S(1)}, f32[672,1]{1,0:T(8,128)}, u32[]{:S(2)}) copy-start(f32[672,1]{1,0:T(8,128)} %constant.35.clone.refs_8_) | copy-start | bytes 8068
  11.9 2.1 %copy-start.7 = (bf16[512,128]{1,0:T(8,128)(2,1)S(1)}, bf16[512,128]{1,0:T(8,128)(2,1)}, u32[]{:S(2)}) copy-start(bf16[512,128]{1,0:T(8,128)(2,1)} %constant.33.clone.refs_6_) | copy-start | bytes 393220
  11.9 2.1 %copy-start.8 = (f32[1,512]{1,0:T(1,128)S(1)}, f32[1,512]{1,0:T(1,128)}, u32[]{:S(2)}) copy-start(f32[1,512]{1,0:T(1,128)} %constant.36.clone.refs_9_) | copy-start | bytes 6148
